TPU v7x, 256 devices: a whole 4x4x8 slice. The times are simulated.
256 devices in a mesh: lon: 16 (over x_hi, z), lat: 16 (over x_lo, y, core).
Axes of the slice: x: 4 (x_hi: 2, x_lo: 2; x = x_hi * 2 + x_lo), y: 4, z: 8, core: 2. Of those that a mesh axis runs over, the one named last changes fastest.
Arguments:
- pressure: float32 [4, 3840, 4096], P(None, 'lat', 'lon'), may hold values from -6 to 6
- wind_east: float32 [4, 3840, 4096], P(None, 'lat', 'lon'), may hold values from -6 to 6
- wind_north: float32 [4, 3840, 4096], P(None, 'lat', 'lon'), may hold values from -6 to 6
- forcing: float32 [4, 3840, 4096], P(None, 'lat', 'lon'), may hold values from -6 to 6
- coef_lon: float32 [4, 3840, 4096], P(None, 'lat', 'lon'), may hold values from 0.2 to 2
- coef_lat: float32 [4, 3840, 4096], P(None, 'lat', 'lon'), may hold values from 0.2 to 2
- coef_vert: float32 [4, 3840, 4096], P(None, 'lat', 'lon'), may hold values from 0.2 to 2
- diag_coef: float32 [4, 3840, 4096], P(None, 'lat', 'lon'), may hold values from 0.5 to 2
Outputs:
- new_pressure: float32 [4, 3840, 4096], P(None, 'lat', 'lon')
- residual: float32 [4, 3840, 4096], P(None, 'lat', 'lon')
All inputs are finite; a program needn't handle non-finite values.
Results may differ from a plain program's by a relative error of at most 0.00002.
Values sent between devices are 32-bit elements; how exact they have to be, the bound alone decides.
No kernel may reach another device: no remote copies, remote signals or barrier semaphores. Data moves between devices by JAX's collectives and lax.ppermute only.
A program may use at most 128 MiB of HBM per device.

v0:
```python
import math

import jax
import jax.numpy as jnp
from jax import lax
from jax.sharding import PartitionSpec as P


def with_halo(block, sides, width, periodic):
    for axis, dim in sides:
        count = lax.axis_size(axis)
        forward = [(i, i + 1) for i in range(count - 1)]
        if periodic:
            forward.append((count - 1, 0))
        backward = [(target, source) for source, target in forward]
        low = lax.ppermute(
            lax.slice_in_dim(block, block.shape[dim] - width, None, axis=dim), axis, forward
        )
        high = lax.ppermute(lax.slice_in_dim(block, 0, width, axis=dim), axis, backward)
        block = jnp.concatenate([low, block, high], axis=dim)
    return block


def from_behind(block, axis, distance):
    devices = range(lax.axis_size(axis))
    route = [((i - distance) % len(devices), i) for i in devices]
    return lax.ppermute(block, axis, route)


def face_cosines(start_row, face_count, lat_total):
    positions = (start_row + jnp.arange(face_count, dtype=jnp.int32)).astype(jnp.float32)
    return jnp.cos(positions * (math.pi / lat_total) - math.pi / 2)


def divergence(east_ext, north_ext, face_cos):
    cos_low = face_cos[:-1][None, :, None]
    cos_high = face_cos[1:][None, :, None]
    middle = north_ext[:, 1:-1, 1:-1]
    zonal = 0.5 * (east_ext[:, 1:-1, 2:] - east_ext[:, 1:-1, :-2])
    merid = 0.5 * (
        cos_high * (middle + north_ext[:, 2:, 1:-1]) - cos_low * (north_ext[:, :-2, 1:-1] + middle)
    )
    return zonal + merid


def helmholtz(field_ext, lon_ext, lat_ext, vert_coef, diag_coef, face_cos):
    centre = field_ext[:, 1:-1, 1:-1]
    lon_mid = lon_ext[:, 1:-1, 1:-1]
    west_weight = 0.5 * (lon_mid + lon_ext[:, 1:-1, :-2])
    east_weight = 0.5 * (lon_mid + lon_ext[:, 1:-1, 2:])
    metric = 0.5 * (1.0 + jnp.abs(face_cos))
    lat_mid = lat_ext[:, 1:-1, 1:-1]
    south_weight = metric[:-1][None, :, None] * (0.5 * (lat_mid + lat_ext[:, :-2, 1:-1]))
    north_weight = metric[1:][None, :, None] * (0.5 * (lat_mid + lat_ext[:, 2:, 1:-1]))
    zero_level = jnp.zeros_like(centre[:1])
    upper_weight = jnp.concatenate((vert_coef[1:], jnp.zeros_like(vert_coef[:1])), 0)
    below = jnp.concatenate((zero_level, centre[:-1]), 0)
    above = jnp.concatenate((centre[1:], zero_level), 0)
    diag_total = (
        diag_coef
        + west_weight
        + east_weight
        + south_weight
        + north_weight
        + vert_coef
        + upper_weight
    )
    coupled = (
        west_weight * field_ext[:, 1:-1, :-2]
        + east_weight * field_ext[:, 1:-1, 2:]
        + south_weight * field_ext[:, :-2, 1:-1]
        + north_weight * field_ext[:, 2:, 1:-1]
        + vert_coef * below
        + upper_weight * above
    )
    return (diag_total * centre - coupled, diag_total)


def place_poles(latitude, partner, rim_width):
    lat_index = lax.axis_index("lat")
    lat_devices = lax.axis_size("lat")
    south_rim = jnp.where(lat_index == 0, partner[0], latitude[:, :, :rim_width])
    north_rim = jnp.where(lat_index == lat_devices - 1, partner[1], latitude[:, :, -rim_width:])
    return jnp.concatenate((south_rim, latitude[:, :, rim_width:-rim_width], north_rim), 2)


def pole_edges(stacked, rim_width):
    return jnp.stack(
        (jnp.flip(stacked[:, :, :rim_width], 2), jnp.flip(stacked[:, :, -rim_width:], 2))
    )


def extend_rows(stacked, rim_width):
    latitude = with_halo(stacked, (("lat", 2),), rim_width, False)
    partner = from_behind(pole_edges(stacked, rim_width), "lon", lax.axis_size("lon") // 2)
    latitude = place_poles(latitude, partner, rim_width)
    return with_halo(latitude, (("lon", 3),), rim_width, True)


def per_device(pressure, wind_east, wind_north, forcing, coef_lon, coef_lat, coef_vert, diag_coef):
    lat_rows = pressure.shape[1]
    lat_total = lat_rows * lax.axis_size("lat")
    start_row = lax.axis_index("lat") * lat_rows
    face_cos = face_cosines(start_row, lat_rows + 1, lat_total)
    extended = extend_rows(jnp.stack((pressure, wind_east, wind_north, coef_lon, coef_lat)), 1)
    rhs_field = forcing - divergence(extended[1], extended[2], face_cos)
    applied, diag_total = helmholtz(
        extended[0], extended[3], extended[4], coef_vert, diag_coef, face_cos
    )
    new_pressure = pressure + (rhs_field - applied) / diag_total
    pressure_ext = extend_rows(new_pressure[None], 1)[0]
    applied_new, unused = helmholtz(
        pressure_ext, extended[3], extended[4], coef_vert, diag_coef, face_cos
    )
    return (new_pressure, rhs_field - applied_new)


def solution(mesh):
    in_specs = (
        P(None, "lat", "lon"),
        P(None, "lat", "lon"),
        P(None, "lat", "lon"),
        P(None, "lat", "lon"),
        P(None, "lat", "lon"),
        P(None, "lat", "lon"),
        P(None, "lat", "lon"),
        P(None, "lat", "lon"),
    )
    out_specs = (P(None, "lat", "lon"), P(None, "lat", "lon"))
    return jax.shard_map(
        per_device, mesh=mesh, in_specs=in_specs, out_specs=out_specs, check_vma=False
    )
```

profile of v0, /device:TPU:2, one launch (start us, length us, event | category | flops | bytes accessed | tf_op | source)
XLA Modules:
  0.0 103.5 jit_solution(11151623272126690223)
XLA Ops:
  0.7 2.0 %bitcast_dynamic-update-slice_fusion.4 = f32[5,4,240,256]{3,1,0,2:T(4,128)S(1)} fusion(f32[4,240,256]{2,1,0:T(8,128)} %param.8), kind=kLoop, calls=%fused_computation.55 | loop fusion | bytes 1966080
  2.7 0.7 bitcast_dynamic-update-slice_fusion.3
  3.4 0.7 bitcast_dynamic-update-slice_fusion.2
  4.1 0.7 bitcast_dynamic-update-slice_fusion.1
  5.5 2.2 %copy-done = f32[5,4,240,256]{3,1,0,2:T(4,128)} copy-done((f32[5,4,240,256]{3,1,0,2:T(4,128)}, f32[5,4,240,256]{3,1,0,2:T(4,128)S(1)}, u32[]{:S(2)}) %copy-start) | copy-done | bytes 4915224
  7.8 2.2 %collective-permute-start = (f32[2,5,4,1,256]{4,2,1,3,0:T(4,128)S(1)}, f32[2,5,4,1,256]{4,2,1,3,0:T(4,128)S(1)}, u32[]{:S(2)}, u32[]{:S(2)}) collective-permute-start(f32[2,5,4,1,256]{4,2,1,3,0:T(4,128)S(1)} %pad_maximum_fusion.3), channel_id=1, source_target_pairs={{128,0},{144,16},{160,32},{176,48},{192,64},{208,80},{224,96},{240... | collective-permute-start | bytes 122888 | tf_op jit(solution)/shard_map/ppermute | solution.py:27
  10.0 1.9 %collective-permute-start.1 = (f32[5,4,1,256]{3,1,0,2:T(4,128)S(1)}, f32[5,4,1,256]{3,1,0,2:T(4,128)S(1)}, u32[]{:S(2)}, u32[]{:S(2)}) collective-permute-start(f32[5,4,1,256]{3,1,0,2:T(4,128)S(1)} %get-tuple-element.15), channel_id=1, source_target_pairs={{0,1},{1,2},{2,3},{3,4},{4,5},{5,6},{6,7},{7,8},{8,9},{9,10},{10,1... | collective-permute-start | bytes 61448 | tf_op jit(solution)/shard_map/ppermute | solution.py:16
  11.9 5.8 %collective-permute-start.2 = (f32[5,4,1,256]{3,1,0,2:T(4,128)S(1)}, f32[5,4,1,256]{3,1,0,2:T(4,128)S(1)}, u32[]{:S(2)}, u32[]{:S(2)}) collective-permute-start(f32[5,4,1,256]{3,1,0,2:T(4,128)S(1)} %get-tuple-element.18), channel_id=1, source_target_pairs={{1,0},{2,1},{3,2},{4,3},{5,4},{6,5},{7,6},{8,7},{9,8},{10,9},{11,1... | collective-permute-start | bytes 61448 | tf_op jit(solution)/shard_map/ppermute | solution.py:19
  17.8 1.3 %collective-permute-done.2 = f32[5,4,1,256]{3,1,0,2:T(4,128)S(1)} collective-permute-done((f32[5,4,1,256]{3,1,0,2:T(4,128)S(1)}, f32[5,4,1,256]{3,1,0,2:T(4,128)S(1)}, u32[]{:S(2)}, u32[]{:S(2)}) %collective-permute-start.2) | collective-permute-done | bytes 20512 | tf_op jit(solution)/shard_map/ppermute | solution.py:19
  19.1 3.5 %pad_maximum_fusion.1 = f32[5,4,242,256]{3,1,0,2:T(4,128)S(1)} fusion(f32[5,4,1,256]{3,1,0,2:T(4,128)S(1)} %get-tuple-element.30, f32[5,4,240,256]{3,1,0,2:T(4,128)} %copy-done, f32[5,4,1,256]{3,1,0,2:T(4,128)S(1)} %get-tuple-element.29), kind=kLoop, calls=%fused_computation.1 | loop fusion | flops 2478080 | bytes 9912320 | tf_op jit(solution)/shard_map/concatenate | solution.py:84
  22.6 3.1 %fusion.36 = (f32[5,4,242,1]{3,1,0,2:T(4,128)}, f32[5,4,242,1]{3,1,0,2:T(4,128)S(1)}) fusion(f32[5,4,242,256]{3,1,0,2:T(4,128)S(1)} %pad_maximum_fusion.1), kind=kLoop, calls=%fused_computation.81 | loop fusion | bytes 77440 | tf_op jit(solution)/shard_map/slice | solution.py:17
  25.7 2.2 %copy.36 = f32[5,4,242,1]{2,1,3,0:T(4,128)S(1)} copy(f32[5,4,242,1]{3,1,0,2:T(4,128)} %get-tuple-element.13) | data formatting | bytes 38720 | tf_op jit(solution)/shard_map/slice | solution.py:17
  27.9 2.0 %collective-permute-start.3 = (f32[5,4,242,1]{2,1,3,0:T(4,128)S(1)}, f32[5,4,242,1]{2,1,3,0:T(4,128)S(1)}, u32[]{:S(2)}, u32[]{:S(2)}) collective-permute-start(f32[5,4,242,1]{2,1,3,0:T(4,128)S(1)} %copy.36), channel_id=1, source_target_pairs={{0,16},{16,32},{32,48},{48,64},{64,80},{80,96},{96,112},{112,128},... | collective-permute-start | bytes 58088 | tf_op jit(solution)/shard_map/ppermute | solution.py:16
  29.9 2.2 %copy.37 = f32[5,4,242,1]{2,1,3,0:T(4,128)} copy(f32[5,4,242,1]{3,1,0,2:T(4,128)S(1)} %get-tuple-element.14) | data formatting | bytes 38720 | tf_op jit(solution)/shard_map/slice | solution.py:19
  32.1 4.8 %collective-permute-start.4 = (f32[5,4,242,1]{2,1,3,0:T(4,128)}, f32[5,4,242,1]{2,1,3,0:T(4,128)}, u32[]{:S(2)}, u32[]{:S(2)}) collective-permute-start(f32[5,4,242,1]{2,1,3,0:T(4,128)} %copy.37), channel_id=1, source_target_pairs={{16,0},{32,16},{48,32},{64,48},{80,64},{96,80},{112,96},{128,112},... | collective-permute-start | bytes 58088 | tf_op jit(solution)/shard_map/ppermute | solution.py:19
  38.2 1.7 %copy.38 = f32[5,4,242,1]{3,1,0,2:T(4,128)S(1)} copy(f32[5,4,242,1]{2,1,3,0:T(4,128)S(1)} %collective-permute-done.3) | data formatting | bytes 38720 | tf_op jit(solution)/shard_map/ppermute | solution.py:16
  39.9 2.6 %copy.39 = f32[5,4,242,1]{3,1,0,2:T(4,128)} copy(f32[5,4,242,1]{2,1,3,0:T(4,128)} %collective-permute-done.4) | data formatting | bytes 38720 | tf_op jit(solution)/shard_map/ppermute | solution.py:19
  42.5 13.0 %pad_maximum_fusion = f32[5,4,242,258]{3,1,0,2:T(4,128)S(1)} fusion(f32[5,4,242,1]{3,1,0,2:T(4,128)} %copy.39, f32[5,4,1,256]{3,1,0,2:T(4,128)S(1)} %get-tuple-element.30, f32[5,4,240,256]{3,1,0,2:T(4,128)} %copy-done, f32[5,4,1,256]{3,1,0,2:T(4,128)S(1)} %get-tuple-element.29, f32[5,4,242,1]{3,1,0,2:T(4,128)S(1)} %copy.38), kind=kLoop, calls=%fused_computation | loop fusion | flops 4994880 | bytes 9989760 | tf_op jit(solution)/shard_map/concatenate | solution.py:20
  55.5 1.3 %slice_bitcast_fusion.4 = (f32[4,242,258]{2,0,1:T(4,128)S(1)}, f32[4,242,258]{2,0,1:T(4,128)S(1)}, f32[4,242,258]{2,0,1:T(4,128)S(1)}, f32[4,242,258]{2,0,1:T(4,128)S(1)}, f32[4,242,258]{2,0,1:T(4,128)S(1)}) fusion(f32[5,4,242,258]{3,1,0,2:T(4,128)S(1)} %pad_maximum_fusion), kind=kLoop, calls=%fused_computation.6 | loop fusion | bytes 9989760 | tf_op jit(solution)/shard_map/squeeze | solution.py:106
  56.9 1.1 %fusion.39 = (f32[3,240,256]{2,0,1:T(4,128)S(1)}, f32[3,240,256]{2,0,1:T(4,128)S(1)}) fusion(f32[4,242,258]{2,0,1:T(4,128)S(1)} %get-tuple-element.11), kind=kLoop, calls=%fused_computation.84 | loop fusion | bytes 2949120 | tf_op jit(solution)/shard_map/slice | solution.py:57
  58.9 9.1 %fusion.30 = (f32[4,240,256]{2,0,1:T(4,128)S(1)}, f32[4,240,256]{2,0,1:T(4,128)S(1)}) fusion(f32[3,240,256]{2,0,1:T(4,128)S(1)} %get-tuple-element.22, f32[3,240,256]{2,0,1:T(4,128)S(1)} %get-tuple-element.21, f32[4,242,258]{2,0,1:T(4,128)S(1)} %get-tuple-element.11, f32[4,240,256]{2,1,0:T(8,128)S(1)} %copy-done.4, f32[4,240,256]{2,1,0:T(8,128)S(1)} %copy-done.3, ...), kind=kLoop, calls=%fused_computation.62 | loop fusion | flops 9584640 | bytes 23842560 | tf_op jit(solution)/shard_map/add | solution.py:110
  68.1 2.2 %collective-permute-start.5 = (f32[2,1,4,1,256]{4,2,3,1,0:T(4,128)S(1)}, f32[2,1,4,1,256]{4,2,3,1,0:T(4,128)S(1)}, u32[]{:S(2)}, u32[]{:S(2)}) collective-permute-start(f32[2,1,4,1,256]{4,2,3,1,0:T(4,128)S(1)} %pad_maximum_fusion.4), channel_id=1, source_target_pairs={{128,0},{144,16},{160,32},{176,48},{192,64},{208,80},{224,96},{240... | collective-permute-start | bytes 24584 | tf_op jit(solution)/shard_map/ppermute | solution.py:27
  70.3 1.9 %collective-permute-start.6 = (f32[1,4,1,256]{3,1,2,0:T(4,128)S(1)}, f32[1,4,1,256]{3,1,2,0:T(4,128)S(1)}, u32[]{:S(2)}, u32[]{:S(2)}) collective-permute-start(f32[1,4,1,256]{3,1,2,0:T(4,128)S(1)} %get-tuple-element.25), channel_id=1, source_target_pairs={{0,1},{1,2},{2,3},{3,4},{4,5},{5,6},{6,7},{7,8},{8,9},{9,10},{10,1... | collective-permute-start | bytes 12296 | tf_op jit(solution)/shard_map/ppermute | solution.py:16
  72.2 5.8 %collective-permute-start.7 = (f32[1,4,1,256]{3,1,2,0:T(4,128)S(1)}, f32[1,4,1,256]{3,1,2,0:T(4,128)S(1)}, u32[]{:S(2)}, u32[]{:S(2)}) collective-permute-start(f32[1,4,1,256]{3,1,2,0:T(4,128)S(1)} %get-tuple-element.28), channel_id=1, source_target_pairs={{1,0},{2,1},{3,2},{4,3},{5,4},{6,5},{7,6},{8,7},{9,8},{10,9},{11,1... | collective-permute-start | bytes 12296 | tf_op jit(solution)/shard_map/ppermute | solution.py:19
  78.0 1.3 %collective-permute-done.7 = f32[1,4,1,256]{3,1,2,0:T(4,128)S(1)} collective-permute-done((f32[1,4,1,256]{3,1,2,0:T(4,128)S(1)}, f32[1,4,1,256]{3,1,2,0:T(4,128)S(1)}, u32[]{:S(2)}, u32[]{:S(2)}) %collective-permute-start.7) | collective-permute-done | bytes 4128 | tf_op jit(solution)/shard_map/ppermute | solution.py:19
  79.9 5.6 %collective-permute-start.9 = (f32[1,4,242,1]{3,1,2,0:T(4,128)S(1)}, f32[1,4,242,1]{3,1,2,0:T(4,128)S(1)}, u32[]{:S(2)}, u32[]{:S(2)}) collective-permute-start(f32[1,4,242,1]{3,1,2,0:T(4,128)S(1)} %get-tuple-element.24), channel_id=1, source_target_pairs={{16,0},{32,16},{48,32},{64,48},{80,64},{96,80},{112,96},{128,112},... | collective-permute-start | bytes 11624 | tf_op jit(solution)/shard_map/ppermute | solution.py:19
  85.5 1.1 %copy.51 = f32[4,240,256]{2,1,0:T(8,128)} copy(f32[4,240,256]{2,0,1:T(4,128)S(1)} %get-tuple-element.6) | data formatting | bytes 1966080
  86.7 7.8 %collective-permute-done.8 = f32[1,4,242,1]{3,1,2,0:T(4,128)S(1)} collective-permute-done((f32[1,4,242,1]{3,1,2,0:T(4,128)S(1)}, f32[1,4,242,1]{3,1,2,0:T(4,128)S(1)}, u32[]{:S(2)}, u32[]{:S(2)}) %collective-permute-start.8) | collective-permute-done | bytes 3904 | tf_op jit(solution)/shard_map/ppermute | solution.py:16
  94.5 1.1 %maximum_bitcast_fusion = f32[4,242,258]{2,0,1:T(4,128)S(1)} fusion(f32[1,4,242,1]{3,1,2,0:T(4,128)S(1)} %collective-permute-done.9, f32[1,4,1,256]{3,1,2,0:T(4,128)S(1)} %get-tuple-element.32, f32[1,4,240,256]{3,1,2,0:T(4,128)S(1)} %bitcast.57, f32[1,4,1,256]{3,1,2,0:T(4,128)S(1)} %get-tuple-element.31, f32[1,4,242,1]{3,1,2,0:T(4,128)S(1)} %collective-permute-done.8), kind=kLoop, calls=%fused_computation.7 | loop fusion | flops 998976 | bytes 1997952 | tf_op jit(solution)/shard_map/squeeze | solution.py:111
  95.5 1.1 %fusion.38 = (f32[3,240,256]{2,0,1:T(4,128)S(1)}, f32[3,240,256]{2,0,1:T(4,128)S(1)}) fusion(f32[4,242,258]{2,0,1:T(4,128)S(1)} %maximum_bitcast_fusion), kind=kLoop, calls=%fused_computation.83 | loop fusion | bytes 2949120 | tf_op jit(solution)/shard_map/slice | solution.py:57
  96.6 5.8 %fusion.4 = f32[4,240,256]{2,0,1:T(4,128)S(1)} fusion(f32[4,240,256]{2,0,1:T(4,128)S(1)} %get-tuple-element.7, f32[4,242,258]{2,0,1:T(4,128)S(1)} %maximum_bitcast_fusion, f32[4,240,256]{2,1,0:T(8,128)S(1)} %copy-done.4, f32[3,240,256]{2,0,1:T(4,128)S(1)} %get-tuple-element.20, f32[3,240,256]{2,0,1:T(4,128)S(1)} %get-tuple-element.19, ...), kind=kLoop, calls=%fused_computation.14 | loop fusion | flops 6881280 | bytes 16959360 | tf_op jit(solution)/shard_map/sub | solution.py:115
  102.4 1.1 %copy.52 = f32[4,240,256]{2,1,0:T(8,128)} copy(f32[4,240,256]{2,0,1:T(4,128)S(1)} %fusion.4) | data formatting | bytes 1966080
  (45 shorter events, 3.7 us)
Async XLA Ops:
  0.6 2.0 %copy-start.5 = (f32[4,240,256]{2,1,0:T(8,128)S(1)}, f32[4,240,256]{2,1,0:T(8,128)}, u32[]{:S(2)}) copy-start(f32[4,240,256]{2,1,0:T(8,128)} %param.9) | copy-start | bytes 2949124
  0.6 2.7 %copy-start.6 = (f32[4,240,256]{2,1,0:T(8,128)S(1)}, f32[4,240,256]{2,1,0:T(8,128)}, u32[]{:S(2)}) copy-start(f32[4,240,256]{2,1,0:T(8,128)} %param.10) | copy-start | bytes 2949124
  0.7 3.4 %copy-start.7 = (f32[4,240,256]{2,1,0:T(8,128)S(1)}, f32[4,240,256]{2,1,0:T(8,128)}, u32[]{:S(2)}) copy-start(f32[4,240,256]{2,1,0:T(8,128)} %param.12) | copy-start | bytes 2949124
  2.7 2.1 %copy-start.8 = (f32[4,240,256]{2,1,0:T(8,128)S(1)}, f32[4,240,256]{2,1,0:T(8,128)}, u32[]{:S(2)}) copy-start(f32[4,240,256]{2,1,0:T(8,128)} %param.13) | copy-start | bytes 2949124
  5.5 2.2 %copy-start = (f32[5,4,240,256]{3,1,0,2:T(4,128)}, f32[5,4,240,256]{3,1,0,2:T(4,128)S(1)}, u32[]{:S(2)}) copy-start(f32[5,4,240,256]{3,1,0,2:T(4,128)S(1)} %bitcast_dynamic-update-slice_fusion) | copy-start | bytes 14745604
  7.8 11.4 %collective-permute-start = (f32[2,5,4,1,256]{4,2,1,3,0:T(4,128)S(1)}, f32[2,5,4,1,256]{4,2,1,3,0:T(4,128)S(1)}, u32[]{:S(2)}, u32[]{:S(2)}) collective-permute-start(f32[2,5,4,1,256]{4,2,1,3,0:T(4,128)S(1)} %pad_maximum_fusion.3), channel_id=1, source_target_pairs={{128,0},{144,16},{160,32},{176,48},{192,64},{208,80},{224,96},{240... | collective-permute-start | bytes 122888 | tf_op jit(solution)/shard_map/ppermute | solution.py:27
  10.0 7.8 %collective-permute-start.1 = (f32[5,4,1,256]{3,1,0,2:T(4,128)S(1)}, f32[5,4,1,256]{3,1,0,2:T(4,128)S(1)}, u32[]{:S(2)}, u32[]{:S(2)}) collective-permute-start(f32[5,4,1,256]{3,1,0,2:T(4,128)S(1)} %get-tuple-element.15), channel_id=1, source_target_pairs={{0,1},{1,2},{2,3},{3,4},{4,5},{5,6},{6,7},{7,8},{8,9},{9,10},{10,1... | collective-permute-start | bytes 61448 | tf_op jit(solution)/shard_map/ppermute | solution.py:16
  11.9 7.2 %collective-permute-start.2 = (f32[5,4,1,256]{3,1,0,2:T(4,128)S(1)}, f32[5,4,1,256]{3,1,0,2:T(4,128)S(1)}, u32[]{:S(2)}, u32[]{:S(2)}) collective-permute-start(f32[5,4,1,256]{3,1,0,2:T(4,128)S(1)} %get-tuple-element.18), channel_id=1, source_target_pairs={{1,0},{2,1},{3,2},{4,3},{5,4},{6,5},{7,6},{8,7},{9,8},{10,9},{11,1... | collective-permute-start | bytes 61448 | tf_op jit(solution)/shard_map/ppermute | solution.py:19
  25.7 11.9 %copy-start.1 = (f32[4,240,256]{2,1,0:T(8,128)S(1)}, f32[4,240,256]{2,1,0:T(8,128)}, u32[]{:S(2)}) copy-start(f32[4,240,256]{2,1,0:T(8,128)} %param.14) | copy-start | bytes 2949124
  27.9 10.2 %collective-permute-start.3 = (f32[5,4,242,1]{2,1,3,0:T(4,128)S(1)}, f32[5,4,242,1]{2,1,3,0:T(4,128)S(1)}, u32[]{:S(2)}, u32[]{:S(2)}) collective-permute-start(f32[5,4,242,1]{2,1,3,0:T(4,128)S(1)} %copy.36), channel_id=1, source_target_pairs={{0,16},{16,32},{32,48},{48,64},{64,80},{80,96},{96,112},{112,128},... | collective-permute-start | bytes 58088 | tf_op jit(solution)/shard_map/ppermute | solution.py:16
  32.1 7.8 %collective-permute-start.4 = (f32[5,4,242,1]{2,1,3,0:T(4,128)}, f32[5,4,242,1]{2,1,3,0:T(4,128)}, u32[]{:S(2)}, u32[]{:S(2)}) collective-permute-start(f32[5,4,242,1]{2,1,3,0:T(4,128)} %copy.37), channel_id=1, source_target_pairs={{16,0},{32,16},{48,32},{64,48},{80,64},{96,80},{112,96},{128,112},... | collective-permute-start | bytes 58088 | tf_op jit(solution)/shard_map/ppermute | solution.py:19
  56.8 1.2 %copy-start.2 = (f32[4,240,256]{2,1,0:T(8,128)S(1)}, f32[4,240,256]{2,1,0:T(8,128)}, u32[]{:S(2)}) copy-start(f32[4,240,256]{2,1,0:T(8,128)} %param.14) | copy-start | bytes 2949124
  56.8 1.5 %copy-start.3 = (f32[4,240,256]{2,1,0:T(8,128)S(1)}, f32[4,240,256]{2,1,0:T(8,128)}, u32[]{:S(2)}) copy-start(f32[4,240,256]{2,1,0:T(8,128)} %param.8) | copy-start | bytes 2949124
  56.9 1.8 %copy-start.4 = (f32[4,240,256]{2,1,0:T(8,128)S(1)}, f32[4,240,256]{2,1,0:T(8,128)}, u32[]{:S(2)}) copy-start(f32[4,240,256]{2,1,0:T(8,128)} %param.15) | copy-start | bytes 2949124
  56.9 2.1 %copy-start.9 = (f32[4,240,256]{2,1,0:T(8,128)S(1)}, f32[4,240,256]{2,1,0:T(8,128)}, u32[]{:S(2)}) copy-start(f32[4,240,256]{2,1,0:T(8,128)} %param.11) | copy-start | bytes 2949124
  56.9 2.1 %copy-start.10 = (f32[240]{0:T(256)S(1)}, f32[240]{0:T(256)}, u32[]{:S(2)}) copy-start(f32[240]{0:T(256)} %get-tuple-element.33) | copy-start | bytes 2884
  56.9 2.0 %copy-start.11 = (f32[240]{0:T(256)S(1)}, f32[240]{0:T(256)}, u32[]{:S(2)}) copy-start(f32[240]{0:T(256)} %get-tuple-element.34) | copy-start | bytes 2884
  68.1 11.2 %collective-permute-start.5 = (f32[2,1,4,1,256]{4,2,3,1,0:T(4,128)S(1)}, f32[2,1,4,1,256]{4,2,3,1,0:T(4,128)S(1)}, u32[]{:S(2)}, u32[]{:S(2)}) collective-permute-start(f32[2,1,4,1,256]{4,2,3,1,0:T(4,128)S(1)} %pad_maximum_fusion.4), channel_id=1, source_target_pairs={{128,0},{144,16},{160,32},{176,48},{192,64},{208,80},{224,96},{240... | collective-permute-start | bytes 24584 | tf_op jit(solution)/shard_map/ppermute | solution.py:27
  70.3 7.7 %collective-permute-start.6 = (f32[1,4,1,256]{3,1,2,0:T(4,128)S(1)}, f32[1,4,1,256]{3,1,2,0:T(4,128)S(1)}, u32[]{:S(2)}, u32[]{:S(2)}) collective-permute-start(f32[1,4,1,256]{3,1,2,0:T(4,128)S(1)} %get-tuple-element.25), channel_id=1, source_target_pairs={{0,1},{1,2},{2,3},{3,4},{4,5},{5,6},{6,7},{7,8},{8,9},{9,10},{10,1... | collective-permute-start | bytes 12296 | tf_op jit(solution)/shard_map/ppermute | solution.py:16
  72.2 7.1 %collective-permute-start.7 = (f32[1,4,1,256]{3,1,2,0:T(4,128)S(1)}, f32[1,4,1,256]{3,1,2,0:T(4,128)S(1)}, u32[]{:S(2)}, u32[]{:S(2)}) collective-permute-start(f32[1,4,1,256]{3,1,2,0:T(4,128)S(1)} %get-tuple-element.28), channel_id=1, source_target_pairs={{1,0},{2,1},{3,2},{4,3},{5,4},{6,5},{7,6},{8,7},{9,8},{10,9},{11,1... | collective-permute-start | bytes 12296 | tf_op jit(solution)/shard_map/ppermute | solution.py:19
  79.8 14.6 %collective-permute-start.8 = (f32[1,4,242,1]{3,1,2,0:T(4,128)S(1)}, f32[1,4,242,1]{3,1,2,0:T(4,128)S(1)}, u32[]{:S(2)}, u32[]{:S(2)}) collective-permute-start(f32[1,4,242,1]{3,1,2,0:T(4,128)S(1)} %get-tuple-element.23), channel_id=1, source_target_pairs={{0,16},{16,32},{32,48},{48,64},{64,80},{80,96},{96,112},{112,128},... | collective-permute-start | bytes 11624 | tf_op jit(solution)/shard_map/ppermute | solution.py:16
  79.9 14.5 %collective-permute-start.9 = (f32[1,4,242,1]{3,1,2,0:T(4,128)S(1)}, f32[1,4,242,1]{3,1,2,0:T(4,128)S(1)}, u32[]{:S(2)}, u32[]{:S(2)}) collective-permute-start(f32[1,4,242,1]{3,1,2,0:T(4,128)S(1)} %get-tuple-element.24), channel_id=1, source_target_pairs={{16,0},{32,16},{48,32},{64,48},{80,64},{96,80},{112,96},{128,112},... | collective-permute-start | bytes 11624 | tf_op jit(solution)/shard_map/ppermute | solution.py:19
where the time goes:
time: 104 us
  other arithmetic  32.8 us (32%)
  starting transfers between devices  32.3 us (31%)
  local copies, waits for them, and re-layouts  27.1 us (26%)
  waiting for transfers between devices  10.4 us (10%)
    ppermute x4, starting transfers between devices, with_halo(): lax.ppermute(lax.slice_in_dim(block, 0, width, axis=dim), axis, backward)  21.9 us
    concatenate x1, other arithmetic, with_halo(): block = jnp.concatenate([low, block, high], axis=dim)  13 us
    unnamed x31, local copies, waits for them, and re-layouts  10 us
    add x1, other arithmetic, per_device(): new_pressure = pressure + (rhs_field - applied) / diag_total  9.08 us
    ppermute x4, waiting for transfers between devices, with_halo(): lax.ppermute(lax.slice_in_dim(block, block.shape[dim] - width, None, axis...  7.8 us
    ppermute x4, starting transfers between devices, with_halo(): lax.ppermute(lax.slice_in_dim(block, block.shape[dim] - width, None, axis...  5.89 us
    sub x1, other arithmetic, per_device(): return (new_pressure, rhs_field - applied_new)  5.77 us
    slice x3, local copies, waits for them, and re-layouts, with_halo(): lax.slice_in_dim(block, block.shape[dim] - width, None, axis=dim)  5.64 us
  transfers between devices with their start and end apart: 10, of which 3 were waited for; matrix products, arithmetic and copies ran while one was open for 6% of the time, Pallas kernels for 0%

commit v1 on v0

v1 whole, which is shorter than its diff:
```python
import math

import jax
import jax.numpy as jnp
from jax import lax
from jax.experimental import pallas as pl
from jax.experimental.pallas import tpu as pltpu
from jax.sharding import PartitionSpec as P

F32 = jnp.float32
AXES = ("lon", "lat")
LANES = 128
ROW_FIELDS = 7
COL_FIELDS = 5


def swap_pairs(lon_count, lat_count):
    def flat(lon, lat):
        return (lon % lon_count) * lat_count + lat

    rows_near, rows_far, cols_near, cols_far = [], [], [], []
    for lon in range(lon_count):
        for lat in range(lat_count):
            me = flat(lon, lat)
            rows_near.append((me, flat(lon, lat ^ 1)))
            if lat in (0, lat_count - 1):
                rows_far.append((me, flat(lon + lon_count // 2, lat)))
            else:
                rows_far.append((me, flat(lon, lat + 1 if lat % 2 else lat - 1)))
            cols_near.append((me, flat(lon ^ 1, lat)))
            cols_far.append((me, flat(lon + 1 if lon % 2 else lon - 1, lat)))
    return rows_near, rows_far, cols_near, cols_far


def face_cos(first, shape, axis, lat_total):
    position = (first + lax.broadcasted_iota(jnp.int32, shape, axis)).astype(F32)
    return jnp.cos(position * (math.pi / lat_total) - math.pi / 2)


def metric(cosine):
    return 0.5 * (1.0 + jnp.abs(cosine))


def up_level(x):
    return jnp.concatenate((x[1:], jnp.zeros_like(x[:1])), 0)


def down_level(x):
    return jnp.concatenate((jnp.zeros_like(x[:1]), x[:-1]), 0)


def one_cos(row, lat_total):
    return face_cos(row, (1, 2 * LANES), 0, lat_total)


def rows_kernel(lat_total, rows, *refs):
    low, high, (near_ref, far_ref) = refs[:8], refs[8:16], refs[16:]
    lat = lax.axis_index("lat")
    width = near_ref.shape[-1]
    lane = lax.broadcasted_iota(jnp.int32, (4, width), 1)

    def message(fields, edge, inner, face, sign):
        p, we, wn, forcing, clon, clat, cvert, diag = [f[:, edge, :] for f in fields]
        p_in, wn_in, clat_in = [fields[i][:, inner, :] for i in (0, 2, 5)]
        cosine = one_cos(face, lat_total)
        east = lane < width - 1
        w_east = jnp.where(east, 0.5 * (clon + pltpu.roll(clon, width - 1, 1)), 0.0)
        h_east = jnp.where(
            east,
            w_east * (pltpu.roll(p, width - 1, 1) - p) - 0.5 * (we + pltpu.roll(we, width - 1, 1)),
            0.0,
        )
        w_in = metric(cosine) * (0.5 * (clat + clat_in))
        h_in = w_in * (p_in - p) - sign * (0.5 * cosine * (wn + wn_in))
        w_up = up_level(cvert)
        h_up = w_up * (up_level(p) - p)
        below = cvert * (p - down_level(p))
        total = diag + w_east + pltpu.roll(w_east, 1, 1) + w_in + cvert + w_up
        number = forcing - diag * p + h_east - pltpu.roll(h_east, 1, 1) + h_in + h_up - below
        return jnp.concatenate((p, wn, clat, total, number, clon, we), 0)

    start = lat * rows
    south = message(low, 0, 1, start + 1, 1.0)
    north = message(high, 7, 6, start + rows - 1, -1.0)
    even = lat % 2 == 0
    near_ref[...] = jnp.where(even, north, south)
    far_ref[...] = jnp.where(even, south, north)


def rows_call(lat_total, fields):
    lev, rows, width = fields[0].shape
    low = pl.BlockSpec((lev, 8, width), lambda i: (0, 0, 0))
    high = pl.BlockSpec((lev, 8, width), lambda i: (0, rows // 8 - 1, 0))
    shape = jax.ShapeDtypeStruct((ROW_FIELDS * lev, width), F32)
    out = pl.BlockSpec((ROW_FIELDS * lev, width), lambda i: (0, 0))
    return pl.pallas_call(
        lambda *refs: rows_kernel(lat_total, rows, *refs),
        grid=(1,),
        in_specs=[low] * 8 + [high] * 8,
        out_specs=[out, out],
        out_shape=[shape, shape],
        name="row_messages",
    )(*fields, *fields)


CHUNKS = 5


def partial_kernel(lat_total, rows, *refs):
    hbm, (total_ref, number_ref, cols_ref) = refs[:8], refs[8:11]
    bufs, pack, sems = refs[11:19], refs[19], refs[20]
    lat = lax.axis_index("lat")
    start = lat * rows
    per = rows // CHUNKS

    def copy(chunk, field, tile):
        return pltpu.make_async_copy(
            hbm[field].at[:, pl.ds(chunk * per, per), pl.ds(tile * LANES, LANES)],
            bufs[field].at[tile, :, pl.ds(chunk * per, per), :],
            sems.at[chunk, field, tile],
        )

    for chunk in range(CHUNKS):
        for field in range(8):
            for tile in range(2):
                copy(chunk, field, tile).start()

    def wait(chunk):
        for field in range(8):
            for tile in range(2):
                copy(chunk, field, tile).wait()

    shape = (8, LANES)
    lane = lax.broadcasted_iota(jnp.int32, shape, 1)
    sub = lax.broadcasted_iota(jnp.int32, shape, 0)
    zero = jnp.zeros(shape, F32)
    pack[pl.ds(rows, 256 - rows), :] = jnp.zeros((256 - rows, LANES), F32)

    def east(t):
        a, b = pltpu.roll(t[0], LANES - 1, 1), pltpu.roll(t[1], LANES - 1, 1)
        return jnp.where(lane == LANES - 1, b, a), b

    def west(t):
        a, b = pltpu.roll(t[0], 1, 1), pltpu.roll(t[1], 1, 1)
        return jnp.where(lane == 0, b, a), jnp.where(lane == 0, a, b)

    def south(x, carried):
        rolled = pltpu.roll(x, 1, 0)
        return jnp.where(sub == 0, carried, rolled), rolled

    def step(r, carry):
        row = pl.multiple_of(r * 8, 8)
        cosine = face_cos(start + row + 1, shape, 0, lat_total)
        half_metric = 0.5 * metric(cosine)
        half_cos = 0.5 * cosine
        last = (row + sub) == rows - 1
        acc = zero
        p_here = [[bufs[0][t, k, pl.ds(row, 8), :] for t in range(2)] for k in range(4)]
        h_below = None
        new_carry = []
        for k in range(4):
            here = lambda f: [bufs[f][t, k, pl.ds(row, 8), :] for t in range(2)]
            above = lambda f: [bufs[f][t, k, pl.ds(row + 1, 8), :] for t in range(2)]
            p, we, wn, forcing, clon, clat, cvert, diag = (
                p_here[k], here(1), here(2), here(3), here(4), here(5), here(6), here(7),
            )
            p_up, wn_up, clat_up = above(0), above(2), above(5)
            p_e, we_e, clon_e = east(p), east(we), east(clon)
            w_e, h_e = [], []
            for t in range(2):
                w = 0.5 * (clon[t] + clon_e[t])
                h = w * (p_e[t] - p[t]) - 0.5 * (we[t] + we_e[t])
                if t == 1:
                    w, h = jnp.where(lane < LANES - 1, w, 0.0), jnp.where(lane < LANES - 1, h, 0.0)
                w_e.append(w)
                h_e.append(h)
            w_w, h_w = west(w_e), west(h_e)
            if k < 3:
                cvert_up = [bufs[6][t, k + 1, pl.ds(row, 8), :] for t in range(2)]
                h_above = [cvert_up[t] * (p_here[k + 1][t] - p[t]) for t in range(2)]
            total, number = [], []
            for t in range(2):
                w_n = jnp.where(last, 0.0, half_metric * (clat[t] + clat_up[t]))
                h_n = w_n * (p_up[t] - p[t]) - half_cos * (wn[t] + wn_up[t])
                h_n = jnp.where(last, 0.0, h_n)
                slot = (k * 2 + t) * 2
                w_s, w_c = south(w_n, carry[slot])
                h_s, h_c = south(h_n, carry[slot + 1])
                new_carry += [w_c, h_c]
                tt = diag[t] + w_e[t] + w_w[t] + w_n + w_s + cvert[t]
                nn = forcing[t] - diag[t] * p[t] + (h_e[t] - h_w[t]) + (h_n - h_s)
                nn = nn - (cvert[t] * p[t] if k == 0 else h_below[t])
                if k < 3:
                    tt = tt + cvert_up[t]
                    nn = nn + h_above[t]
                total_ref[t, k, pl.ds(row, 8), :] = tt
                number_ref[t, k, pl.ds(row, 8), :] = nn
                total.append(tt)
                number.append(nn)
            for side in range(2):
                for i, f in enumerate((p, we, clon, total, number)):
                    j = (side * COL_FIELDS + i) * 4 + k
                    source = 0 if side == 0 else LANES - 1
                    acc = jnp.where(lane == j, pltpu.roll(f[side], (j - source) % LANES, 1), acc)
            if k < 3:
                h_below = h_above
        pack[pl.ds(row, 8), :] = acc
        return tuple(new_carry)

    carry = tuple([zero] * 16)
    wait(0)
    for chunk in range(CHUNKS):
        if chunk + 1 < CHUNKS:
            wait(chunk + 1)
        carry = lax.fori_loop(chunk * per // 8, (chunk + 1) * per // 8, step, carry)
    cols_ref[...] = pack[...].T[: 2 * COL_FIELDS * 4]


def partial_call(lat_total, fields):
    lev, rows, width = fields[0].shape
    tiles = width // LANES
    plane = jax.ShapeDtypeStruct((tiles, lev, rows, LANES), F32)
    cols = jax.ShapeDtypeStruct((2 * COL_FIELDS * lev, 256), F32)
    vmem = pl.BlockSpec(memory_space=pltpu.VMEM)
    return pl.pallas_call(
        lambda *refs: partial_kernel(lat_total, rows, *refs),
        in_specs=[pl.BlockSpec(memory_space=pl.ANY)] * 8,
        out_specs=[vmem, vmem, vmem],
        out_shape=[plane, plane, cols],
        scratch_shapes=[pltpu.VMEM((tiles, lev, rows + 8, LANES), F32)] * 8
        + [pltpu.VMEM((256, LANES), F32), pltpu.SemaphoreType.DMA((CHUNKS, 8, tiles))],
        compiler_params=pltpu.CompilerParams(vmem_limit_bytes=40 * 2**20),
        cost_estimate=pl.CostEstimate(flops=20_000_000, bytes_accessed=10_000_000, transcendentals=0),
        name="partial_sums",
    )(*fields)


def edge_rows(own, halo, cosine, low):
    w = metric(cosine) * (0.5 * (own[8:12] + halo[8:12]))
    g = 0.5 * cosine * (own[4:8] + halo[4:8])
    f = w * (own[0:4] - halo[0:4]) if low else w * (halo[0:4] - own[0:4])
    return w, f, g


def pick(even, near, far):
    return jnp.where(even, far, near), jnp.where(even, near, far)


def columns_kernel(lat_total, rows, cols, near, far, near_in, far_in, near_ref, far_ref):
    lat, lon = lax.axis_index("lat"), lax.axis_index("lon")
    even = lat % 2 == 0
    own_s, own_n = pick(even, near[...], far[...])
    halo_s, halo_n = pick(even, near_in[...], far_in[...])
    w_s, f_s, g_s = edge_rows(own_s, halo_s, one_cos(lat * rows, lat_total), True)
    w_n, f_n, g_n = edge_rows(own_n, halo_n, one_cos((lat + 1) * rows, lat_total), False)
    h_s, h_n = f_s - g_s, f_n - g_n
    width = w_s.shape[-1]
    lane = lax.broadcasted_iota(jnp.int32, (4, width), 1)

    def side(at):
        source = 0 if at == 0 else width - 1
        base = at * COL_FIELDS * 4
        p, we, clon, total, number = [cols[pl.ds(base + i * 4, 4), :] for i in range(COL_FIELDS)]

        def put(x, value, target):
            return jnp.where(lane == target, pltpu.roll(value, (target - source) % width, 1), x)

        no = jnp.zeros_like(p)
        total = total + put(put(no, w_s, 0), w_n, rows - 1)
        number = number + put(put(no, -h_s, 0), h_n, rows - 1)
        p = put(put(p, halo_s[0:4], rows), halo_n[0:4], rows + 1)
        clon = put(put(clon, halo_s[20:24], rows), halo_n[20:24], rows + 1)
        we = put(put(we, halo_s[24:28], rows), halo_n[24:28], rows + 1)
        return jnp.concatenate((p, we, clon, total, number), 0)

    west, east = side(0), side(1)
    lon_even = lon % 2 == 0
    near_ref[...] = jnp.where(lon_even, east, west)
    far_ref[...] = jnp.where(lon_even, west, east)


def columns_call(lat_total, rows, cols, near, far, near_in, far_in):
    shape = jax.ShapeDtypeStruct((cols.shape[0] // 2, cols.shape[1]), F32)
    vmem = pl.BlockSpec(memory_space=pltpu.VMEM)
    return pl.pallas_call(
        lambda *refs: columns_kernel(lat_total, rows, *refs),
        in_specs=[vmem] * 5,
        out_specs=[vmem, vmem],
        out_shape=[shape, shape],
        name="column_messages",
    )(cols, near, far, near_in, far_in)


def final_kernel(lat_total, rows, *refs):
    (p_hbm, clon_hbm, clat_hbm, cvert_hbm, total_ref, number_ref) = refs[:6]
    rn, rf, rn_in, rf_in, cn, cf, cn_in, cf_in = refs[6:14]
    new_ref, res_ref = refs[14:16]
    pb, lonb, latb, vertb, delta, colv, sems = refs[16:]
    bufs = (pb, lonb, latb, vertb)
    hbm = (p_hbm, clon_hbm, clat_hbm, cvert_hbm)
    lat, lon = lax.axis_index("lat"), lax.axis_index("lon")

    def copy(field, tile):
        return pltpu.make_async_copy(
            hbm[field].at[:, :, pl.ds(tile * LANES, LANES)],
            bufs[field].at[tile, :, pl.ds(0, rows), :],
            sems.at[field, tile],
        )

    for field in range(4):
        for tile in range(2):
            copy(field, tile).start()

    width = 2 * LANES
    wide = lax.broadcasted_iota(jnp.int32, (4, width), 1)
    even = lat % 2 == 0
    own_s, own_n = pick(even, rn[...], rf[...])
    halo_s, halo_n = pick(even, rn_in[...], rf_in[...])
    w_s, f_s, g_s = edge_rows(own_s, halo_s, one_cos(lat * rows, lat_total), True)
    w_n, f_n, g_n = edge_rows(own_n, halo_n, one_cos((lat + 1) * rows, lat_total), False)
    lon_even = lon % 2 == 0
    own_w, own_e = pick(lon_even, cn[...], cf[...])
    halo_w, halo_e = pick(lon_even, cn_in[...], cf_in[...])

    def edge_cols(own, halo, sign):
        w = 0.5 * (own[8:12] + halo[8:12])
        h = sign * w * (own[0:4] - halo[0:4]) - 0.5 * (own[4:8] + halo[4:8])
        d_own = (own[16:20] - sign * h) / (own[12:16] + w)
        d_halo = (halo[16:20] + sign * h) / (halo[12:16] + w)
        inside = wide < rows
        return w, h, jnp.where(inside, d_own, 0.0), jnp.where(inside, w * d_halo, 0.0)

    w_w, h_w, d_w, r_w = edge_cols(own_w, halo_w, 1.0)
    w_e, h_e, d_e, r_e = edge_cols(own_e, halo_e, -1.0)

    def put(x, value, source, target):
        return jnp.where(wide == target, pltpu.roll(value, (target - source) % width, 1), x)

    no = jnp.zeros((4, width), F32)

    def halo_delta(halo, w, f, g, source, low, pole):
        add_w = put(put(no, w_w, source, 0), w_e, source, width - 1)
        add_h = put(put(no, -h_w, source, 0), h_e, source, width - 1)
        turned = jnp.where(pole, -g, g)
        flux = f - turned if low else turned - f
        return (halo[16:20] + add_h + flux) / (halo[12:16] + add_w + w)

    lat_last = lax.axis_size("lat") - 1
    d_s = halo_delta(halo_s, w_s, f_s, g_s, rows, True, lat == 0)
    d_n = halo_delta(halo_n, w_n, f_n, g_n, rows + 1, False, lat == lat_last)
    r_s, r_n = w_s * d_s, w_n * d_n
    row_s = (own_s[16:20] - (f_s - g_s)) / (own_s[12:16] + w_s)
    row_n = (own_n[16:20] + (f_n - g_n)) / (own_n[12:16] + w_n)
    row_s = put(put(row_s, d_w, 0, 0), d_e, 0, width - 1)
    row_n = put(put(row_n, d_w, rows - 1, 0), d_e, rows - 1, width - 1)
    stack = jnp.concatenate((d_w, d_e, r_w, r_e, jnp.zeros((LANES - 16, width), F32)), 0)
    colv[...] = stack.T

    for field in range(4):
        for tile in range(2):
            copy(field, tile).wait()

    shape = (8, LANES)
    lane = lax.broadcasted_iota(jnp.int32, shape, 1)
    sub = lax.broadcasted_iota(jnp.int32, shape, 0)
    zero = jnp.zeros(shape, F32)
    edge = (0, LANES - 1)

    def first(r, carry):
        row = pl.multiple_of(r * 8, 8)
        packed = colv[pl.ds(row, 8), :]
        for k in range(4):
            for t in range(2):
                d = number_ref[t, k, pl.ds(row, 8), :] / total_ref[t, k, pl.ds(row, 8), :]
                column = pltpu.roll(packed, (edge[t] - (t * 4 + k)) % LANES, 1)
                d = jnp.where(lane == edge[t], column, d)
                delta[t, k, pl.ds(row + 8, 8), :] = d
                new_ref[k, pl.ds(row, 8), pl.ds(t * LANES, LANES)] = pb[t, k, pl.ds(row, 8), :] + d
        return carry

    lax.fori_loop(0, rows // 8, first, 0)
    for k in range(4):
        for t in range(2):
            cut = slice(t * LANES, (t + 1) * LANES)
            delta[t, k, 7:8, :] = jnp.zeros((1, LANES), F32)
            delta[t, k, rows + 8 : rows + 9, :] = jnp.zeros((1, LANES), F32)
            for at, value in ((0, row_s), (rows - 1, row_n)):
                delta[t, k, at + 8 : at + 9, :] = value[k : k + 1, cut]
                new_ref[k, at : at + 1, cut] = pb[t, k, at : at + 1, :] + value[k : k + 1, cut]

    start = lat * rows

    def second(r, carry):
        row = pl.multiple_of(r * 8, 8)
        packed = colv[pl.ds(row, 8), :]
        cosine = face_cos(start + row + 1, shape, 0, lat_total)
        half_metric = 0.5 * metric(cosine)
        last = (row + sub) == rows - 1
        new_carry = []
        d_here = [[delta[t, k, pl.ds(row + 8, 8), :] for t in range(2)] for k in range(4)]
        for k in range(4):
            d = d_here[k]
            clon = [lonb[t, k, pl.ds(row, 8), :] for t in range(2)]
            c0, c1 = [pltpu.roll(c, LANES - 1, 1) for c in clon]
            e0, e1 = [pltpu.roll(x, LANES - 1, 1) for x in d]
            w0 = 0.5 * (clon[0] + jnp.where(lane == LANES - 1, c1, c0))
            w1 = jnp.where(lane < LANES - 1, 0.5 * (clon[1] + c1), 0.0)
            east = w0 * jnp.where(lane == LANES - 1, e1, e0), w1 * e1
            v0, v1 = pltpu.roll(w0 * d[0], 1, 1), pltpu.roll(w1 * d[1], 1, 1)
            west = jnp.where(lane == 0, v1, v0), jnp.where(lane == 0, v0, v1)
            for t in range(2):
                clat = latb[t, k, pl.ds(row, 8), :]
                clat_up = latb[t, k, pl.ds(row + 1, 8), :]
                w_north = jnp.where(last, 0.0, half_metric * (clat + clat_up))
                sent = pltpu.roll(w_north * d[t], 1, 0)
                from_south = jnp.where(sub == 0, carry[k * 2 + t], sent)
                new_carry.append(sent)
                out = east[t] + west[t] + w_north * delta[t, k, pl.ds(row + 9, 8), :] + from_south
                if k > 0:
                    out = out + vertb[t, k, pl.ds(row, 8), :] * d_here[k - 1][t]
                if k < 3:
                    out = out + vertb[t, k + 1, pl.ds(row, 8), :] * d_here[k + 1][t]
                column = pltpu.roll(packed, (edge[t] - (8 + t * 4 + k)) % LANES, 1)
                out = out + jnp.where(lane == edge[t], column, 0.0)
                res_ref[k, pl.ds(row, 8), pl.ds(t * LANES, LANES)] = out
        return tuple(new_carry)

    lax.fori_loop(0, rows // 8, second, tuple([zero] * 8))
    for k in range(4):
        for t in range(2):
            cut = slice(t * LANES, (t + 1) * LANES)
            for at, value in ((0, r_s), (rows - 1, r_n)):
                res_ref[k, at : at + 1, cut] = res_ref[k, at : at + 1, cut] + value[k : k + 1, cut]


def final_call(lat_total, fields, planes, messages):
    lev, rows, width = fields[0].shape
    tiles = width // LANES
    vmem = pl.BlockSpec(memory_space=pltpu.VMEM)
    shape = jax.ShapeDtypeStruct(fields[0].shape, F32)
    buf = pltpu.VMEM((tiles, lev, rows + 8, LANES), F32)
    return pl.pallas_call(
        lambda *refs: final_kernel(lat_total, rows, *refs),
        in_specs=[pl.BlockSpec(memory_space=pl.ANY)] * 4 + [vmem] * 10,
        out_specs=[vmem, vmem],
        out_shape=[shape, shape],
        scratch_shapes=[buf] * 4
        + [
            pltpu.VMEM((tiles, lev, rows + 24, LANES), F32),
            pltpu.VMEM((256, LANES), F32),
            pltpu.SemaphoreType.DMA((4, tiles)),
        ],
        compiler_params=pltpu.CompilerParams(vmem_limit_bytes=40 * 2**20),
        name="corrected",
    )(*fields, *planes, *messages)


def per_device(pressure, wind_east, wind_north, forcing, coef_lon, coef_lat, coef_vert, diag_coef):
    fields = (pressure, wind_east, wind_north, forcing, coef_lon, coef_lat, coef_vert, diag_coef)
    rows = pressure.shape[1]
    lat_total = rows * lax.axis_size("lat")
    rows_near, rows_far, cols_near, cols_far = swap_pairs(
        lax.axis_size("lon"), lax.axis_size("lat")
    )
    near, far = rows_call(lat_total, fields)
    far_in = lax.ppermute(far, AXES, rows_far)
    near_in = lax.ppermute(near, AXES, rows_near)
    total, number, cols = partial_call(lat_total, fields)
    col_near, col_far = columns_call(lat_total, rows, cols, near, far, near_in, far_in)
    col_far_in = lax.ppermute(col_far, AXES, cols_far)
    col_near_in = lax.ppermute(col_near, AXES, cols_near)
    return final_call(
        lat_total,
        (pressure, coef_lon, coef_lat, coef_vert),
        (total, number),
        (near, far, near_in, far_in, col_near, col_far, col_near_in, col_far_in),
    )


def solution(mesh):
    spec = P(None, "lat", "lon")
    return jax.shard_map(
        per_device, mesh=mesh, in_specs=(spec,) * 8, out_specs=(spec, spec), check_vma=False
    )
```

time: 104 us -> 52.1 us (0.50)
  other arithmetic: 32.8 us -> 0 us
  Pallas kernels: 0 us -> 21.1 us
  starting transfers between devices: 32.3 us -> 11.8 us
  local copies, waits for them, and re-layouts: 27.1 us -> 15.7 us
  waiting for transfers between devices: 10.4 us -> 2.02 us
    pallas_call x0 -> x4, Pallas kernels: none -> 21.1 us  [the longest x1 8.99 us: partial_call(): pl.pallas_call(lambda *refs: partial_kernel(lat_total, rows, *refs), in_s...]
    ppermute x10 -> x4, starting transfers between devices: 32.3 us -> 11.8 us  [the longest x1 6.8 us: per_device(): col_far_in = lax.ppermute(col_far, AXES, cols_far)]
    concatenate x3 -> x0, other arithmetic: 16.7 us -> none  [the longest x1 13 us: with_halo(): block = jnp.concatenate([low, block, high], axis=dim)]
    slice x10 -> x0, local copies, waits for them, and re-layouts: 10.7 us -> none  [the longest x3 5.64 us: with_halo(): lax.slice_in_dim(block, block.shape[dim] - width, None, axis=dim)]
    add x1 -> x0, other arithmetic: 9.08 us -> none  [per_device(): new_pressure = pressure + (rhs_field - applied) / diag_total]
    ppermute x10 -> x4, waiting for transfers between devices: 10.4 us -> 2.02 us  [the longest x1 2.01 us: per_device(): col_far_in = lax.ppermute(col_far, AXES, cols_far)]
    sub x1 -> x0, other arithmetic: 5.77 us -> none  [per_device(): return (new_pressure, rhs_field - applied_new)]
    unnamed x31 -> x44, local copies, waits for them, and re-layouts: 10 us -> 15.7 us
  transfers between devices with their start and end apart: 10 -> 4, of which waited for: 3 -> 1; matrix products, arithmetic and copies ran while one was open for 6% -> 0% of each run, Pallas kernels for 0% -> 17%
where the time goes in v1:
time: 52.1 us; the launch traced here: 51.4 us
  Pallas kernels  21.1 us (40%)
  local copies, waits for them, and re-layouts  15.7 us (30%)
  starting transfers between devices  11.8 us (23%)
  waiting for transfers between devices  2.02 us (4%)
  between operations  0.71 us (1%)
    unnamed x44, local copies, waits for them, and re-layouts  15.7 us
    pallas_call x1, Pallas kernels, partial_call(): pl.pallas_call(lambda *refs: partial_kernel(lat_total, rows, *refs), in_s...  8.99 us
    pallas_call x1, Pallas kernels, final_call(): pl.pallas_call(lambda *refs: final_kernel(lat_total, rows, *refs), in_spe...  8.58 us
    ppermute x1, starting transfers between devices, per_device(): col_far_in = lax.ppermute(col_far, AXES, cols_far)  6.8 us
    ppermute x1, starting transfers between devices, per_device(): far_in = lax.ppermute(far, AXES, rows_far)  3.1 us
    ppermute x1, waiting for transfers between devices, per_device(): col_far_in = lax.ppermute(col_far, AXES, cols_far)  2.01 us
    pallas_call x1, Pallas kernels, rows_call(): pl.pallas_call(lambda *refs: rows_kernel(lat_total, rows, *refs), grid=(1...  1.95 us
    ppermute x1, starting transfers between devices, per_device(): col_near_in = lax.ppermute(col_near, AXES, cols_near)  1.92 us
  transfers between devices with their start and end apart: 4, of which 1 were waited for; matrix products, arithmetic and copies ran while one was open for 0% of the time, Pallas kernels for 17%

profile of v1, /device:TPU:2, one launch (start us, length us, event | category | flops | bytes accessed | tf_op | source)
XLA Modules:
  0.0 51.4 jit_solution(8568937857732876274)
XLA Ops:
  0.7 2.0 %row_messages.1 = (f32[28,256]{1,0:T(8,128)}, f32[28,256]{1,0:T(8,128)}) custom-call(f32[4,240,256]{2,1,0:T(8,128)} %refs_0_.5, f32[4,240,256]{2,1,0:T(8,128)} %refs_9_.1, f32[4,240,256]{2,1,0:T(8,128)} %refs_10_.1, f32[4,240,256]{2,1,0:T(8,128)} %refs_11_.1, f32[4,240,256]{2,1,0:T(8,128)} %refs_1_.5, f32[4,240,256]{2,1,0:T(8,128)} %refs_2_.5, ...), custom_call_target="tpu_custom_call" | custom-call | tf_op jit(solution)/shard_map/row_messages/pallas_call | solution.py:96
  2.6 0.0 collective-permute-start
  2.6 3.1 %collective-permute-start.1 = (f32[28,256]{1,0:T(8,128)}, f32[28,256]{1,0:T(8,128)S(1)}, u32[]{:S(2)}, u32[]{:S(2)}) collective-permute-start(f32[28,256]{1,0:T(8,128)} %get-tuple-element.12.refs_2_.refs_7_), channel_id=1, source_target_pairs={{0,128},{1,2},{2,1},{3,4},{4,3},{5,6},{6,5},{7,8},{8,7},{9,10},{10... | collective-permute-start | bytes 86024 | tf_op jit(solution)/shard_map/ppermute | solution.py:466
  5.7 0.0 copy-done.2
  5.7 0.0 copy-done
  5.7 1.2 %copy-done.3 = f32[4,240,256]{2,1,0:T(8,128)S(1)} copy-done((f32[4,240,256]{2,1,0:T(8,128)S(1)}, f32[4,240,256]{2,1,0:T(8,128)}, u32[]{:S(2)}) %copy-start.3) | copy-done | bytes 983064
  6.9 1.2 %copy-done.5 = f32[4,240,256]{2,1,0:T(8,128)S(1)} copy-done((f32[4,240,256]{2,1,0:T(8,128)S(1)}, f32[4,240,256]{2,1,0:T(8,128)}, u32[]{:S(2)}) %copy-start.5) | copy-done | bytes 983064
  8.1 1.2 %copy-done.6 = f32[4,240,256]{2,1,0:T(8,128)S(1)} copy-done((f32[4,240,256]{2,1,0:T(8,128)S(1)}, f32[4,240,256]{2,1,0:T(8,128)}, u32[]{:S(2)}) %copy-start.6) | copy-done | bytes 983064
  9.3 1.2 %copy-done.7 = f32[4,240,256]{2,1,0:T(8,128)S(1)} copy-done((f32[4,240,256]{2,1,0:T(8,128)S(1)}, f32[4,240,256]{2,1,0:T(8,128)}, u32[]{:S(2)}) %copy-start.7) | copy-done | bytes 983064
  10.5 1.2 %copy-done.8 = f32[4,240,256]{2,1,0:T(8,128)S(1)} copy-done((f32[4,240,256]{2,1,0:T(8,128)S(1)}, f32[4,240,256]{2,1,0:T(8,128)}, u32[]{:S(2)}) %copy-start.8) | copy-done | bytes 983064
  11.7 9.0 %partial_sums.1 = (f32[2,4,240,128]{3,2,1,0:T(8,128)S(1)}, f32[2,4,240,128]{3,2,1,0:T(8,128)S(1)}, f32[40,256]{1,0:T(8,128)S(1)}) custom-call(f32[4,240,256]{2,1,0:T(8,128)S(1)} %copy-done, f32[4,240,256]{2,1,0:T(8,128)S(1)} %copy-done.5, f32[4,240,256]{2,1,0:T(8,128)S(1)} %copy-done.6, f32[4,240,256]{2,1,0:T(8,128)S(1)} %copy-done.7, ...), custom_call_target="tpu_custom_call" | custom-call | flops 20000000 | bytes 10000000 | tf_op jit(solution)/shard_map/partial_sums/pallas_call | solution.py:225
  20.7 0.0 copy-start.9
  20.7 0.9 %copy-done.9 = f32[2,4,240,128]{3,2,1,0:T(8,128)} copy-done((f32[2,4,240,128]{3,2,1,0:T(8,128)}, f32[2,4,240,128]{3,2,1,0:T(8,128)S(1)}, u32[]{:S(2)}) %copy-start.9) | copy-done | bytes 983064
  21.7 0.9 %copy-done.11 = f32[2,4,240,128]{3,2,1,0:T(8,128)} copy-done((f32[2,4,240,128]{3,2,1,0:T(8,128)}, f32[2,4,240,128]{3,2,1,0:T(8,128)S(1)}, u32[]{:S(2)}) %copy-start.11) | copy-done | bytes 983064
  22.6 0.6 %copy-done.19 = f32[40,256]{1,0:T(8,128)} copy-done((f32[40,256]{1,0:T(8,128)}, f32[40,256]{1,0:T(8,128)S(1)}, u32[]{:S(2)}) %copy-start.19) | copy-done | bytes 40984
  23.2 0.0 collective-permute-done.refs_3_.refs_8_
  23.2 0.0 collective-permute-done.1.refs_4_.refs_9_
  23.3 0.6 %copy-done.15 = f32[28,256]{1,0:T(8,128)} copy-done((f32[28,256]{1,0:T(8,128)}, f32[28,256]{1,0:T(8,128)S(1)}, u32[]{:S(2)}) %copy-start.15) | copy-done | bytes 28696
  23.8 0.0 copy-done.17
  23.9 1.6 %column_messages.1 = (f32[20,256]{1,0:T(8,128)}, f32[20,256]{1,0:T(8,128)}) custom-call(f32[40,256]{1,0:T(8,128)} %copy-done.19, f32[28,256]{1,0:T(8,128)} %get-tuple-element.11.refs_1_.refs_6_, f32[28,256]{1,0:T(8,128)} %get-tuple-element.12.refs_2_.refs_7_, f32[28,256]{1,0:T(8,128)} %copy-done.15, f32[28,256]{1,0:T(8,128)} %copy-done.17), custom_call_target="tpu_custom_call" | custom-call | tf_op jit(solution)/shard_map/column_messages/pallas_call | solution.py:285
  25.5 1.9 %collective-permute-start.2 = (f32[20,256]{1,0:T(8,128)}, f32[20,256]{1,0:T(8,128)S(1)}, u32[]{:S(2)}, u32[]{:S(2)}) collective-permute-start(f32[20,256]{1,0:T(8,128)} %get-tuple-element.14.refs_10_), channel_id=1, source_target_pairs={{0,16},{1,17},{2,18},{3,19},{4,20},{5,21},{6,22},{7,23},{8,24},{9,... | collective-permute-start | bytes 61448 | tf_op jit(solution)/shard_map/ppermute | solution.py:471
  27.4 6.8 %collective-permute-start.3 = (f32[20,256]{1,0:T(8,128)}, f32[20,256]{1,0:T(8,128)S(1)}, u32[]{:S(2)}, u32[]{:S(2)}) collective-permute-start(f32[20,256]{1,0:T(8,128)} %get-tuple-element.15.refs_11_), channel_id=1, source_target_pairs={{0,240},{1,241},{2,242},{3,243},{4,244},{5,245},{6,246},{7,247},{8... | collective-permute-start | bytes 61448 | tf_op jit(solution)/shard_map/ppermute | solution.py:470
  34.2 0.0 collective-permute-done.2.refs_12_
  34.2 2.0 %collective-permute-done.3.refs_13_ = f32[20,256]{1,0:T(8,128)S(1)} collective-permute-done((f32[20,256]{1,0:T(8,128)}, f32[20,256]{1,0:T(8,128)S(1)}, u32[]{:S(2)}, u32[]{:S(2)}) %collective-permute-start.3) | collective-permute-done | bytes 20512 | tf_op jit(solution)/shard_map/ppermute | solution.py:470
  36.2 1.2 %copy-done.4 = f32[4,240,256]{2,1,0:T(8,128)S(1)} copy-done((f32[4,240,256]{2,1,0:T(8,128)S(1)}, f32[4,240,256]{2,1,0:T(8,128)}, u32[]{:S(2)}) %copy-start.4) | copy-done | bytes 983064
  37.4 1.2 %copy-done.10 = f32[2,4,240,128]{3,2,1,0:T(8,128)S(1)} copy-done((f32[2,4,240,128]{3,2,1,0:T(8,128)S(1)}, f32[2,4,240,128]{3,2,1,0:T(8,128)}, u32[]{:S(2)}) %copy-start.10) | copy-done | bytes 983064
  38.6 1.2 %copy-done.12 = f32[2,4,240,128]{3,2,1,0:T(8,128)S(1)} copy-done((f32[2,4,240,128]{3,2,1,0:T(8,128)S(1)}, f32[2,4,240,128]{3,2,1,0:T(8,128)}, u32[]{:S(2)}) %copy-start.12) | copy-done | bytes 983064
  39.8 0.8 %copy-done.16 = f32[28,256]{1,0:T(8,128)S(1)} copy-done((f32[28,256]{1,0:T(8,128)S(1)}, f32[28,256]{1,0:T(8,128)}, u32[]{:S(2)}) %copy-start.16) | copy-done | bytes 28696
  40.6 0.8 %copy-done.18 = f32[28,256]{1,0:T(8,128)S(1)} copy-done((f32[28,256]{1,0:T(8,128)S(1)}, f32[28,256]{1,0:T(8,128)}, u32[]{:S(2)}) %copy-start.18) | copy-done | bytes 28696
  41.3 0.7 %copy-done.20 = f32[20,256]{1,0:T(8,128)S(1)} copy-done((f32[20,256]{1,0:T(8,128)S(1)}, f32[20,256]{1,0:T(8,128)}, u32[]{:S(2)}) %copy-start.20) | copy-done | bytes 20504
  42.1 0.7 %copy-done.21 = f32[20,256]{1,0:T(8,128)S(1)} copy-done((f32[20,256]{1,0:T(8,128)S(1)}, f32[20,256]{1,0:T(8,128)}, u32[]{:S(2)}) %copy-start.21) | copy-done | bytes 20504
  42.8 8.6 %corrected.1 = (f32[4,240,256]{2,1,0:T(8,128)}, f32[4,240,256]{2,1,0:T(8,128)}) custom-call(f32[4,240,256]{2,1,0:T(8,128)S(1)} %copy-done, f32[4,240,256]{2,1,0:T(8,128)S(1)} %copy-done.1, f32[4,240,256]{2,1,0:T(8,128)S(1)} %copy-done.2, f32[4,240,256]{2,1,0:T(8,128)S(1)} %copy-done.4, f32[2,4,240,128]{3,2,1,0:T(8,128)S(1)} %copy-done.10, ...), custom_call_target="tpu_custom_call" | custom-call | tf_op jit(solution)/shard_map/corrected/pallas_call | solution.py:442
  (24 shorter events, 0.0 us)
Async XLA Ops:
  0.6 5.1 %copy-start.2 = (f32[4,240,256]{2,1,0:T(8,128)S(1)}, f32[4,240,256]{2,1,0:T(8,128)}, u32[]{:S(2)}) copy-start(f32[4,240,256]{2,1,0:T(8,128)} %refs_2_.5) | copy-start | bytes 2949124
  0.6 5.1 %copy-start.1 = (f32[4,240,256]{2,1,0:T(8,128)S(1)}, f32[4,240,256]{2,1,0:T(8,128)}, u32[]{:S(2)}) copy-start(f32[4,240,256]{2,1,0:T(8,128)} %refs_1_.5) | copy-start | bytes 2949124
  0.6 5.1 %copy-start = (f32[4,240,256]{2,1,0:T(8,128)S(1)}, f32[4,240,256]{2,1,0:T(8,128)}, u32[]{:S(2)}) copy-start(f32[4,240,256]{2,1,0:T(8,128)} %refs_0_.5) | copy-start | bytes 2949124
  2.6 20.6 %collective-permute-start = (f32[28,256]{1,0:T(8,128)}, f32[28,256]{1,0:T(8,128)S(1)}, u32[]{:S(2)}, u32[]{:S(2)}) collective-permute-start(f32[28,256]{1,0:T(8,128)} %get-tuple-element.11.refs_1_.refs_6_), channel_id=1, source_target_pairs={{0,1},{1,0},{2,3},{3,2},{4,5},{5,4},{6,7},{7,6},{8,9},{9,8},{10,11... | collective-permute-start | bytes 86024 | tf_op jit(solution)/shard_map/ppermute | solution.py:467
  2.6 20.6 %collective-permute-start.1 = (f32[28,256]{1,0:T(8,128)}, f32[28,256]{1,0:T(8,128)S(1)}, u32[]{:S(2)}, u32[]{:S(2)}) collective-permute-start(f32[28,256]{1,0:T(8,128)} %get-tuple-element.12.refs_2_.refs_7_), channel_id=1, source_target_pairs={{0,128},{1,2},{2,1},{3,4},{4,3},{5,6},{6,5},{7,8},{8,7},{9,10},{10... | collective-permute-start | bytes 86024 | tf_op jit(solution)/shard_map/ppermute | solution.py:466
  5.7 1.2 %copy-start.3 = (f32[4,240,256]{2,1,0:T(8,128)S(1)}, f32[4,240,256]{2,1,0:T(8,128)}, u32[]{:S(2)}) copy-start(f32[4,240,256]{2,1,0:T(8,128)} %refs_3_.5) | copy-start | bytes 2949124
  6.9 1.2 %copy-start.5 = (f32[4,240,256]{2,1,0:T(8,128)S(1)}, f32[4,240,256]{2,1,0:T(8,128)}, u32[]{:S(2)}) copy-start(f32[4,240,256]{2,1,0:T(8,128)} %refs_9_.1) | copy-start | bytes 2949124
  8.1 1.2 %copy-start.6 = (f32[4,240,256]{2,1,0:T(8,128)S(1)}, f32[4,240,256]{2,1,0:T(8,128)}, u32[]{:S(2)}) copy-start(f32[4,240,256]{2,1,0:T(8,128)} %refs_10_.1) | copy-start | bytes 2949124
  9.3 1.2 %copy-start.7 = (f32[4,240,256]{2,1,0:T(8,128)S(1)}, f32[4,240,256]{2,1,0:T(8,128)}, u32[]{:S(2)}) copy-start(f32[4,240,256]{2,1,0:T(8,128)} %refs_11_.1) | copy-start | bytes 2949124
  10.5 1.2 %copy-start.8 = (f32[4,240,256]{2,1,0:T(8,128)S(1)}, f32[4,240,256]{2,1,0:T(8,128)}, u32[]{:S(2)}) copy-start(f32[4,240,256]{2,1,0:T(8,128)} %refs_15_.1) | copy-start | bytes 2949124
  20.7 0.9 %copy-start.9 = (f32[2,4,240,128]{3,2,1,0:T(8,128)}, f32[2,4,240,128]{3,2,1,0:T(8,128)S(1)}, u32[]{:S(2)}) copy-start(f32[2,4,240,128]{3,2,1,0:T(8,128)S(1)} %get-tuple-element.9.refs_4_) | copy-start | bytes 2949124
  21.7 0.9 %copy-start.11 = (f32[2,4,240,128]{3,2,1,0:T(8,128)}, f32[2,4,240,128]{3,2,1,0:T(8,128)S(1)}, u32[]{:S(2)}) copy-start(f32[2,4,240,128]{3,2,1,0:T(8,128)S(1)} %get-tuple-element.10.refs_5_) | copy-start | bytes 2949124
  22.6 0.6 %copy-start.19 = (f32[40,256]{1,0:T(8,128)}, f32[40,256]{1,0:T(8,128)S(1)}, u32[]{:S(2)}) copy-start(f32[40,256]{1,0:T(8,128)S(1)} %get-tuple-element.13.refs_0_) | copy-start | bytes 122884
  23.2 0.6 %copy-start.15 = (f32[28,256]{1,0:T(8,128)}, f32[28,256]{1,0:T(8,128)S(1)}, u32[]{:S(2)}) copy-start(f32[28,256]{1,0:T(8,128)S(1)} %collective-permute-done.refs_3_.refs_8_) | copy-start | bytes 86020
  23.2 0.6 %copy-start.17 = (f32[28,256]{1,0:T(8,128)}, f32[28,256]{1,0:T(8,128)S(1)}, u32[]{:S(2)}) copy-start(f32[28,256]{1,0:T(8,128)S(1)} %collective-permute-done.1.refs_4_.refs_9_) | copy-start | bytes 86020
  23.9 12.3 %copy-start.13 = (f32[28,256]{1,0:T(8,128)S(1)}, f32[28,256]{1,0:T(8,128)}, u32[]{:S(2)}) copy-start(f32[28,256]{1,0:T(8,128)} %get-tuple-element.11.refs_1_.refs_6_) | copy-start | bytes 86020
  23.9 12.3 %copy-start.14 = (f32[28,256]{1,0:T(8,128)S(1)}, f32[28,256]{1,0:T(8,128)}, u32[]{:S(2)}) copy-start(f32[28,256]{1,0:T(8,128)} %get-tuple-element.12.refs_2_.refs_7_) | copy-start | bytes 86020
  25.5 8.7 %collective-permute-start.2 = (f32[20,256]{1,0:T(8,128)}, f32[20,256]{1,0:T(8,128)S(1)}, u32[]{:S(2)}, u32[]{:S(2)}) collective-permute-start(f32[20,256]{1,0:T(8,128)} %get-tuple-element.14.refs_10_), channel_id=1, source_target_pairs={{0,16},{1,17},{2,18},{3,19},{4,20},{5,21},{6,22},{7,23},{8,24},{9,... | collective-permute-start | bytes 61448 | tf_op jit(solution)/shard_map/ppermute | solution.py:471
  27.4 8.8 %collective-permute-start.3 = (f32[20,256]{1,0:T(8,128)}, f32[20,256]{1,0:T(8,128)S(1)}, u32[]{:S(2)}, u32[]{:S(2)}) collective-permute-start(f32[20,256]{1,0:T(8,128)} %get-tuple-element.15.refs_11_), channel_id=1, source_target_pairs={{0,240},{1,241},{2,242},{3,243},{4,244},{5,245},{6,246},{7,247},{8... | collective-permute-start | bytes 61448 | tf_op jit(solution)/shard_map/ppermute | solution.py:470
  36.2 1.2 %copy-start.4 = (f32[4,240,256]{2,1,0:T(8,128)S(1)}, f32[4,240,256]{2,1,0:T(8,128)}, u32[]{:S(2)}) copy-start(f32[4,240,256]{2,1,0:T(8,128)} %refs_3_.5) | copy-start | bytes 2949124
  37.4 1.2 %copy-start.10 = (f32[2,4,240,128]{3,2,1,0:T(8,128)S(1)}, f32[2,4,240,128]{3,2,1,0:T(8,128)}, u32[]{:S(2)}) copy-start(f32[2,4,240,128]{3,2,1,0:T(8,128)} %copy-done.9) | copy-start | bytes 2949124
  38.6 1.2 %copy-start.12 = (f32[2,4,240,128]{3,2,1,0:T(8,128)S(1)}, f32[2,4,240,128]{3,2,1,0:T(8,128)}, u32[]{:S(2)}) copy-start(f32[2,4,240,128]{3,2,1,0:T(8,128)} %copy-done.11) | copy-start | bytes 2949124
  39.8 0.8 %copy-start.16 = (f32[28,256]{1,0:T(8,128)S(1)}, f32[28,256]{1,0:T(8,128)}, u32[]{:S(2)}) copy-start(f32[28,256]{1,0:T(8,128)} %copy-done.15) | copy-start | bytes 86020
  40.6 0.8 %copy-start.18 = (f32[28,256]{1,0:T(8,128)S(1)}, f32[28,256]{1,0:T(8,128)}, u32[]{:S(2)}) copy-start(f32[28,256]{1,0:T(8,128)} %copy-done.17) | copy-start | bytes 86020
  41.3 0.7 %copy-start.20 = (f32[20,256]{1,0:T(8,128)S(1)}, f32[20,256]{1,0:T(8,128)}, u32[]{:S(2)}) copy-start(f32[20,256]{1,0:T(8,128)} %get-tuple-element.14.refs_10_) | copy-start | bytes 61444
  42.1 0.7 %copy-start.21 = (f32[20,256]{1,0:T(8,128)S(1)}, f32[20,256]{1,0:T(8,128)}, u32[]{:S(2)}) copy-start(f32[20,256]{1,0:T(8,128)} %get-tuple-element.15.refs_11_) | copy-start | bytes 61444

commit v2 on v1

v2 whole, which is shorter than its diff:
```python
import math

import jax
import jax.numpy as jnp
from jax import lax
from jax.experimental import pallas as pl
from jax.experimental.pallas import tpu as pltpu
from jax.sharding import PartitionSpec as P

F32 = jnp.float32
AXES = ("lon", "lat")
LANES = 128
VMEM_LIMIT = 24 * 2**20
ROW_FIELDS = 7
COL_FIELDS = 5


def swap_pairs(lon_count, lat_count):
    def flat(lon, lat):
        return (lon % lon_count) * lat_count + lat

    rows_near, rows_far, cols_near, cols_far = [], [], [], []
    for lon in range(lon_count):
        for lat in range(lat_count):
            me = flat(lon, lat)
            rows_near.append((me, flat(lon, lat ^ 1)))
            if lat in (0, lat_count - 1):
                rows_far.append((me, flat(lon + lon_count // 2, lat)))
            else:
                rows_far.append((me, flat(lon, lat + 1 if lat % 2 else lat - 1)))
            cols_near.append((me, flat(lon ^ 1, lat)))
            cols_far.append((me, flat(lon + 1 if lon % 2 else lon - 1, lat)))
    return rows_near, rows_far, cols_near, cols_far


def face_cos(first, shape, axis, lat_total):
    position = (first + lax.broadcasted_iota(jnp.int32, shape, axis)).astype(F32)
    angle = position * (math.pi / lat_total) - math.pi / 2
    square = angle * angle
    cosine = jnp.full(shape, 1.0 / math.factorial(16), F32)
    for power in range(14, -1, -2):
        cosine = (-1.0) ** (power // 2) / math.factorial(power) + square * cosine
    return cosine


def metric(cosine):
    return 0.5 * (1.0 + jnp.abs(cosine))


def up_level(x):
    return jnp.concatenate((x[1:], jnp.zeros_like(x[:1])), 0)


def down_level(x):
    return jnp.concatenate((jnp.zeros_like(x[:1]), x[:-1]), 0)


def one_cos(row, lat_total):
    return face_cos(row, (1, 2 * LANES), 0, lat_total)


def rows_kernel(lat_total, rows, *refs):
    low, high, (near_ref, far_ref) = refs[:8], refs[8:16], refs[16:]
    lat = lax.axis_index("lat")
    width = near_ref.shape[-1]
    lane = lax.broadcasted_iota(jnp.int32, (4, width), 1)

    def message(fields, edge, inner, face, sign):
        p, we, wn, forcing, clon, clat, cvert, diag = [f[:, edge, :] for f in fields]
        p_in, wn_in, clat_in = [fields[i][:, inner, :] for i in (0, 2, 5)]
        cosine = one_cos(face, lat_total)
        east = lane < width - 1
        w_east = jnp.where(east, 0.5 * (clon + pltpu.roll(clon, width - 1, 1)), 0.0)
        h_east = jnp.where(
            east,
            w_east * (pltpu.roll(p, width - 1, 1) - p) - 0.5 * (we + pltpu.roll(we, width - 1, 1)),
            0.0,
        )
        w_in = metric(cosine) * (0.5 * (clat + clat_in))
        h_in = w_in * (p_in - p) - sign * (0.5 * cosine * (wn + wn_in))
        w_up = up_level(cvert)
        h_up = w_up * (up_level(p) - p)
        below = cvert * (p - down_level(p))
        total = diag + w_east + pltpu.roll(w_east, 1, 1) + w_in + cvert + w_up
        number = forcing - diag * p + h_east - pltpu.roll(h_east, 1, 1) + h_in + h_up - below
        return jnp.concatenate((p, wn, clat, total, number, clon, we), 0)

    start = lat * rows
    south = message(low, 0, 1, start + 1, 1.0)
    north = message(high, 7, 6, start + rows - 1, -1.0)
    even = lat % 2 == 0
    near_ref[...] = jnp.where(even, north, south)
    far_ref[...] = jnp.where(even, south, north)


def rows_call(lat_total, fields):
    lev, rows, width = fields[0].shape
    low = pl.BlockSpec((lev, 8, width), lambda i: (0, 0, 0))
    high = pl.BlockSpec((lev, 8, width), lambda i: (0, rows // 8 - 1, 0))
    shape = jax.ShapeDtypeStruct((ROW_FIELDS * lev, width), F32)
    pinned = [pltpu.with_memory_space_constraint(f, pltpu.HBM) for f in fields]
    out = pl.BlockSpec((ROW_FIELDS * lev, width), lambda i: (0, 0))
    return pl.pallas_call(
        lambda *refs: rows_kernel(lat_total, rows, *refs),
        grid=(1,),
        in_specs=[low] * 8 + [high] * 8,
        out_specs=[out, out],
        out_shape=[shape, shape],
        compiler_params=pltpu.CompilerParams(vmem_limit_bytes=4 * 2**20),
        name="row_messages",
    )(*pinned, *pinned)


CHUNKS = 5
PAD = 8
BLOCK = 48


def west_of(tiles, lane, edge):
    a, b = [pltpu.roll(x, 1, 1) for x in tiles]
    return jnp.where(lane == 0, edge, a), jnp.where(lane == 0, a, b)


def east_of(tiles, lane, edge):
    a, b = [pltpu.roll(x, LANES - 1, 1) for x in tiles]
    return jnp.where(lane == LANES - 1, b, a), jnp.where(lane == LANES - 1, edge, b)


def tile_copy(hbm, buf, sem, row, count, tile, pad=0):
    return pltpu.make_async_copy(
        hbm.at[:, pl.ds(row, count), pl.ds(tile * LANES, LANES)],
        buf.at[tile, :, pl.ds(pad + row, count), :],
        sem,
    )


def partial_kernel(lat_total, rows, *refs):
    hbm, (delta_hbm, cols_ref) = refs[:8], refs[8:10]
    bufs, delta, pack, cosines, sems, out_sems = refs[10:18], *refs[18:]
    start = lax.axis_index("lat") * rows
    per = rows // CHUNKS

    def copies(chunk):
        return [
            tile_copy(hbm[f], bufs[f], sems.at[chunk, f, t], chunk * per, per, t, PAD)
            for f in range(8)
            for t in range(2)
        ]

    def sends(chunk):
        cut = pl.ds(chunk * per, per)
        return [
            pltpu.make_async_copy(
                delta.at[t, :, cut, :], delta_hbm.at[t, :, cut, :], out_sems.at[chunk, t]
            )
            for t in range(2)
        ]

    def pads(inside, outside):
        for f, sign in ((0, 1.0), (2, -1.0), (5, -1.0)):
            for t in range(2):
                for k in range(4):
                    edge = bufs[f][t, k, inside : inside + 1, :]
                    bufs[f][t, k, outside : outside + 1, :] = sign * edge

    for chunk in range(CHUNKS):
        for c in copies(chunk):
            c.start()
    cosines[...] = face_cos(start, cosines.shape, 0, lat_total)
    pack[pl.ds(rows, 256 - rows), :] = jnp.zeros((256 - rows, LANES), F32)
    shape = (BLOCK, LANES)
    lane = lax.broadcasted_iota(jnp.int32, shape, 1)

    def step(r, carry):
        row = pl.multiple_of(r * BLOCK, BLOCK)
        c_s, c_n = cosines[pl.ds(row, BLOCK), :], cosines[pl.ds(row + 1, BLOCK), :]
        m_s, m_n = metric(c_s), metric(c_n)
        acc = [jnp.zeros(shape, F32) for _ in range(4)]
        for k in range(4):

            def get(f, shift=0, level=k):
                at = pl.ds(row + PAD + shift, BLOCK)
                return [bufs[f][t, level, at, :] for t in range(2)]

            p, we, clon = get(0), get(1), get(4)
            p_w, p_e = west_of(p, lane, p[0]), east_of(p, lane, p[1])
            we_w, we_e = west_of(we, lane, -we[0]), east_of(we, lane, -we[1])
            clon_w, clon_e = west_of(clon, lane, -clon[0]), east_of(clon, lane, -clon[1])
            wn, wn_s, wn_n = get(2), get(2, -1), get(2, 1)
            clat, clat_s, clat_n = get(5), get(5, -1), get(5, 1)
            p_s, p_n = get(0, -1), get(0, 1)
            forcing, below, diag = get(3), get(6), get(7)
            if k < 3:
                above, p_a = get(6, 0, k + 1), get(0, 0, k + 1)
            if k > 0:
                p_b = get(0, 0, k - 1)
            total, number = [], []
            for t in range(2):
                w_e, w_w = clon[t] + clon_e[t], clon[t] + clon_w[t]
                w_n, w_s = m_n * (clat[t] + clat_n[t]), m_s * (clat[t] + clat_s[t])
                flux = w_e * (p_e[t] - p[t]) + w_w * (p_w[t] - p[t]) - (we_e[t] - we_w[t])
                flux += w_n * (p_n[t] - p[t]) + w_s * (p_s[t] - p[t])
                flux += c_s * (wn[t] + wn_s[t]) - c_n * (wn[t] + wn_n[t])
                weight = (w_e + w_w) + (w_n + w_s)
                tt = diag[t] + below[t]
                nn = forcing[t] - diag[t] * p[t]
                nn += below[t] * (p_b[t] - p[t]) if k > 0 else -below[t] * p[t]
                if k < 3:
                    tt += above[t]
                    nn += above[t] * (p_a[t] - p[t])
                tt = tt + 0.5 * weight
                nn = nn + 0.5 * flux
                delta[t, k, pl.ds(row, BLOCK), :] = nn / tt
                total.append(tt)
                number.append(nn)
            for side in range(2):
                for i, f in enumerate((p, we, clon, total, number)):
                    j = (side * COL_FIELDS + i) * 4 + k
                    source = 0 if side == 0 else LANES - 1
                    moved = pltpu.roll(f[side], (j - source) % LANES, 1)
                    acc[k] = jnp.where(lane == j, moved, acc[k])
        pack[pl.ds(row, BLOCK), :] = (acc[0] + acc[1]) + (acc[2] + acc[3])
        return carry

    for c in copies(0):
        c.wait()
    pads(PAD, PAD - 1)
    for chunk in range(CHUNKS):
        if chunk + 1 < CHUNKS:
            for c in copies(chunk + 1):
                c.wait()
        if chunk == CHUNKS - 1:
            pads(PAD + rows - 1, PAD + rows)
        lax.fori_loop(chunk * per // BLOCK, (chunk + 1) * per // BLOCK, step, 0)
        for c in sends(chunk):
            c.start()
    cols_ref[...] = pack[...].T[: 2 * COL_FIELDS * 4]
    for chunk in range(CHUNKS):
        for c in sends(chunk):
            c.wait()


def partial_call(lat_total, fields):
    lev, rows, width = fields[0].shape
    tiles = width // LANES
    plane = jax.ShapeDtypeStruct((tiles, lev, rows, LANES), F32)
    cols = jax.ShapeDtypeStruct((2 * COL_FIELDS * lev, 256), F32)
    hbm, vmem = pl.BlockSpec(memory_space=pl.ANY), pl.BlockSpec(memory_space=pltpu.VMEM)
    return pl.pallas_call(
        lambda *refs: partial_kernel(lat_total, rows, *refs),
        in_specs=[hbm] * 8,
        out_specs=[hbm, vmem],
        out_shape=[plane, cols],
        scratch_shapes=[pltpu.VMEM((tiles, lev, rows + 2 * PAD, LANES), F32)] * 8
        + [
            pltpu.VMEM((tiles, lev, rows, LANES), F32),
            pltpu.VMEM((256, LANES), F32),
            pltpu.VMEM((rows + 8, LANES), F32),
            pltpu.SemaphoreType.DMA((CHUNKS, 8, tiles)),
            pltpu.SemaphoreType.DMA((CHUNKS, tiles)),
        ],
        compiler_params=pltpu.CompilerParams(vmem_limit_bytes=VMEM_LIMIT),
        cost_estimate=pl.CostEstimate(flops=20_000_000, bytes_accessed=10_000_000, transcendentals=0),
        name="partial_sums",
    )(*fields)


def edge_rows(own, halo, cosine, low):
    w = metric(cosine) * (0.5 * (own[8:12] + halo[8:12]))
    g = 0.5 * cosine * (own[4:8] + halo[4:8])
    f = w * (own[0:4] - halo[0:4]) if low else w * (halo[0:4] - own[0:4])
    return w, f, g


def pick(even, near, far):
    return jnp.where(even, far, near), jnp.where(even, near, far)


def columns_kernel(lat_total, rows, cols, near, far, near_in, far_in, near_ref, far_ref):
    lat, lon = lax.axis_index("lat"), lax.axis_index("lon")
    even = lat % 2 == 0
    own_s, own_n = pick(even, near[...], far[...])
    halo_s, halo_n = pick(even, near_in[...], far_in[...])
    w_s, f_s, g_s = edge_rows(own_s, halo_s, one_cos(lat * rows, lat_total), True)
    w_n, f_n, g_n = edge_rows(own_n, halo_n, one_cos((lat + 1) * rows, lat_total), False)
    h_s, h_n = f_s - g_s, f_n - g_n
    width = w_s.shape[-1]
    lane = lax.broadcasted_iota(jnp.int32, (4, width), 1)

    def side(at):
        source = 0 if at == 0 else width - 1
        base = at * COL_FIELDS * 4
        p, we, clon, total, number = [cols[pl.ds(base + i * 4, 4), :] for i in range(COL_FIELDS)]

        def put(x, value, target):
            return jnp.where(lane == target, pltpu.roll(value, (target - source) % width, 1), x)

        no = jnp.zeros_like(p)
        total = total + put(put(no, w_s, 0), w_n, rows - 1)
        number = number + put(put(no, -h_s, 0), h_n, rows - 1)
        p = put(put(p, halo_s[0:4], rows), halo_n[0:4], rows + 1)
        clon = put(put(clon, halo_s[20:24], rows), halo_n[20:24], rows + 1)
        we = put(put(we, halo_s[24:28], rows), halo_n[24:28], rows + 1)
        return jnp.concatenate((p, we, clon, total, number), 0)

    west, east = side(0), side(1)
    lon_even = lon % 2 == 0
    near_ref[...] = jnp.where(lon_even, east, west)
    far_ref[...] = jnp.where(lon_even, west, east)


def columns_call(lat_total, rows, cols, near, far, near_in, far_in):
    shape = jax.ShapeDtypeStruct((cols.shape[0] // 2, cols.shape[1]), F32)
    vmem = pl.BlockSpec(memory_space=pltpu.VMEM)
    return pl.pallas_call(
        lambda *refs: columns_kernel(lat_total, rows, *refs),
        in_specs=[vmem] * 5,
        out_specs=[vmem, vmem],
        out_shape=[shape, shape],
        compiler_params=pltpu.CompilerParams(vmem_limit_bytes=4 * 2**20),
        name="column_messages",
    )(cols, near, far, near_in, far_in)


def final_kernel(lat_total, rows, *refs):
    hbm, (rn, rf, rn_in, rf_in, cn, cf, cn_in, cf_in) = refs[:5], refs[5:13]
    new_hbm, res_hbm = refs[13:15]
    bufs, new_buf, res_buf, colv, cosines, sems, out_sems = refs[15:20], *refs[20:]
    pb, lonb, latb, vertb, delta = bufs
    lat, lon = lax.axis_index("lat"), lax.axis_index("lon")
    per = rows // CHUNKS

    def load(field, tile):
        if field == 4:
            return pltpu.make_async_copy(
                hbm[field].at[tile], delta.at[tile, :, pl.ds(PAD, rows), :], sems.at[field, tile]
            )
        return tile_copy(hbm[field], bufs[field], sems.at[field, tile], 0, rows, tile, PAD)

    def send(chunk, which, tile):
        buf, out = ((new_buf, new_hbm), (res_buf, res_hbm))[which]
        return pltpu.make_async_copy(
            buf.at[tile, :, pl.ds(chunk * per, per), :],
            out.at[:, pl.ds(chunk * per, per), pl.ds(tile * LANES, LANES)],
            out_sems.at[chunk, which, tile],
        )

    order = (4, 0, 1, 2, 3)
    for field in order:
        for tile in range(2):
            load(field, tile).start()

    width = 2 * LANES
    wide = lax.broadcasted_iota(jnp.int32, (4, width), 1)
    even = lat % 2 == 0
    cosines[...] = face_cos(lat * rows, cosines.shape, 0, lat_total)

    def two(x):
        return jnp.concatenate((x, x), 1)

    own_s, own_n = pick(even, rn[...], rf[...])
    halo_s, halo_n = pick(even, rn_in[...], rf_in[...])
    w_s, f_s, g_s = edge_rows(own_s, halo_s, two(cosines[0:1, :]), True)
    w_n, f_n, g_n = edge_rows(own_n, halo_n, two(cosines[rows : rows + 1, :]), False)
    lon_even = lon % 2 == 0
    own_w, own_e = pick(lon_even, cn[...], cf[...])
    halo_w, halo_e = pick(lon_even, cn_in[...], cf_in[...])

    def edge_cols(own, halo, sign):
        w = 0.5 * (own[8:12] + halo[8:12])
        h = sign * w * (own[0:4] - halo[0:4]) - 0.5 * (own[4:8] + halo[4:8])
        d_own = (own[16:20] - sign * h) / (own[12:16] + w)
        d_halo = (halo[16:20] + sign * h) / (halo[12:16] + w)
        inside = wide < rows
        return w, h, jnp.where(inside, d_own, 0.0), jnp.where(inside, w * d_halo, 0.0)

    w_w, h_w, d_w, r_w = edge_cols(own_w, halo_w, 1.0)
    w_e, h_e, d_e, r_e = edge_cols(own_e, halo_e, -1.0)

    def put(x, value, source, target):
        return jnp.where(wide == target, pltpu.roll(value, (target - source) % width, 1), x)

    no = jnp.zeros((4, width), F32)

    def halo_delta(halo, w, f, g, source, low, pole):
        add_w = put(put(no, w_w, source, 0), w_e, source, width - 1)
        add_h = put(put(no, -h_w, source, 0), h_e, source, width - 1)
        turned = jnp.where(pole, -g, g)
        flux = f - turned if low else turned - f
        return (halo[16:20] + add_h + flux) / (halo[12:16] + add_w + w)

    lat_last = lax.axis_size("lat") - 1
    d_s = halo_delta(halo_s, w_s, f_s, g_s, rows, True, lat == 0)
    d_n = halo_delta(halo_n, w_n, f_n, g_n, rows + 1, False, lat == lat_last)
    row_s = (own_s[16:20] - (f_s - g_s)) / (own_s[12:16] + w_s)
    row_n = (own_n[16:20] + (f_n - g_n)) / (own_n[12:16] + w_n)
    stack = jnp.concatenate((d_w, d_e, r_w, r_e, jnp.zeros((LANES - 16, width), F32)), 0)
    colv[...] = stack.T

    def put_rows(buf, at, value):
        for t in range(2):
            for k in range(4):
                buf[t, k, at : at + 1, :] = value[k : k + 1, t * LANES : (t + 1) * LANES]

    for tile in range(2):
        load(4, tile).wait()
    for at, value in ((PAD - 1, d_s), (PAD, row_s), (PAD + rows - 1, row_n), (PAD + rows, d_n)):
        put_rows(delta, at, value)

    shape = (BLOCK, LANES)
    lane = lax.broadcasted_iota(jnp.int32, shape, 1)
    edge = (0, LANES - 1)

    def fix(r, carry):
        row = pl.multiple_of(r * BLOCK, BLOCK)
        packed = colv[pl.ds(row, BLOCK), :]
        for k in range(4):
            for t in range(2):
                column = pltpu.roll(packed, (edge[t] - (t * 4 + k)) % LANES, 1)
                at = pl.ds(row + PAD, BLOCK)
                delta[t, k, at, :] = jnp.where(lane == edge[t], column, delta[t, k, at, :])
        return carry

    lax.fori_loop(0, rows // BLOCK, fix, 0)
    for field in order[1:]:
        for tile in range(2):
            load(field, tile).wait()
    put_rows(latb, PAD - 1, halo_s[8:12])
    put_rows(latb, PAD + rows, halo_n[8:12])

    def step(r, carry):
        row = pl.multiple_of(r * BLOCK, BLOCK)
        packed = colv[pl.ds(row, BLOCK), :]
        m_s, m_n = metric(cosines[pl.ds(row, BLOCK), :]), metric(cosines[pl.ds(row + 1, BLOCK), :])
        for k in range(4):

            def get(f, shift=0, level=k):
                at = pl.ds(row + PAD + shift, BLOCK)
                return [bufs[f][t, level, at, :] for t in range(2)]

            d, d_s, d_n = get(4), get(4, -1), get(4, 1)
            clat, clat_s, clat_n = get(2), get(2, -1), get(2, 1)
            clon, p = get(1), get(0)
            d_w, d_e = west_of(d, lane, d[0]), east_of(d, lane, d[1])
            clon_w, clon_e = west_of(clon, lane, clon[0]), east_of(clon, lane, clon[1])
            for t in range(2):
                column = pltpu.roll(packed, (edge[t] - (8 + t * 4 + k)) % LANES, 1)
                x_w = (clon[t] + clon_w[t]) * d_w[t]
                x_e = (clon[t] + clon_e[t]) * d_e[t]
                if t == 0:
                    x_w = jnp.where(lane == 0, 2.0 * column, x_w)
                else:
                    x_e = jnp.where(lane == LANES - 1, 2.0 * column, x_e)
                y = m_n * (clat[t] + clat_n[t]) * d_n[t] + m_s * (clat[t] + clat_s[t]) * d_s[t]
                out = 0.5 * ((x_w + x_e) + y)
                if k > 0:
                    out += get(3)[t] * get(4, 0, k - 1)[t]
                if k < 3:
                    out += get(3, 0, k + 1)[t] * get(4, 0, k + 1)[t]
                res_buf[t, k, pl.ds(row, BLOCK), :] = out
                new_buf[t, k, pl.ds(row, BLOCK), :] = p[t] + d[t]
        return carry

    for chunk in range(CHUNKS):
        lax.fori_loop(chunk * per // BLOCK, (chunk + 1) * per // BLOCK, step, 0)
        for which in range(2):
            for tile in range(2):
                send(chunk, which, tile).start()
    for chunk in range(CHUNKS):
        for which in range(2):
            for tile in range(2):
                send(chunk, which, tile).wait()


def final_call(lat_total, fields, planes, messages):
    lev, rows, width = fields[0].shape
    tiles = width // LANES
    hbm, vmem = pl.BlockSpec(memory_space=pl.ANY), pl.BlockSpec(memory_space=pltpu.VMEM)
    shape = jax.ShapeDtypeStruct(fields[0].shape, F32)
    return pl.pallas_call(
        lambda *refs: final_kernel(lat_total, rows, *refs),
        in_specs=[hbm] * 5 + [vmem] * 8,
        out_specs=[hbm, hbm],
        out_shape=[shape, shape],
        scratch_shapes=[pltpu.VMEM((tiles, lev, rows + 2 * PAD, LANES), F32)] * 5
        + [pltpu.VMEM((tiles, lev, rows, LANES), F32)] * 2
        + [
            pltpu.VMEM((256, LANES), F32),
            pltpu.VMEM((rows + 8, LANES), F32),
            pltpu.SemaphoreType.DMA((5, tiles)),
            pltpu.SemaphoreType.DMA((CHUNKS, 2, tiles)),
        ],
        compiler_params=pltpu.CompilerParams(vmem_limit_bytes=VMEM_LIMIT),
        name="corrected",
    )(*fields, *planes, *messages)


def per_device(pressure, wind_east, wind_north, forcing, coef_lon, coef_lat, coef_vert, diag_coef):
    fields = (pressure, wind_east, wind_north, forcing, coef_lon, coef_lat, coef_vert, diag_coef)
    rows = pressure.shape[1]
    lat_total = rows * lax.axis_size("lat")
    rows_near, rows_far, cols_near, cols_far = swap_pairs(
        lax.axis_size("lon"), lax.axis_size("lat")
    )
    near, far = rows_call(lat_total, fields)
    far_in = lax.ppermute(far, AXES, rows_far)
    near_in = lax.ppermute(near, AXES, rows_near)
    delta, cols = partial_call(lat_total, fields)
    col_near, col_far = columns_call(lat_total, rows, cols, near, far, near_in, far_in)
    col_far_in = lax.ppermute(col_far, AXES, cols_far)
    col_near_in = lax.ppermute(col_near, AXES, cols_near)
    return final_call(
        lat_total,
        (pressure, coef_lon, coef_lat, coef_vert),
        (delta,),
        (near, far, near_in, far_in, col_near, col_far, col_near_in, col_far_in),
    )


def solution(mesh):
    spec = P(None, "lat", "lon")
    return jax.shard_map(
        per_device, mesh=mesh, in_specs=(spec,) * 8, out_specs=(spec, spec), check_vma=False
    )
```

time: 52.1 us -> 26.8 us (0.51); the launches traced: 51.4 us -> 26.7 us
  local copies, waits for them, and re-layouts: 15.7 us -> 0.03 us
  Pallas kernels: 21.1 us -> 12.1 us
    unnamed x44 -> x16, local copies, waits for them, and re-layouts: 15.7 us -> 0.03 us
    pallas_call x1, Pallas kernels: 8.58 us -> 3.94 us  [final_call(): pl.pallas_call(lambda *refs: final_kernel(lat_total, rows, *refs), in_spe...]
    pallas_call x1, Pallas kernels: 8.99 us -> 6.74 us  [partial_call(): pl.pallas_call(lambda *refs: partial_kernel(lat_total, rows, *refs), in_s...]
    pallas_call x1, Pallas kernels: 1.6 us -> 0.12 us  [columns_call(): pl.pallas_call(lambda *refs: columns_kernel(lat_total, rows, *refs), in_s...]
    pallas_call x1, Pallas kernels: 1.95 us -> 1.32 us  [rows_call(): pl.pallas_call(lambda *refs: rows_kernel(lat_total, rows, *refs), grid=(1...]
  transfers between devices with their start and end apart: 4 -> 4, of which waited for: 1 -> 1; matrix products, arithmetic and copies ran while one was open for 0% -> 0% of each run, Pallas kernels for 17% -> 25%
where the time goes in v2:
time: 26.8 us; the launch traced here: 26.7 us
  Pallas kernels  12.1 us (45%)
  starting transfers between devices  12 us (45%)
  waiting for transfers between devices  1.81 us (7%)
  between operations  0.78 us (3%)
    ppermute x1, starting transfers between devices, per_device(): col_far_in = lax.ppermute(col_far, AXES, cols_far)  6.8 us
    pallas_call x1, Pallas kernels, partial_call(): pl.pallas_call(lambda *refs: partial_kernel(lat_total, rows, *refs), in_s...  6.74 us
    pallas_call x1, Pallas kernels, final_call(): pl.pallas_call(lambda *refs: final_kernel(lat_total, rows, *refs), in_spe...  3.94 us
    ppermute x1, starting transfers between devices, per_device(): far_in = lax.ppermute(far, AXES, rows_far)  3.09 us
    ppermute x1, starting transfers between devices, per_device(): col_near_in = lax.ppermute(col_near, AXES, cols_near)  2 us
    ppermute x1, waiting for transfers between devices, per_device(): col_far_in = lax.ppermute(col_far, AXES, cols_far)  1.8 us
    pallas_call x1, Pallas kernels, rows_call(): pl.pallas_call(lambda *refs: rows_kernel(lat_total, rows, *refs), grid=(1...  1.32 us
  transfers between devices with their start and end apart: 4, of which 1 were waited for; matrix products, arithmetic and copies ran while one was open for 0% of the time, Pallas kernels for 25%

profile of v2, /device:TPU:2, one launch (start us, length us, event | category | flops | bytes accessed | tf_op | source)
XLA Modules:
  0.0 26.7 jit_solution(8070402497985282333)
XLA Ops:
  0.6 0.0 copy-start.3
  0.6 0.0 copy-start.2
  0.7 0.0 copy-start.1
  0.7 0.0 copy-start
  0.7 0.0 copy-start.7
  0.7 0.0 copy-start.6
  0.7 0.0 copy-start.5
  0.7 0.0 copy-start.4
  0.7 1.3 %row_messages.1 = (f32[28,256]{1,0:T(8,128)S(1)}, f32[28,256]{1,0:T(8,128)S(1)}) custom-call(f32[4,240,256]{2,1,0:T(8,128)} %refs_0_.5, f32[4,240,256]{2,1,0:T(8,128)} %refs_9_.1, f32[4,240,256]{2,1,0:T(8,128)} %refs_10_.1, f32[4,240,256]{2,1,0:T(8,128)} %refs_11_.1, f32[4,240,256]{2,1,0:T(8,128)} %refs_1_.5, f32[4,240,256]{2,1,0:T(8,128)} %refs_2_.5, ...), custom_call_target="tpu_custom_call" | custom-call | tf_op jit(solution)/shard_map/row_messages/pallas_call | solution.py:103
  2.0 0.1 collective-permute-start
  2.1 3.1 %collective-permute-start.1 = (f32[28,256]{1,0:T(8,128)S(1)}, f32[28,256]{1,0:T(8,128)S(1)}, u32[]{:S(2)}, u32[]{:S(2)}) collective-permute-start(f32[28,256]{1,0:T(8,128)S(1)} %get-tuple-element.10.refs_2_.refs_6_), channel_id=1, source_target_pairs={{0,128},{1,2},{2,1},{3,4},{4,3},{5,6},{6,5},{7,8},{8,7},{9,10},{10... | collective-permute-start | bytes 86024 | tf_op jit(solution)/shard_map/ppermute | solution.py:506
  5.2 0.0 copy-done.3
  5.2 0.0 copy-done.2
  5.2 0.0 copy-done.1
  5.2 0.0 copy-done
  5.2 0.0 copy-done.7
  5.2 0.0 copy-done.6
  5.3 0.0 copy-done.5
  5.3 0.0 copy-done.4
  5.3 6.7 %partial_sums.1 = (f32[2,4,240,128]{3,2,1,0:T(8,128)S(1)}, f32[40,256]{1,0:T(8,128)S(1)}) custom-call(f32[4,240,256]{2,1,0:T(8,128)S(1)} %copy-done, f32[4,240,256]{2,1,0:T(8,128)S(1)} %copy-done.4, f32[4,240,256]{2,1,0:T(8,128)S(1)} %copy-done.5, f32[4,240,256]{2,1,0:T(8,128)S(1)} %copy-done.6, f32[4,240,256]{2,1,0:T(8,128)S(1)} %copy-done.1, ...), custom_call_target="tpu_custom_call" | custom-call | flops 20000000 | bytes 10000000 | tf_op jit(solution)/shard_map/partial_sums/pallas_call | solution.py:249
  12.0 0.0 collective-permute-done.refs_3_.refs_7_
  12.0 0.0 collective-permute-done.1.refs_4_.refs_8_
  12.0 0.1 column_messages.1
  12.2 2.0 %collective-permute-start.2 = (f32[20,256]{1,0:T(8,128)S(1)}, f32[20,256]{1,0:T(8,128)S(1)}, u32[]{:S(2)}, u32[]{:S(2)}) collective-permute-start(f32[20,256]{1,0:T(8,128)S(1)} %get-tuple-element.12.refs_9_), channel_id=1, source_target_pairs={{0,16},{1,17},{2,18},{3,19},{4,20},{5,21},{6,22},{7,23},{8,24},{9,... | collective-permute-start | bytes 61448 | tf_op jit(solution)/shard_map/ppermute | solution.py:511
  14.2 6.8 %collective-permute-start.3 = (f32[20,256]{1,0:T(8,128)S(1)}, f32[20,256]{1,0:T(8,128)S(1)}, u32[]{:S(2)}, u32[]{:S(2)}) collective-permute-start(f32[20,256]{1,0:T(8,128)S(1)} %get-tuple-element.13.refs_10_), channel_id=1, source_target_pairs={{0,240},{1,241},{2,242},{3,243},{4,244},{5,245},{6,246},{7,247},{8... | collective-permute-start | bytes 61448 | tf_op jit(solution)/shard_map/ppermute | solution.py:510
  21.0 0.0 collective-permute-done.2.refs_11_
  21.0 1.8 %collective-permute-done.3.refs_12_ = f32[20,256]{1,0:T(8,128)S(1)} collective-permute-done((f32[20,256]{1,0:T(8,128)S(1)}, f32[20,256]{1,0:T(8,128)S(1)}, u32[]{:S(2)}, u32[]{:S(2)}) %collective-permute-start.3) | collective-permute-done | bytes 20512 | tf_op jit(solution)/shard_map/ppermute | solution.py:510
  22.8 3.9 %corrected.1 = (f32[4,240,256]{2,1,0:T(8,128)}, f32[4,240,256]{2,1,0:T(8,128)}) custom-call(f32[4,240,256]{2,1,0:T(8,128)S(1)} %copy-done, f32[4,240,256]{2,1,0:T(8,128)S(1)} %copy-done.1, f32[4,240,256]{2,1,0:T(8,128)S(1)} %copy-done.2, f32[4,240,256]{2,1,0:T(8,128)S(1)} %copy-done.3, f32[2,4,240,128]{3,2,1,0:T(8,128)S(1)} %get-tuple-element.8.refs_4_, ...), custom_call_target="tpu_custom_call" | custom-call | tf_op jit(solution)/shard_map/corrected/pallas_call | solution.py:480
Async XLA Ops:
  0.6 4.6 %copy-start.3 = (f32[4,240,256]{2,1,0:T(8,128)S(1)}, f32[4,240,256]{2,1,0:T(8,128)}, u32[]{:S(2)}) copy-start(f32[4,240,256]{2,1,0:T(8,128)} %refs_3_.5) | copy-start | bytes 2949124
  0.6 4.6 %copy-start.2 = (f32[4,240,256]{2,1,0:T(8,128)S(1)}, f32[4,240,256]{2,1,0:T(8,128)}, u32[]{:S(2)}) copy-start(f32[4,240,256]{2,1,0:T(8,128)} %refs_2_.5) | copy-start | bytes 2949124
  0.7 4.6 %copy-start.1 = (f32[4,240,256]{2,1,0:T(8,128)S(1)}, f32[4,240,256]{2,1,0:T(8,128)}, u32[]{:S(2)}) copy-start(f32[4,240,256]{2,1,0:T(8,128)} %refs_1_.5) | copy-start | bytes 2949124
  0.7 4.6 %copy-start = (f32[4,240,256]{2,1,0:T(8,128)S(1)}, f32[4,240,256]{2,1,0:T(8,128)}, u32[]{:S(2)}) copy-start(f32[4,240,256]{2,1,0:T(8,128)} %refs_0_.5) | copy-start | bytes 2949124
  0.7 4.6 %copy-start.7 = (f32[4,240,256]{2,1,0:T(8,128)S(1)}, f32[4,240,256]{2,1,0:T(8,128)}, u32[]{:S(2)}) copy-start(f32[4,240,256]{2,1,0:T(8,128)} %refs_15_.1) | copy-start | bytes 2949124
  0.7 4.6 %copy-start.6 = (f32[4,240,256]{2,1,0:T(8,128)S(1)}, f32[4,240,256]{2,1,0:T(8,128)}, u32[]{:S(2)}) copy-start(f32[4,240,256]{2,1,0:T(8,128)} %refs_11_.1) | copy-start | bytes 2949124
  0.7 4.6 %copy-start.5 = (f32[4,240,256]{2,1,0:T(8,128)S(1)}, f32[4,240,256]{2,1,0:T(8,128)}, u32[]{:S(2)}) copy-start(f32[4,240,256]{2,1,0:T(8,128)} %refs_10_.1) | copy-start | bytes 2949124
  0.7 4.6 %copy-start.4 = (f32[4,240,256]{2,1,0:T(8,128)S(1)}, f32[4,240,256]{2,1,0:T(8,128)}, u32[]{:S(2)}) copy-start(f32[4,240,256]{2,1,0:T(8,128)} %refs_9_.1) | copy-start | bytes 2949124
  2.0 10.0 %collective-permute-start = (f32[28,256]{1,0:T(8,128)S(1)}, f32[28,256]{1,0:T(8,128)S(1)}, u32[]{:S(2)}, u32[]{:S(2)}) collective-permute-start(f32[28,256]{1,0:T(8,128)S(1)} %get-tuple-element.9.refs_1_.refs_5_), channel_id=1, source_target_pairs={{0,1},{1,0},{2,3},{3,2},{4,5},{5,4},{6,7},{7,6},{8,9},{9,8},{10,11... | collective-permute-start | bytes 86024 | tf_op jit(solution)/shard_map/ppermute | solution.py:507
  2.1 9.9 %collective-permute-start.1 = (f32[28,256]{1,0:T(8,128)S(1)}, f32[28,256]{1,0:T(8,128)S(1)}, u32[]{:S(2)}, u32[]{:S(2)}) collective-permute-start(f32[28,256]{1,0:T(8,128)S(1)} %get-tuple-element.10.refs_2_.refs_6_), channel_id=1, source_target_pairs={{0,128},{1,2},{2,1},{3,4},{4,3},{5,6},{6,5},{7,8},{8,7},{9,10},{10... | collective-permute-start | bytes 86024 | tf_op jit(solution)/shard_map/ppermute | solution.py:506
  12.2 8.8 %collective-permute-start.2 = (f32[20,256]{1,0:T(8,128)S(1)}, f32[20,256]{1,0:T(8,128)S(1)}, u32[]{:S(2)}, u32[]{:S(2)}) collective-permute-start(f32[20,256]{1,0:T(8,128)S(1)} %get-tuple-element.12.refs_9_), channel_id=1, source_target_pairs={{0,16},{1,17},{2,18},{3,19},{4,20},{5,21},{6,22},{7,23},{8,24},{9,... | collective-permute-start | bytes 61448 | tf_op jit(solution)/shard_map/ppermute | solution.py:511
  14.2 8.6 %collective-permute-start.3 = (f32[20,256]{1,0:T(8,128)S(1)}, f32[20,256]{1,0:T(8,128)S(1)}, u32[]{:S(2)}, u32[]{:S(2)}) collective-permute-start(f32[20,256]{1,0:T(8,128)S(1)} %get-tuple-element.13.refs_10_), channel_id=1, source_target_pairs={{0,240},{1,241},{2,242},{3,243},{4,244},{5,245},{6,246},{7,247},{8... | collective-permute-start | bytes 61448 | tf_op jit(solution)/shard_map/ppermute | solution.py:510

commit v3 on v2

v3 whole, which is shorter than its diff:
```python
import math

import jax
import jax.numpy as jnp
from jax import lax
from jax.experimental import pallas as pl
from jax.experimental.pallas import tpu as pltpu
from jax.sharding import PartitionSpec as P

F32 = jnp.float32
AXES = ("lon", "lat")
LANES = 128
ROW_FIELDS = 7
COL_FIELDS = 5


def swap_pairs(lon_count, lat_count):
    def flat(lon, lat):
        return (lon % lon_count) * lat_count + lat

    rows_near, rows_far, cols_near, cols_far = [], [], [], []
    for lon in range(lon_count):
        for lat in range(lat_count):
            me = flat(lon, lat)
            rows_near.append((me, flat(lon, lat ^ 1)))
            if lat in (0, lat_count - 1):
                rows_far.append((me, flat(lon + lon_count // 2, lat)))
            else:
                rows_far.append((me, flat(lon, lat + 1 if lat % 2 else lat - 1)))
            cols_near.append((me, flat(lon ^ 1, lat)))
            cols_far.append((me, flat(lon + 1 if lon % 2 else lon - 1, lat)))
    return rows_near, rows_far, cols_near, cols_far


def face_cos(first, shape, axis, lat_total):
    position = (first + lax.broadcasted_iota(jnp.int32, shape, axis)).astype(F32)
    angle = position * (math.pi / lat_total) - math.pi / 2
    square = angle * angle
    cosine = jnp.full(shape, 1.0 / math.factorial(16), F32)
    for power in range(14, -1, -2):
        cosine = (-1.0) ** (power // 2) / math.factorial(power) + square * cosine
    return cosine


def metric(cosine):
    return 0.5 * (1.0 + jnp.abs(cosine))


def up_level(x):
    return jnp.concatenate((x[1:], jnp.zeros_like(x[:1])), 0)


def down_level(x):
    return jnp.concatenate((jnp.zeros_like(x[:1]), x[:-1]), 0)


def one_cos(row, lat_total):
    return face_cos(row, (1, 2 * LANES), 0, lat_total)


def rows_kernel(lat_total, rows, *refs):
    low, high, (near_ref, far_ref) = refs[:8], refs[8:16], refs[16:]
    lat = lax.axis_index("lat")
    width = near_ref.shape[-1]
    lane = lax.broadcasted_iota(jnp.int32, (4, width), 1)

    def message(fields, edge, inner, face, sign):
        p, we, wn, forcing, clon, clat, cvert, diag = [f[:, edge, :] for f in fields]
        p_in, wn_in, clat_in = [fields[i][:, inner, :] for i in (0, 2, 5)]
        cosine = one_cos(face, lat_total)
        east = lane < width - 1
        w_east = jnp.where(east, 0.5 * (clon + pltpu.roll(clon, width - 1, 1)), 0.0)
        h_east = jnp.where(
            east,
            w_east * (pltpu.roll(p, width - 1, 1) - p) - 0.5 * (we + pltpu.roll(we, width - 1, 1)),
            0.0,
        )
        w_in = metric(cosine) * (0.5 * (clat + clat_in))
        h_in = w_in * (p_in - p) - sign * (0.5 * cosine * (wn + wn_in))
        w_up = up_level(cvert)
        h_up = w_up * (up_level(p) - p)
        below = cvert * (p - down_level(p))
        total = diag + w_east + pltpu.roll(w_east, 1, 1) + w_in + cvert + w_up
        number = forcing - diag * p + h_east - pltpu.roll(h_east, 1, 1) + h_in + h_up - below
        return jnp.concatenate((p, wn, clat, total, number, clon, we), 0)

    start = lat * rows
    south = message(low, 0, 1, start + 1, 1.0)
    north = message(high, 7, 6, start + rows - 1, -1.0)
    even = lat % 2 == 0
    near_ref[...] = jnp.where(even, north, south)
    far_ref[...] = jnp.where(even, south, north)


def rows_call(lat_total, fields):
    lev, rows, width = fields[0].shape
    low = pl.BlockSpec((lev, 8, width), lambda i: (0, 0, 0))
    high = pl.BlockSpec((lev, 8, width), lambda i: (0, rows // 8 - 1, 0))
    shape = jax.ShapeDtypeStruct((ROW_FIELDS * lev, width), F32)
    pinned = [pltpu.with_memory_space_constraint(f, pltpu.HBM) for f in fields]
    out = pl.BlockSpec((ROW_FIELDS * lev, width), lambda i: (0, 0))
    return pl.pallas_call(
        lambda *refs: rows_kernel(lat_total, rows, *refs),
        grid=(1,),
        in_specs=[low] * 8 + [high] * 8,
        out_specs=[out, out],
        out_shape=[shape, shape],
        compiler_params=pltpu.CompilerParams(vmem_limit_bytes=SMALL_VMEM),
        name="row_messages",
    )(*pinned, *pinned)


CHUNKS = 5
PAD = 8
BLOCK = 48
SMALL_VMEM = 4 * 2**20
VMEM_LIMIT = 24 * 2**20


def window_mask(lane, index):
    return lane // 4 == index


def window_row(index, offset):
    return 4 * index + offset


def merged(ref, level, row, count, lane):
    at = pl.ds(row, count)
    return jnp.where(lane < LANES // 2, ref[level, at, 0:LANES], ref[level, at, LANES : 2 * LANES])


def window_move(x, index):
    return pltpu.roll(x, (4 * index + 2) % LANES, 1)


def edge_kernel(lat_total, rows, *refs):
    p_ref, we_ref, wn_ref, f_ref, clon_ref, clat_ref, cv_ref, diag_ref = refs[:8]
    cols_ref, pm, wnm, clatm, pack, packed, cosines = refs[8:]
    start = lax.axis_index("lat") * rows
    cosines[...] = face_cos(start, cosines.shape, 0, lat_total)
    shape = (BLOCK, LANES)
    lane = lax.broadcasted_iota(jnp.int32, shape, 1)

    def gather(r, carry):
        row = pl.multiple_of(r * BLOCK, BLOCK)
        for ref, buf in ((p_ref, pm), (wn_ref, wnm), (clat_ref, clatm)):
            for k in range(4):
                buf[k, pl.ds(row + PAD, BLOCK), :] = merged(ref, k, row, BLOCK, lane)
        return carry

    lax.fori_loop(0, rows // BLOCK, gather, 0)
    for buf, sign in ((pm, 1.0), (wnm, -1.0), (clatm, -1.0)):
        for k in range(4):
            for inside, outside in ((PAD, PAD - 1), (PAD + rows - 1, PAD + rows)):
                buf[k, outside : outside + 1, :] = sign * buf[k, inside : inside + 1, :]
    pack[pl.ds(rows, 256 - rows), :] = jnp.zeros((256 - rows, LANES), F32)

    def step(r, carry):
        row = pl.multiple_of(r * BLOCK, BLOCK)
        c_s, c_n = cosines[pl.ds(row, BLOCK), :], cosines[pl.ds(row + 1, BLOCK), :]
        m_s, m_n = metric(c_s), metric(c_n)
        acc = [jnp.zeros(shape, F32) for _ in range(4)]
        for k in range(4):

            def get(buf, shift=0, level=k):
                return buf[level, pl.ds(row + PAD + shift, BLOCK), :]

            def raw(ref, level=k):
                return merged(ref, level, row, BLOCK, lane)

            p, clat, wn = get(pm), get(clatm), get(wnm)
            below, diag = raw(cv_ref), raw(diag_ref)
            w_n, w_s = m_n * (clat + get(clatm, 1)), m_s * (clat + get(clatm, -1))
            flux = w_n * (get(pm, 1) - p) + w_s * (get(pm, -1) - p)
            flux += c_s * (wn + get(wnm, -1)) - c_n * (wn + get(wnm, 1))
            total = diag + below
            number = raw(f_ref) - diag * p
            number += below * (get(pm, 0, k - 1) - p) if k > 0 else -below * p
            if k < 3:
                above = raw(cv_ref, k + 1)
                total += above
                number += above * (get(pm, 0, k + 1) - p)
            total += 0.5 * (w_n + w_s)
            number += 0.5 * flux
            for i, x in enumerate((p, raw(we_ref), raw(clon_ref), total, number)):
                index = i * 4 + k
                acc[k] = jnp.where(window_mask(lane, index), window_move(x, index), acc[k])
        pack[pl.ds(row, BLOCK), :] = (acc[0] + acc[1]) + (acc[2] + acc[3])
        return carry

    lax.fori_loop(0, rows // BLOCK, step, 0)
    packed[...] = pack[...].T

    def column(field, offset):
        return jnp.concatenate(
            [packed[pl.ds(window_row(field * 4 + k, offset), 1), :] for k in range(4)], 0
        )

    for side, (edge, inner, sign) in enumerate(((2, 3, 1.0), (1, 0, -1.0))):
        p, we, clon, total, number = [column(i, edge) for i in range(COL_FIELDS)]
        p_in, we_in, clon_in = [column(i, inner) for i in range(3)]
        w = 0.5 * (clon + clon_in)
        number = number + w * (p_in - p) - sign * (0.5 * (we + we_in))
        for i, x in enumerate((p, we, clon, total + w, number)):
            cols_ref[pl.ds((side * COL_FIELDS + i) * 4, 4), :] = x


def edge_call(lat_total, fields):
    lev, rows, width = fields[0].shape
    cols = jax.ShapeDtypeStruct((2 * COL_FIELDS * lev, 256), F32)
    vmem = pl.BlockSpec(memory_space=pltpu.VMEM)
    return pl.pallas_call(
        lambda *refs: edge_kernel(lat_total, rows, *refs),
        in_specs=[vmem] * 8,
        out_specs=vmem,
        out_shape=cols,
        scratch_shapes=[pltpu.VMEM((lev, rows + 2 * PAD, LANES), F32)] * 3
        + [
            pltpu.VMEM((256, LANES), F32),
            pltpu.VMEM((LANES, 256), F32),
            pltpu.VMEM((rows + 8, LANES), F32),
        ],
        compiler_params=pltpu.CompilerParams(vmem_limit_bytes=VMEM_LIMIT),
        cost_estimate=pl.CostEstimate(flops=10_000_000, bytes_accessed=8_000_000, transcendentals=0),
        name="edge_columns",
    )(*fields)


def edge_rows(own, halo, cosine, low):
    w = metric(cosine) * (0.5 * (own[8:12] + halo[8:12]))
    g = 0.5 * cosine * (own[4:8] + halo[4:8])
    f = w * (own[0:4] - halo[0:4]) if low else w * (halo[0:4] - own[0:4])
    return w, f, g


def pick(even, near, far):
    return jnp.where(even, far, near), jnp.where(even, near, far)


def columns_kernel(lat_total, rows, cols, far, near, far_in, near_in, _, near_ref, far_ref):
    lat, lon = lax.axis_index("lat"), lax.axis_index("lon")
    even = lat % 2 == 0
    own_s, own_n = pick(even, near[...], far[...])
    halo_s, halo_n = pick(even, near_in[...], far_in[...])
    w_s, f_s, g_s = edge_rows(own_s, halo_s, one_cos(lat * rows, lat_total), True)
    w_n, f_n, g_n = edge_rows(own_n, halo_n, one_cos((lat + 1) * rows, lat_total), False)
    h_s, h_n = f_s - g_s, f_n - g_n
    width = w_s.shape[-1]
    lane = lax.broadcasted_iota(jnp.int32, (4, width), 1)

    def side(at):
        source = 0 if at == 0 else width - 1
        base = at * COL_FIELDS * 4
        p, we, clon, total, number = [cols[pl.ds(base + i * 4, 4), :] for i in range(COL_FIELDS)]

        def put(x, value, target):
            return jnp.where(lane == target, pltpu.roll(value, (target - source) % width, 1), x)

        no = jnp.zeros_like(p)
        total = total + put(put(no, w_s, 0), w_n, rows - 1)
        number = number + put(put(no, -h_s, 0), h_n, rows - 1)
        p = put(put(p, halo_s[0:4], rows), halo_n[0:4], rows + 1)
        clon = put(put(clon, halo_s[20:24], rows), halo_n[20:24], rows + 1)
        we = put(put(we, halo_s[24:28], rows), halo_n[24:28], rows + 1)
        return jnp.concatenate((p, we, clon, total, number), 0)

    west, east = side(0), side(1)
    lon_even = lon % 2 == 0
    near_ref[...] = jnp.where(lon_even, east, west)
    far_ref[...] = jnp.where(lon_even, west, east)


def columns_call(lat_total, rows, cols, far, near, far_in, near_in, after):
    shape = jax.ShapeDtypeStruct((cols.shape[0] // 2, cols.shape[1]), F32)
    vmem = pl.BlockSpec(memory_space=pltpu.VMEM)
    return pl.pallas_call(
        lambda *refs: columns_kernel(lat_total, rows, *refs),
        in_specs=[vmem] * 6,
        out_specs=[vmem, vmem],
        out_shape=[shape, shape],
        compiler_params=pltpu.CompilerParams(vmem_limit_bytes=SMALL_VMEM),
        name="column_messages",
    )(cols, far, near, far_in, near_in, after)


def roll_west(tiles, lane):
    a, b = [pltpu.roll(x, 1, 1) for x in tiles]
    return a, jnp.where(lane == 0, a, b)


def roll_east(tiles, lane):
    a, b = [pltpu.roll(x, LANES - 1, 1) for x in tiles]
    return jnp.where(lane == LANES - 1, b, a), b


def halo_rows(lat_total, rows, messages):
    far, near, far_in, near_in = messages
    lat = lax.axis_index("lat")
    even = lat % 2 == 0
    own_s, own_n = pick(even, near, far)
    halo_s, halo_n = pick(even, near_in, far_in)
    w_s, f_s, g_s = edge_rows(own_s, halo_s, one_cos(lat * rows, lat_total), True)
    w_n, f_n, g_n = edge_rows(own_n, halo_n, one_cos((lat + 1) * rows, lat_total), False)
    into_s = f_s - jnp.where(lat == 0, -g_s, g_s)
    into_n = jnp.where(lat == lax.axis_size("lat") - 1, -g_n, g_n) - f_n
    return (halo_s, w_s, into_s), (halo_n, w_n, into_n)


EARLY = 2


def interior_kernel(lat_total, rows, before, *refs):
    early = lax.rem(lax.axis_index("lon"), lax.axis_size("lon") // 2) < EARLY
    state = refs[12:18] if before else refs[19:25]
    scratch = refs[18:] if before else refs[26:]

    @pl.when(early if before else jnp.logical_not(early))
    def _():
        correction(lat_total, rows, refs[:12], state, scratch)

    if not before:
        neighbours(lat_total, rows, refs[6], state, refs[25], scratch[3])


def correction(lat_total, rows, refs, state, scratch):
    p_ref, we_ref, wn_ref, f_ref, clon_ref, clat_ref, cv_ref, diag_ref = refs[:8]
    messages = refs[8:12]
    new_ref, delta, clatb, w_west, w_east, cols_ref = state
    pb, wnb, pack, cosines, sems = scratch
    moves = [
        pltpu.make_async_copy(
            ref.at[:, :, pl.ds(t * LANES, LANES)],
            buf.at[t, :, pl.ds(PAD, rows), :],
            sems.at[i, t],
        )
        for i, (ref, buf) in enumerate(((p_ref, pb), (wn_ref, wnb), (clat_ref, clatb)))
        for t in range(2)
    ]
    for move in moves:
        move.start()
    cosines[...] = face_cos(lax.axis_index("lat") * rows, cosines.shape, 0, lat_total)
    south, north = halo_rows(lat_total, rows, [m[...] for m in messages])
    wide = lax.broadcasted_iota(jnp.int32, (4, 2 * LANES), 1)
    inside = (wide > 0) & (wide < 2 * LANES - 1)

    def put_rows(buf, at, value):
        for t in range(2):
            for k in range(4):
                buf[t, k, at : at + 1, :] = value[k : k + 1, t * LANES : (t + 1) * LANES]

    for at, (halo, w, into) in ((PAD - 1, south), (PAD + rows, north)):
        put_rows(pb, at, halo[0:4])
        put_rows(wnb, at, halo[4:8])
        put_rows(clatb, at, halo[8:12])
        put_rows(delta, at, jnp.where(inside, (halo[16:20] + into) / (halo[12:16] + w), 0.0))
    pack[pl.ds(rows, 256 - rows), :] = jnp.zeros((256 - rows, LANES), F32)
    for move in moves:
        move.wait()

    shape = (BLOCK, LANES)
    lane = lax.broadcasted_iota(jnp.int32, shape, 1)
    edge = (lane == 0, lane == LANES - 1)
    tiles = [pl.ds(t * LANES, LANES) for t in range(2)]

    def first(r, carry):
        row = pl.multiple_of(r * BLOCK, BLOCK)
        c_s, c_n = cosines[pl.ds(row, BLOCK), :], cosines[pl.ds(row + 1, BLOCK), :]
        m_s, m_n = metric(c_s), metric(c_n)
        acc = [jnp.zeros(shape, F32) for _ in range(4)]
        for k in range(4):

            def get(buf, shift=0, level=k):
                return [buf[t, level, pl.ds(row + PAD + shift, BLOCK), :] for t in range(2)]

            def raw(ref, level=k):
                return [ref[level, pl.ds(row, BLOCK), tile] for tile in tiles]

            p, we, clon, clat, wn = get(pb), raw(we_ref), raw(clon_ref), get(clatb), get(wnb)
            p_w, p_e = roll_west(p, lane), roll_east(p, lane)
            we_w, we_e = roll_west(we, lane), roll_east(we, lane)
            clon_w, clon_e = roll_west(clon, lane), roll_east(clon, lane)
            wn_s, wn_n, clat_s, clat_n = get(wnb, -1), get(wnb, 1), get(clatb, -1), get(clatb, 1)
            p_s, p_n = get(pb, -1), get(pb, 1)
            forcing, below, diag = raw(f_ref), raw(cv_ref), raw(diag_ref)
            if k < 3:
                above, p_a = raw(cv_ref, k + 1), get(pb, 0, k + 1)
            if k > 0:
                p_b = get(pb, 0, k - 1)
            for t in range(2):
                w_e, w_w = clon[t] + clon_e[t], clon[t] + clon_w[t]
                w_n, w_s = m_n * (clat[t] + clat_n[t]), m_s * (clat[t] + clat_s[t])
                flux = w_e * (p_e[t] - p[t]) + w_w * (p_w[t] - p[t]) - (we_e[t] - we_w[t])
                flux += w_n * (p_n[t] - p[t]) + w_s * (p_s[t] - p[t])
                flux += c_s * (wn[t] + wn_s[t]) - c_n * (wn[t] + wn_n[t])
                weight = (w_e + w_w) + (w_n + w_s)
                total = diag[t] + below[t]
                number = forcing[t] - diag[t] * p[t]
                number += below[t] * (p_b[t] - p[t]) if k > 0 else -below[t] * p[t]
                if k < 3:
                    total += above[t]
                    number += above[t] * (p_a[t] - p[t])
                d = (number + 0.5 * flux) / (total + 0.5 * weight)
                d = jnp.where(edge[t], 0.0, d)
                at = pl.ds(row, BLOCK)
                delta[t, k, pl.ds(row + PAD, BLOCK), :] = d
                new_ref[t, k, at, :] = p[t] + d
                w_west[t, k, at, :] = jnp.where(edge[0], 0.0, w_w) if t == 0 else w_w
                w_east[t, k, at, :] = jnp.where(edge[1], 0.0, w_e) if t == 1 else w_e
            for i, x in enumerate((clon, clat, below)):
                index = i * 4 + k
                both = jnp.where(lane < LANES // 2, x[0], x[1])
                acc[k] = jnp.where(window_mask(lane, index), window_move(both, index), acc[k])
        pack[pl.ds(row, BLOCK), :] = (acc[0] + acc[1]) + (acc[2] + acc[3])
        return carry

    lax.fori_loop(0, rows // BLOCK, first, 0)
    cols_ref[...] = pack[...].T[:48]


def neighbours(lat_total, rows, cv_ref, state, res_ref, cosines):
    _, delta, clatb, w_west, w_east, _ = state
    cosines[...] = face_cos(lax.axis_index("lat") * rows, cosines.shape, 0, lat_total)
    lane = lax.broadcasted_iota(jnp.int32, (BLOCK, LANES), 1)
    tiles = [pl.ds(t * LANES, LANES) for t in range(2)]

    def second(r, carry):
        row = pl.multiple_of(r * BLOCK, BLOCK)
        at = pl.ds(row, BLOCK)
        m_s, m_n = metric(cosines[at, :]), metric(cosines[pl.ds(row + 1, BLOCK), :])
        for k in range(4):

            def get(buf, shift=0, level=k):
                return [buf[t, level, pl.ds(row + PAD + shift, BLOCK), :] for t in range(2)]

            d, d_s, d_n = get(delta), get(delta, -1), get(delta, 1)
            clat, clat_s, clat_n = get(clatb), get(clatb, -1), get(clatb, 1)
            d_w, d_e = roll_west(d, lane), roll_east(d, lane)
            for t in range(2):
                x_w, x_e = w_west[t, k, at, :] * d_w[t], w_east[t, k, at, :] * d_e[t]
                y = m_n * (clat[t] + clat_n[t]) * d_n[t] + m_s * (clat[t] + clat_s[t]) * d_s[t]
                out = 0.5 * ((x_w + x_e) + y)
                if k > 0:
                    out += cv_ref[k, at, tiles[t]] * get(delta, 0, k - 1)[t]
                if k < 3:
                    out += cv_ref[k + 1, at, tiles[t]] * get(delta, 0, k + 1)[t]
                res_ref[t, k, at, :] = out
        return carry

    lax.fori_loop(0, rows // BLOCK, second, 0)


def interior_call(lat_total, fields, messages, state=(), after=()):
    lev, rows, width = fields[0].shape
    tiles = width // LANES
    vmem = pl.BlockSpec(memory_space=pltpu.VMEM)
    plane = jax.ShapeDtypeStruct((tiles, lev, rows, LANES), F32)
    padded = jax.ShapeDtypeStruct((tiles, lev, rows + 2 * PAD, LANES), F32)
    cols = jax.ShapeDtypeStruct((12 * lev, 256), F32)
    out_shape = [plane, padded, padded, plane, plane, cols]
    before = not state
    if not before:
        out_shape.append(plane)
    operands = (*fields, *messages, *state, *after)
    return pl.pallas_call(
        lambda *refs: interior_kernel(lat_total, rows, before, *refs),
        in_specs=[vmem] * len(operands),
        out_specs=[vmem] * len(out_shape),
        out_shape=out_shape,
        scratch_shapes=[pltpu.VMEM(padded.shape, F32)] * 2
        + [
            pltpu.VMEM((256, LANES), F32),
            pltpu.VMEM((rows + 8, LANES), F32),
            pltpu.SemaphoreType.DMA((3, tiles)),
        ],
        input_output_aliases={12 + i: i for i in range(len(state))},
        compiler_params=pltpu.CompilerParams(vmem_limit_bytes=VMEM_LIMIT),
        cost_estimate=pl.CostEstimate(flops=20_000_000, bytes_accessed=16_000_000, transcendentals=0),
        name="interior_before" if before else "interior_beside",
    )(*operands)


def final_kernel(lat_total, rows, *refs):
    new_in, res_in, cols = refs[:3]
    rf, rn, rf_in, rn_in, cf, cn, cf_in, cn_in = refs[3:11]
    new_hbm, res_hbm = refs[11:13]
    new_buf, res_buf, stack, colv, sems = refs[13:]
    lat, lon = lax.axis_index("lat"), lax.axis_index("lon")
    width = 2 * LANES
    wide = lax.broadcasted_iota(jnp.int32, (4, width), 1)
    south, north = halo_rows(lat_total, rows, (rf[...], rn[...], rf_in[...], rn_in[...]))
    lon_even = lon % 2 == 0
    own_w, own_e = pick(lon_even, cn[...], cf[...])
    halo_w, halo_e = pick(lon_even, cn_in[...], cf_in[...])

    def put(x, value, source, target):
        return jnp.where(wide == target, pltpu.roll(value, (target - source) % width, 1), x)

    def edge_cols(own, halo, sign):
        w = 0.5 * (own[8:12] + halo[8:12])
        h = sign * w * (own[0:4] - halo[0:4]) - 0.5 * (own[4:8] + halo[4:8])
        d_own = (own[16:20] - sign * h) / (own[12:16] + w)
        d_halo = (halo[16:20] + sign * h) / (halo[12:16] + w)
        inside = wide < rows
        return w, h, jnp.where(inside, d_own, 0.0), jnp.where(inside, w * d_halo, 0.0)

    w_w, h_w, d_w, r_w = edge_cols(own_w, halo_w, 1.0)
    w_e, h_e, d_e, r_e = edge_cols(own_e, halo_e, -1.0)
    no = jnp.zeros((4, width), F32)

    def corner(source, halo, w, into):
        add_w = put(put(no, w_w, source, 0), w_e, source, width - 1)
        add_h = put(put(no, -h_w, source, 0), h_e, source, width - 1)
        return w * ((halo[16:20] + add_h + into) / (halo[12:16] + add_w + w))

    corner_s, corner_n = corner(rows, *south), corner(rows + 1, *north)
    m_s = metric(face_cos(lat * rows, (4, width), 1, lat_total))
    m_n = metric(face_cos(lat * rows + 1, (4, width), 1, lat_total))

    def column(field, offset):
        return jnp.concatenate(
            [cols[pl.ds(window_row(field * 4 + k, offset), 1), :] for k in range(4)], 0
        )

    stack[...] = jnp.zeros(stack.shape, F32)
    for edge, inner, source, d, beyond in ((2, 3, 0, d_w, r_w), (1, 0, width - 1, d_e, r_e)):
        clon, clat, below = [column(i, edge) for i in range(3)]
        clat_n, clat_s = pltpu.roll(clat, width - 1, 1), pltpu.roll(clat, 1, 1)
        d_n, d_s = pltpu.roll(d, width - 1, 1), pltpu.roll(d, 1, 1)
        at_edge = 0.5 * (m_n * (clat + clat_n) * d_n + m_s * (clat + clat_s) * d_s)
        at_edge += up_level(below) * up_level(d) + below * down_level(d) + beyond
        at_edge += put(put(no, corner_s, source, 0), corner_n, source, rows - 1)
        at_inner = 0.5 * (clon + column(0, inner)) * d
        for k in range(4):
            stack[pl.ds(window_row(k, edge), 1), :] = at_edge[k : k + 1]
            stack[pl.ds(window_row(k, inner), 1), :] = at_inner[k : k + 1]
            stack[pl.ds(window_row(4 + k, edge), 1), :] = d[k : k + 1]
    colv[...] = stack[...].T

    per = rows // CHUNKS
    lane = lax.broadcasted_iota(jnp.int32, (per, LANES), 1)
    edges = (lane < 2, lane >= LANES - 2)

    def sends(chunk):
        return [
            pltpu.make_async_copy(
                buf.at[t, :, pl.ds(chunk * per, per), :],
                out.at[:, pl.ds(chunk * per, per), pl.ds(t * LANES, LANES)],
                sems.at[chunk, i, t],
            )
            for i, (buf, out) in enumerate(((new_buf, new_hbm), (res_buf, res_hbm)))
            for t in range(2)
        ]

    for chunk in range(CHUNKS):
        at = pl.ds(chunk * per, per)
        packed = colv[at, :]
        for k in range(4):
            to_res = pltpu.roll(packed, (-4 * k - 2) % LANES, 1)
            to_new = pltpu.roll(packed, (-4 * (4 + k) - 2) % LANES, 1)
            for t in range(2):
                res_buf[t, k, at, :] = res_in[t, k, at, :] + jnp.where(edges[t], to_res, 0.0)
                new_buf[t, k, at, :] = new_in[t, k, at, :] + jnp.where(edges[t], to_new, 0.0)
        for copy in sends(chunk):
            copy.start()
    for chunk in range(CHUNKS):
        for copy in sends(chunk):
            copy.wait()


def final_call(lat_total, shape, planes, messages):
    lev, rows, width = shape
    tiles = width // LANES
    hbm, vmem = pl.BlockSpec(memory_space=pl.ANY), pl.BlockSpec(memory_space=pltpu.VMEM)
    out = jax.ShapeDtypeStruct(shape, F32)
    return pl.pallas_call(
        lambda *refs: final_kernel(lat_total, rows, *refs),
        in_specs=[vmem] * 11,
        out_specs=[hbm, hbm],
        out_shape=[out, out],
        scratch_shapes=[pltpu.VMEM((tiles, lev, rows, LANES), F32)] * 2
        + [
            pltpu.VMEM((LANES, 256), F32),
            pltpu.VMEM((256, LANES), F32),
            pltpu.SemaphoreType.DMA((CHUNKS, 2, tiles)),
        ],
        compiler_params=pltpu.CompilerParams(vmem_limit_bytes=VMEM_LIMIT),
        name="edges_and_store",
    )(*planes, *messages)


def per_device(pressure, wind_east, wind_north, forcing, coef_lon, coef_lat, coef_vert, diag_coef):
    fields = (pressure, wind_east, wind_north, forcing, coef_lon, coef_lat, coef_vert, diag_coef)
    rows = pressure.shape[1]
    lat_total = rows * lax.axis_size("lat")
    rows_near, rows_far, cols_near, cols_far = swap_pairs(
        lax.axis_size("lon"), lax.axis_size("lat")
    )
    near, far = rows_call(lat_total, fields)
    far_in = lax.ppermute(far, AXES, rows_far)
    near_in = lax.ppermute(near, AXES, rows_near)
    cols = edge_call(lat_total, fields)
    row_messages = (far, near, far_in, near_in)
    state = interior_call(lat_total, fields, row_messages)
    col_near, col_far = columns_call(lat_total, rows, cols, *row_messages, state[5])
    col_far_in = lax.ppermute(col_far, AXES, cols_far)
    col_near_in = lax.ppermute(col_near, AXES, cols_near)
    state = interior_call(lat_total, fields, row_messages, state, (col_near,))
    planes = (state[0], state[6], state[5])
    col_messages = (col_far, col_near, col_far_in, col_near_in)
    return final_call(lat_total, pressure.shape, planes, row_messages + col_messages)


def solution(mesh):
    spec = P(None, "lat", "lon")
    return jax.shard_map(
        per_device, mesh=mesh, in_specs=(spec,) * 8, out_specs=(spec, spec), check_vma=False
    )
```

time: 26.8 us -> 21 us (0.78)
  starting transfers between devices: 12 us -> 6.8 us
  Pallas kernels: 12.1 us -> 9.32 us
  waiting for transfers between devices: 1.81 us -> 3.99 us
    ppermute x1, starting transfers between devices: 6.8 us -> 4.28 us  [per_device(): col_far_in = lax.ppermute(col_far, AXES, cols_far)]
    pallas_call x1, Pallas kernels: 3.94 us -> 1.83 us  [final_call(): pl.pallas_call(lambda *refs: final_kernel(lat_total, rows, *refs), in_spe...]
    ppermute x1, starting transfers between devices: 2 us -> 0.01 us  [per_device(): col_near_in = lax.ppermute(col_near, AXES, cols_near)]
    ppermute x1, waiting for transfers between devices: 0.01 us -> 1.37 us  [per_device(): far_in = lax.ppermute(far, AXES, rows_far)]
    pallas_call x1 -> x3, Pallas kernels: 6.74 us -> 6.04 us  [the longest x2 4.47 us: interior_call(): pl.pallas_call(lambda *refs: interior_kernel(lat_total, rows, before, *re...]
    ppermute x1, waiting for transfers between devices: 0.01 us -> 0.58 us  [per_device(): col_near_in = lax.ppermute(col_near, AXES, cols_near)]
    ppermute x1, starting transfers between devices: 3.09 us -> 2.51 us  [per_device(): far_in = lax.ppermute(far, AXES, rows_far)]
  transfers between devices with their start and end apart: 4 -> 4, of which waited for: 1 -> 3; matrix products, arithmetic and copies ran while one was open for 0% -> 0% of each run, Pallas kernels for 25% -> 13%
where the time goes in v3:
time: 21 us; the launch traced here: 20.9 us
  Pallas kernels  9.32 us (44%)
  starting transfers between devices  6.8 us (32%)
  waiting for transfers between devices  3.99 us (19%)
  between operations  0.79 us (4%)
    pallas_call x2, Pallas kernels, interior_call(): pl.pallas_call(lambda *refs: interior_kernel(lat_total, rows, before, *re...  4.47 us
    ppermute x1, starting transfers between devices, per_device(): col_far_in = lax.ppermute(col_far, AXES, cols_far)  4.28 us
    ppermute x1, starting transfers between devices, per_device(): far_in = lax.ppermute(far, AXES, rows_far)  2.51 us
    ppermute x1, waiting for transfers between devices, per_device(): col_far_in = lax.ppermute(col_far, AXES, cols_far)  2.04 us
    pallas_call x1, Pallas kernels, final_call(): pl.pallas_call(lambda *refs: final_kernel(lat_total, rows, *refs), in_spe...  1.83 us
    pallas_call x1, Pallas kernels, edge_call(): pl.pallas_call(lambda *refs: edge_kernel(lat_total, rows, *refs), in_spec...  1.57 us
    ppermute x1, waiting for transfers between devices, per_device(): far_in = lax.ppermute(far, AXES, rows_far)  1.37 us
    pallas_call x1, Pallas kernels, rows_call(): pl.pallas_call(lambda *refs: rows_kernel(lat_total, rows, *refs), grid=(1...  1.32 us
  transfers between devices with their start and end apart: 4, of which 3 were waited for; matrix products, arithmetic and copies ran while one was open for 0% of the time, Pallas kernels for 13%

profile of v3, /device:TPU:2, one launch (start us, length us, event | category | flops | bytes accessed | tf_op | source)
XLA Modules:
  0.0 20.9 jit_solution(5031329697211047888)
XLA Ops:
  0.6 0.0 copy-start.2
  0.6 0.0 copy-start.3
  0.7 0.0 copy-start.4
  0.7 0.0 copy-start.5
  0.7 0.0 copy-start.6
  0.7 0.0 copy-start.7
  0.7 0.0 copy-start
  0.7 0.0 copy-start.1
  0.7 1.3 %row_messages.1 = (f32[28,256]{1,0:T(8,128)S(1)}, f32[28,256]{1,0:T(8,128)S(1)}) custom-call(f32[4,240,256]{2,1,0:T(8,128)} %refs_0_.7, f32[4,240,256]{2,1,0:T(8,128)} %refs_1_.7, f32[4,240,256]{2,1,0:T(8,128)} %refs_2_.7, f32[4,240,256]{2,1,0:T(8,128)} %refs_3_.7, f32[4,240,256]{2,1,0:T(8,128)} %refs_4_.7, f32[4,240,256]{2,1,0:T(8,128)} %refs_5_.7, ...), custom_call_target="tpu_custom_call" | custom-call | tf_op jit(solution)/shard_map/row_messages/pallas_call | solution.py:102
  2.0 2.5 %collective-permute-start = (f32[28,256]{1,0:T(8,128)S(1)}, f32[28,256]{1,0:T(8,128)S(1)}, u32[]{:S(2)}, u32[]{:S(2)}) collective-permute-start(f32[28,256]{1,0:T(8,128)S(1)} %get-tuple-element.15.refs_8_.refs_1_.refs_3_), channel_id=1, source_target_pairs={{0,128},{1,2},{2,1},{3,4},{4,3},{5,6},{6,5},{7,8},{8,7},{9,10},{10... | collective-permute-start | bytes 86024 | tf_op jit(solution)/shard_map/ppermute | solution.py:600
  4.5 0.0 collective-permute-start.1
  4.6 0.0 copy-done.2
  4.6 0.0 copy-done.3
  4.6 0.0 copy-done.4
  4.6 0.0 copy-done.5
  4.6 0.0 copy-done.6
  4.6 0.0 copy-done.7
  4.6 0.0 copy-done
  4.6 0.0 copy-done.1
  4.6 1.6 %edge_columns.1.refs_0_ = f32[40,256]{1,0:T(8,128)S(1)} custom-call(f32[4,240,256]{2,1,0:T(8,128)S(1)} %copy-done, f32[4,240,256]{2,1,0:T(8,128)S(1)} %copy-done.1, f32[4,240,256]{2,1,0:T(8,128)S(1)} %copy-done.2, f32[4,240,256]{2,1,0:T(8,128)S(1)} %copy-done.3, f32[4,240,256]{2,1,0:T(8,128)S(1)} %copy-done.4, f32[4,240,256]{2,1,0:T(8,128)S(1)} %copy-done.5, ...), custom_call_target="tpu_custom_call" | custom-call | flops 10000000 | bytes 8000000 | tf_op jit(solution)/shard_map/edge_columns/pallas_call | solution.py:213
  6.2 1.4 %collective-permute-done.refs_10_.refs_3_.refs_5_ = f32[28,256]{1,0:T(8,128)S(1)} collective-permute-done((f32[28,256]{1,0:T(8,128)S(1)}, f32[28,256]{1,0:T(8,128)S(1)}, u32[]{:S(2)}, u32[]{:S(2)}) %collective-permute-start) | collective-permute-done | bytes 28704 | tf_op jit(solution)/shard_map/ppermute | solution.py:600
  7.6 0.0 collective-permute-done.1.refs_11_.refs_4_.refs_6_
  7.6 3.3 %interior_before.1 = (f32[2,4,240,128]{3,2,1,0:T(8,128)S(1)}, f32[2,4,256,128]{3,2,1,0:T(8,128)S(1)}, f32[2,4,256,128]{3,2,1,0:T(8,128)S(1)}, f32[2,4,240,128]{3...) custom-call(f32[4,240,256]{2,1,0:T(8,128)S(1)} %copy-done, f32[4,240,256]{2,1,0:T(8,128)S(1)} %copy-done.1, ...), custom_call_target="tpu_custom_call" | custom-call | flops 20000000 | bytes 16000000 | tf_op jit(solution)/shard_map/interior_before/pallas_call | solution.py:465
  10.9 0.1 column_messages.1
  11.0 4.3 %collective-permute-start.2 = (f32[20,256]{1,0:T(8,128)S(1)}, f32[20,256]{1,0:T(8,128)S(1)}, u32[]{:S(2)}, u32[]{:S(2)}) collective-permute-start(f32[20,256]{1,0:T(8,128)S(1)} %get-tuple-element.27.refs_7_), channel_id=1, source_target_pairs={{0,240},{1,241},{2,242},{3,243},{4,244},{5,245},{6,246},{7,247},{8... | collective-permute-start | bytes 61448 | tf_op jit(solution)/shard_map/ppermute | solution.py:606
  15.3 0.0 collective-permute-start.3
  15.3 1.2 %interior_beside.1 = (f32[2,4,240,128]{3,2,1,0:T(8,128)S(1)}, f32[2,4,256,128]{3,2,1,0:T(8,128)S(1)}, f32[2,4,256,128]{3,2,1,0:T(8,128)S(1)}, f32[2,4,240,128]{3...) custom-call(f32[4,240,256]{2,1,0:T(8,128)S(1)} %copy-done, ...), custom_call_target="tpu_custom_call", output_to_operand_aliasing={{0}: (12, {}), {1}: (13, {}), {2}: (14, {}), {3}: (15, {}),... | custom-call | flops 20000000 | bytes 16000000 | tf_op jit(solution)/shard_map/interior_beside/pallas_call | solution.py:465
  16.5 2.0 %collective-permute-done.2.refs_9_ = f32[20,256]{1,0:T(8,128)S(1)} collective-permute-done((f32[20,256]{1,0:T(8,128)S(1)}, f32[20,256]{1,0:T(8,128)S(1)}, u32[]{:S(2)}, u32[]{:S(2)}) %collective-permute-start.2) | collective-permute-done | bytes 20512 | tf_op jit(solution)/shard_map/ppermute | solution.py:606
  18.5 0.6 %collective-permute-done.3.refs_10_ = f32[20,256]{1,0:T(8,128)S(1)} collective-permute-done((f32[20,256]{1,0:T(8,128)S(1)}, f32[20,256]{1,0:T(8,128)S(1)}, u32[]{:S(2)}, u32[]{:S(2)}) %collective-permute-start.3) | collective-permute-done | bytes 20512 | tf_op jit(solution)/shard_map/ppermute | solution.py:607
  19.1 1.8 %edges_and_store.1 = (f32[4,240,256]{2,1,0:T(8,128)}, f32[4,240,256]{2,1,0:T(8,128)}) custom-call(f32[2,4,240,128]{3,2,1,0:T(8,128)S(1)} %get-tuple-element.24.refs_0_, f32[2,4,240,128]{3,2,1,0:T(8,128)S(1)} %get-tuple-element.25.refs_1_, f32[48,256]{1,0:T(8,128)S(1)} %get-tuple-element.26.refs_2_, f32[28,256]{1,0:T(8,128)S(1)} %get-tuple-element.15.refs_8_.refs_1_.refs_3_, ...), custom_call_target="tpu_custom_call" | custom-call | tf_op jit(solution)/shard_map/edges_and_store/pallas_call | solution.py:576
Async XLA Ops:
  0.6 3.9 %copy-start.2 = (f32[4,240,256]{2,1,0:T(8,128)S(1)}, f32[4,240,256]{2,1,0:T(8,128)}, u32[]{:S(2)}) copy-start(f32[4,240,256]{2,1,0:T(8,128)} %refs_2_.7) | copy-start | bytes 2949124
  0.6 3.9 %copy-start.3 = (f32[4,240,256]{2,1,0:T(8,128)S(1)}, f32[4,240,256]{2,1,0:T(8,128)}, u32[]{:S(2)}) copy-start(f32[4,240,256]{2,1,0:T(8,128)} %refs_3_.7) | copy-start | bytes 2949124
  0.7 3.9 %copy-start.4 = (f32[4,240,256]{2,1,0:T(8,128)S(1)}, f32[4,240,256]{2,1,0:T(8,128)}, u32[]{:S(2)}) copy-start(f32[4,240,256]{2,1,0:T(8,128)} %refs_4_.7) | copy-start | bytes 2949124
  0.7 3.9 %copy-start.5 = (f32[4,240,256]{2,1,0:T(8,128)S(1)}, f32[4,240,256]{2,1,0:T(8,128)}, u32[]{:S(2)}) copy-start(f32[4,240,256]{2,1,0:T(8,128)} %refs_5_.7) | copy-start | bytes 2949124
  0.7 3.9 %copy-start.6 = (f32[4,240,256]{2,1,0:T(8,128)S(1)}, f32[4,240,256]{2,1,0:T(8,128)}, u32[]{:S(2)}) copy-start(f32[4,240,256]{2,1,0:T(8,128)} %refs_6_.7) | copy-start | bytes 2949124
  0.7 3.9 %copy-start.7 = (f32[4,240,256]{2,1,0:T(8,128)S(1)}, f32[4,240,256]{2,1,0:T(8,128)}, u32[]{:S(2)}) copy-start(f32[4,240,256]{2,1,0:T(8,128)} %refs_7_.7) | copy-start | bytes 2949124
  0.7 3.9 %copy-start = (f32[4,240,256]{2,1,0:T(8,128)S(1)}, f32[4,240,256]{2,1,0:T(8,128)}, u32[]{:S(2)}) copy-start(f32[4,240,256]{2,1,0:T(8,128)} %refs_0_.7) | copy-start | bytes 2949124
  0.7 3.9 %copy-start.1 = (f32[4,240,256]{2,1,0:T(8,128)S(1)}, f32[4,240,256]{2,1,0:T(8,128)}, u32[]{:S(2)}) copy-start(f32[4,240,256]{2,1,0:T(8,128)} %refs_1_.7) | copy-start | bytes 2949124
  2.0 5.5 %collective-permute-start = (f32[28,256]{1,0:T(8,128)S(1)}, f32[28,256]{1,0:T(8,128)S(1)}, u32[]{:S(2)}, u32[]{:S(2)}) collective-permute-start(f32[28,256]{1,0:T(8,128)S(1)} %get-tuple-element.15.refs_8_.refs_1_.refs_3_), channel_id=1, source_target_pairs={{0,128},{1,2},{2,1},{3,4},{4,3},{5,6},{6,5},{7,8},{8,7},{9,10},{10... | collective-permute-start | bytes 86024 | tf_op jit(solution)/shard_map/ppermute | solution.py:600
  4.5 3.0 %collective-permute-start.1 = (f32[28,256]{1,0:T(8,128)S(1)}, f32[28,256]{1,0:T(8,128)S(1)}, u32[]{:S(2)}, u32[]{:S(2)}) collective-permute-start(f32[28,256]{1,0:T(8,128)S(1)} %get-tuple-element.16.refs_9_.refs_2_.refs_4_), channel_id=1, source_target_pairs={{0,1},{1,0},{2,3},{3,2},{4,5},{5,4},{6,7},{7,6},{8,9},{9,8},{10,11... | collective-permute-start | bytes 86024 | tf_op jit(solution)/shard_map/ppermute | solution.py:601
  11.0 7.5 %collective-permute-start.2 = (f32[20,256]{1,0:T(8,128)S(1)}, f32[20,256]{1,0:T(8,128)S(1)}, u32[]{:S(2)}, u32[]{:S(2)}) collective-permute-start(f32[20,256]{1,0:T(8,128)S(1)} %get-tuple-element.27.refs_7_), channel_id=1, source_target_pairs={{0,240},{1,241},{2,242},{3,243},{4,244},{5,245},{6,246},{7,247},{8... | collective-permute-start | bytes 61448 | tf_op jit(solution)/shard_map/ppermute | solution.py:606
  15.3 3.8 %collective-permute-start.3 = (f32[20,256]{1,0:T(8,128)S(1)}, f32[20,256]{1,0:T(8,128)S(1)}, u32[]{:S(2)}, u32[]{:S(2)}) collective-permute-start(f32[20,256]{1,0:T(8,128)S(1)} %get-tuple-element.23.refs_18_.refs_8_), channel_id=1, source_target_pairs={{0,16},{1,17},{2,18},{3,19},{4,20},{5,21},{6,22},{7,23},{8,24},{9,... | collective-permute-start | bytes 61448 | tf_op jit(solution)/shard_map/ppermute | solution.py:607

commit v4 on v3

v4 whole, which is shorter than its diff:
```python
import math

import jax
import jax.numpy as jnp
from jax import lax
from jax.experimental import pallas as pl
from jax.experimental.pallas import tpu as pltpu
from jax.sharding import PartitionSpec as P

F32 = jnp.float32
AXES = ("lon", "lat")
LANES = 128
ROW_FIELDS = 7
COL_FIELDS = 5


def exchange_pairs(lon_count, lat_count):
    def flat(lon, lat):
        return (lon % lon_count) * lat_count + lat

    rows_near, rows_far, eastward, westward = [], [], [], []
    for lon in range(lon_count):
        for lat in range(lat_count):
            me = flat(lon, lat)
            rows_near.append((me, flat(lon, lat ^ 1)))
            if lat in (0, lat_count - 1):
                rows_far.append((me, flat(lon + lon_count // 2, lat)))
            else:
                rows_far.append((me, flat(lon, lat + 1 if lat % 2 else lat - 1)))
            eastward.append((me, flat(lon + 1, lat)))
            westward.append((me, flat(lon - 1, lat)))
    return rows_near, rows_far, eastward, westward


def face_cos(first, shape, axis, lat_total):
    position = (first + lax.broadcasted_iota(jnp.int32, shape, axis)).astype(F32)
    angle = position * (math.pi / lat_total) - math.pi / 2
    square = angle * angle
    cosine = jnp.full(shape, 1.0 / math.factorial(16), F32)
    for power in range(14, -1, -2):
        cosine = (-1.0) ** (power // 2) / math.factorial(power) + square * cosine
    return cosine


def metric(cosine):
    return 0.5 * (1.0 + jnp.abs(cosine))


def up_level(x):
    return jnp.concatenate((x[1:], jnp.zeros_like(x[:1])), 0)


def down_level(x):
    return jnp.concatenate((jnp.zeros_like(x[:1]), x[:-1]), 0)


def one_cos(row, lat_total):
    return face_cos(row, (1, 2 * LANES), 0, lat_total)


SMALL_VMEM = 4 * 2**20


def rows_kernel(lat_total, rows, *refs):
    low, high, (near_ref, far_ref) = refs[:8], refs[8:16], refs[16:]
    lat = lax.axis_index("lat")
    width = near_ref.shape[-1]
    lane = lax.broadcasted_iota(jnp.int32, (4, width), 1)

    def message(fields, edge, inner, face, sign):
        p, we, wn, forcing, clon, clat, cvert, diag = [f[:, edge, :] for f in fields]
        p_in, wn_in, clat_in = [fields[i][:, inner, :] for i in (0, 2, 5)]
        cosine = one_cos(face, lat_total)
        east = lane < width - 1
        w_east = jnp.where(east, 0.5 * (clon + pltpu.roll(clon, width - 1, 1)), 0.0)
        h_east = jnp.where(
            east,
            w_east * (pltpu.roll(p, width - 1, 1) - p) - 0.5 * (we + pltpu.roll(we, width - 1, 1)),
            0.0,
        )
        w_in = metric(cosine) * (0.5 * (clat + clat_in))
        h_in = w_in * (p_in - p) - sign * (0.5 * cosine * (wn + wn_in))
        w_up = up_level(cvert)
        h_up = w_up * (up_level(p) - p)
        below = cvert * (p - down_level(p))
        total = diag + w_east + pltpu.roll(w_east, 1, 1) + w_in + cvert + w_up
        number = forcing - diag * p + h_east - pltpu.roll(h_east, 1, 1) + h_in + h_up - below
        return jnp.concatenate((p, wn, clat, total, number, clon, we), 0)

    start = lat * rows
    south = message(low, 0, 1, start + 1, 1.0)
    north = message(high, 7, 6, start + rows - 1, -1.0)
    even = lat % 2 == 0
    near_ref[...] = jnp.where(even, north, south)
    far_ref[...] = jnp.where(even, south, north)


def rows_call(lat_total, fields):
    lev, rows, width = fields[0].shape
    low = pl.BlockSpec((lev, 8, width), lambda i: (0, 0, 0))
    high = pl.BlockSpec((lev, 8, width), lambda i: (0, rows // 8 - 1, 0))
    shape = jax.ShapeDtypeStruct((ROW_FIELDS * lev, width), F32)
    pinned = [pltpu.with_memory_space_constraint(f, pltpu.HBM) for f in fields]
    out = pl.BlockSpec((ROW_FIELDS * lev, width), lambda i: (0, 0))
    return pl.pallas_call(
        lambda *refs: rows_kernel(lat_total, rows, *refs),
        grid=(1,),
        in_specs=[low] * 8 + [high] * 8,
        out_specs=[out, out],
        out_shape=[shape, shape],
        compiler_params=pltpu.CompilerParams(vmem_limit_bytes=SMALL_VMEM),
        name="row_messages",
    )(*pinned, *pinned)


CHUNKS = 5
PAD = 8
BLOCK = 48
VMEM_LIMIT = 24 * 2**20


def window_mask(lane, index):
    return lane // 4 == index


def window_row(index, offset):
    return 4 * index + offset


def merged(ref, level, row, count, lane):
    at = pl.ds(row, count)
    return jnp.where(lane < LANES // 2, ref[level, at, 0:LANES], ref[level, at, LANES : 2 * LANES])


def window_move(x, index):
    return pltpu.roll(x, (4 * index + 2) % LANES, 1)


def edge_kernel(lat_total, rows, *refs):
    p_ref, we_ref, wn_ref, f_ref, clon_ref, clat_ref, cv_ref, diag_ref = refs[:8]
    cols_ref, *planes = refs[8:12]
    pm, wnm, clatm, pack, packed, cosines, sems = refs[12:]
    moves = [
        pltpu.make_async_copy(
            ref.at[:, :, pl.ds(t * LANES, LANES)],
            plane.at[t, :, pl.ds(PAD, rows), :],
            sems.at[i, t],
        )
        for i, (ref, plane) in enumerate(zip((p_ref, wn_ref, clat_ref), planes))
        for t in range(2)
    ]
    for move in moves:
        move.start()
    start = lax.axis_index("lat") * rows
    cosines[...] = face_cos(start, cosines.shape, 0, lat_total)
    shape = (BLOCK, LANES)
    lane = lax.broadcasted_iota(jnp.int32, shape, 1)

    def gather(r, carry):
        row = pl.multiple_of(r * BLOCK, BLOCK)
        for ref, buf in ((p_ref, pm), (wn_ref, wnm), (clat_ref, clatm)):
            for k in range(4):
                buf[k, pl.ds(row + PAD, BLOCK), :] = merged(ref, k, row, BLOCK, lane)
        return carry

    lax.fori_loop(0, rows // BLOCK, gather, 0)
    for buf, sign in ((pm, 1.0), (wnm, -1.0), (clatm, -1.0)):
        for k in range(4):
            for inside, outside in ((PAD, PAD - 1), (PAD + rows - 1, PAD + rows)):
                buf[k, outside : outside + 1, :] = sign * buf[k, inside : inside + 1, :]
    pack[pl.ds(rows, 256 - rows), :] = jnp.zeros((256 - rows, LANES), F32)

    def step(r, carry):
        row = pl.multiple_of(r * BLOCK, BLOCK)
        c_s, c_n = cosines[pl.ds(row, BLOCK), :], cosines[pl.ds(row + 1, BLOCK), :]
        m_s, m_n = metric(c_s), metric(c_n)
        acc = [jnp.zeros(shape, F32) for _ in range(4)]
        for k in range(4):

            def get(buf, shift=0, level=k):
                return buf[level, pl.ds(row + PAD + shift, BLOCK), :]

            def raw(ref, level=k):
                return merged(ref, level, row, BLOCK, lane)

            p, clat, wn = get(pm), get(clatm), get(wnm)
            below, diag = raw(cv_ref) if k == 0 else above, raw(diag_ref)
            w_n, w_s = m_n * (clat + get(clatm, 1)), m_s * (clat + get(clatm, -1))
            flux = w_n * (get(pm, 1) - p) + w_s * (get(pm, -1) - p)
            flux += c_s * (wn + get(wnm, -1)) - c_n * (wn + get(wnm, 1))
            total = diag + below
            number = raw(f_ref) - diag * p - (below * p if k == 0 else lifted)
            if k < 3:
                above = raw(cv_ref, k + 1)
                lifted = above * (get(pm, 0, k + 1) - p)
                total += above
                number += lifted
            total += 0.5 * (w_n + w_s)
            number += 0.5 * flux
            for i, x in enumerate((p, raw(we_ref), raw(clon_ref), total, number)):
                index = i * 4 + k
                acc[k] = jnp.where(window_mask(lane, index), window_move(x, index), acc[k])
        pack[pl.ds(row, BLOCK), :] = (acc[0] + acc[1]) + (acc[2] + acc[3])
        return carry

    lax.fori_loop(0, rows // BLOCK, step, 0)
    packed[...] = pack[...].T

    def column(field, offset):
        return jnp.concatenate(
            [packed[pl.ds(window_row(field * 4 + k, offset), 1), :] for k in range(4)], 0
        )

    for side, (edge, inner, sign) in enumerate(((2, 3, 1.0), (1, 0, -1.0))):
        p, we, clon, total, number = [column(i, edge) for i in range(COL_FIELDS)]
        p_in, we_in, clon_in = [column(i, inner) for i in range(3)]
        w = 0.5 * (clon + clon_in)
        number = number + w * (p_in - p) - sign * (0.5 * (we + we_in))
        for i, x in enumerate((p, we, clon, total + w, number)):
            cols_ref[pl.ds((side * COL_FIELDS + i) * 4, 4), :] = x
    for move in moves:
        move.wait()


def edge_call(lat_total, fields):
    lev, rows, width = fields[0].shape
    cols = jax.ShapeDtypeStruct((2 * COL_FIELDS * lev, 256), F32)
    vmem = pl.BlockSpec(memory_space=pltpu.VMEM)
    return pl.pallas_call(
        lambda *refs: edge_kernel(lat_total, rows, *refs),
        in_specs=[vmem] * 8,
        out_specs=[vmem] * 4,
        out_shape=[cols] + [jax.ShapeDtypeStruct((2, lev, rows + 2 * PAD, LANES), F32)] * 3,
        scratch_shapes=[pltpu.VMEM((lev, rows + 2 * PAD, LANES), F32)] * 3
        + [
            pltpu.VMEM((256, LANES), F32),
            pltpu.VMEM((LANES, 256), F32),
            pltpu.VMEM((rows + 8, LANES), F32),
            pltpu.SemaphoreType.DMA((3, 2)),
        ],
        compiler_params=pltpu.CompilerParams(vmem_limit_bytes=VMEM_LIMIT),
        cost_estimate=pl.CostEstimate(flops=10_000_000, bytes_accessed=8_000_000, transcendentals=0),
        name="edge_columns",
    )(*fields)


def edge_rows(own, halo, cosine, low):
    w = metric(cosine) * (0.5 * (own[8:12] + halo[8:12]))
    g = 0.5 * cosine * (own[4:8] + halo[4:8])
    f = w * (own[0:4] - halo[0:4]) if low else w * (halo[0:4] - own[0:4])
    return w, f, g


def pick(even, near, far):
    return jnp.where(even, far, near), jnp.where(even, near, far)


def columns_kernel(lat_total, rows, cols, near, far, near_in, far_in, _, west_ref, east_ref, sent_ref):
    lat = lax.axis_index("lat")
    even = lat % 2 == 0
    own_s, own_n = pick(even, near[...], far[...])
    halo_s, halo_n = pick(even, near_in[...], far_in[...])
    w_s, f_s, g_s = edge_rows(own_s, halo_s, one_cos(lat * rows, lat_total), True)
    w_n, f_n, g_n = edge_rows(own_n, halo_n, one_cos((lat + 1) * rows, lat_total), False)
    h_s, h_n = f_s - g_s, f_n - g_n
    width = w_s.shape[-1]
    lane = lax.broadcasted_iota(jnp.int32, (4, width), 1)

    def side(at):
        source = 0 if at == 0 else width - 1
        base = at * COL_FIELDS * 4
        p, we, clon, total, number = [cols[pl.ds(base + i * 4, 4), :] for i in range(COL_FIELDS)]

        def put(x, value, target):
            return jnp.where(lane == target, pltpu.roll(value, (target - source) % width, 1), x)

        no = jnp.zeros_like(p)
        total = total + put(put(no, w_s, 0), w_n, rows - 1)
        number = number + put(put(no, -h_s, 0), h_n, rows - 1)
        p = put(put(p, halo_s[0:4], rows), halo_n[0:4], rows + 1)
        clon = put(put(clon, halo_s[20:24], rows), halo_n[20:24], rows + 1)
        we = put(put(we, halo_s[24:28], rows), halo_n[24:28], rows + 1)
        return jnp.concatenate((p, we, clon, total, number), 0)

    west_ref[...] = side(0)
    east = side(1)
    east_ref[...] = east
    sent_ref[...] = east


def columns_call(lat_total, rows, cols, near, far, near_in, far_in, after):
    shape = jax.ShapeDtypeStruct((cols.shape[0] // 2, cols.shape[1]), F32)
    vmem = pl.BlockSpec(memory_space=pltpu.VMEM)
    return pl.pallas_call(
        lambda *refs: columns_kernel(lat_total, rows, *refs),
        in_specs=[vmem] * 6,
        out_specs=[vmem] * 3,
        out_shape=[shape] * 3,
        compiler_params=pltpu.CompilerParams(vmem_limit_bytes=SMALL_VMEM),
        name="column_messages",
    )(cols, near, far, near_in, far_in, after)


def roll_west(tiles, lane):
    a, b = [pltpu.roll(x, 1, 1) for x in tiles]
    return a, jnp.where(lane == 0, a, b)


def roll_east(tiles, lane):
    a, b = [pltpu.roll(x, LANES - 1, 1) for x in tiles]
    return jnp.where(lane == LANES - 1, b, a), b


EDGE_TERMS = 8
STATE = 5
AHEAD = 3
BETWEEN = 3


def place():
    return lax.rem(lax.axis_index("lon"), lax.axis_size("lon") // 2)


def interior_ahead(lat_total, rows, *refs):
    @pl.when(place() == 0)
    def _():
        correction(lat_total, rows, refs[:8], refs[8:11], refs[11:15], refs[15:], 0, AHEAD)


def interior_between(lat_total, rows, *refs):
    fields, messages, planes, refs = refs[:8], refs[8:12], refs[12:14], refs[14 + STATE + 1 :]
    state, (_, terms_ref, res_ref), scratch = refs[:STATE], refs[STATE : STATE + 3], refs[STATE + 3 :]
    first = place() == 0

    @pl.when(place() < 2)
    def _():
        begin, end = jnp.where(first, AHEAD, 0), jnp.where(first, rows // BLOCK, BETWEEN)
        planes_here = (*planes, state[4])
        correction(lat_total, rows, fields, planes_here, state[:4], scratch, begin, end)

    @pl.when(first)
    def _():
        edges(lat_total, rows, fields[4:7], messages, state, terms_ref, scratch)
        residual(lat_total, rows, fields[6], state, res_ref, scratch)


def interior(lat_total, rows, *refs):
    fields, messages, planes, refs = refs[:8], refs[8:12], refs[12:14], refs[14 + STATE + 2 + 1 :]
    state, terms_ref, res_ref, scratch = refs[:STATE], refs[STATE], refs[STATE + 1], refs[STATE + 2 :]

    @pl.when(place() > 0)
    def _():
        begin, planes_here = jnp.where(place() == 1, BETWEEN, 0), (*planes, state[4])
        correction(lat_total, rows, fields, planes_here, state[:4], scratch, begin, rows // BLOCK)
        edges(lat_total, rows, fields[4:7], messages, state, terms_ref, scratch)
        residual(lat_total, rows, fields[6], state, res_ref, scratch)


def quotient(x, y):
    guess = pl.reciprocal(y, approx=True)
    guess = guess * (2.0 - y * guess)
    return x * guess


def correction(lat_total, rows, fields, planes, outs, scratch, begin, end):
    _, we_ref, _, f_ref, clon_ref, _, cv_ref, diag_ref = fields
    pb, wnb, clatb = planes
    new_ref, delta, w_west, w_east = outs
    cosines = scratch[-1]
    cosines[...] = face_cos(lax.axis_index("lat") * rows, cosines.shape, 0, lat_total)
    shape = (BLOCK, LANES)
    lane = lax.broadcasted_iota(jnp.int32, shape, 1)
    edge = (lane == 0, lane == LANES - 1)
    tiles = [pl.ds(t * LANES, LANES) for t in range(2)]

    def first(r, carry):
        row = pl.multiple_of(r * BLOCK, BLOCK)
        c_s, c_n = cosines[pl.ds(row, BLOCK), :], cosines[pl.ds(row + 1, BLOCK), :]
        m_s, m_n = metric(c_s), metric(c_n)
        lifted = None
        for k in range(4):

            def get(buf, shift=0, level=k):
                return [buf[t, level, pl.ds(row + PAD + shift, BLOCK), :] for t in range(2)]

            def raw(ref, level=k):
                return [ref[level, pl.ds(row, BLOCK), tile] for tile in tiles]

            p, we, clon, clat, wn = get(pb), raw(we_ref), raw(clon_ref), get(clatb), get(wnb)
            p_e, we_e, clon_e = [roll_east(x, lane) for x in (p, we, clon)]
            p_w, we_w, clon_w = [roll_west(x, lane) for x in (p, we, clon)]
            wn_s, wn_n, clat_s, clat_n = get(wnb, -1), get(wnb, 1), get(clatb, -1), get(clatb, 1)
            p_s, p_n = get(pb, -1), get(pb, 1)
            forcing, diag = raw(f_ref), raw(diag_ref)
            below = raw(cv_ref) if k == 0 else above
            if k < 3:
                above, p_a = raw(cv_ref, k + 1), get(pb, 0, k + 1)
            fallen, lifted = lifted, []
            for t in range(2):
                w_e, w_w = clon[t] + clon_e[t], clon[t] + clon_w[t]
                w_n, w_s = m_n * (clat[t] + clat_n[t]), m_s * (clat[t] + clat_s[t])
                flux = w_e * (p_e[t] - p[t]) + w_w * (p_w[t] - p[t]) - (we_e[t] - we_w[t])
                flux += w_n * (p_n[t] - p[t]) + w_s * (p_s[t] - p[t])
                flux += c_s * (wn[t] + wn_s[t]) - c_n * (wn[t] + wn_n[t])
                weight = (w_e + w_w) + (w_n + w_s)
                total = diag[t] + below[t]
                number = forcing[t] - diag[t] * p[t] - (below[t] * p[t] if k == 0 else fallen[t])
                if k < 3:
                    lifted.append(above[t] * (p_a[t] - p[t]))
                    total += above[t]
                    number += lifted[t]
                d = quotient(number + 0.5 * flux, total + 0.5 * weight)
                d = jnp.where(edge[t], 0.0, d)
                at = pl.ds(row, BLOCK)
                delta[t, k, pl.ds(row + PAD, BLOCK), :] = d
                new_ref[t, k, at, :] = p[t] + d
                w_west[t, k, at, :] = jnp.where(edge[0], 0.0, w_w) if t == 0 else w_w
                w_east[t, k, at, :] = jnp.where(edge[1], 0.0, w_e) if t == 1 else w_e
        return carry

    lax.fori_loop(begin, end, first, 0)


def edges(lat_total, rows, coefs, messages, state, terms_ref, scratch):
    clon_ref, clat_ref, cv_ref = coefs
    near, far, near_in, far_in = [m[...] for m in messages]
    new_ref, delta, _, _, clatb = state
    pack, packed, _ = scratch
    lat = lax.axis_index("lat")
    width = 2 * LANES
    wide = lax.broadcasted_iota(jnp.int32, (4, width), 1)
    inside = (wide > 0) & (wide < width - 1)
    even = lat % 2 == 0
    own_s, own_n = pick(even, near, far)
    halo_s, halo_n = pick(even, near_in, far_in)
    w_s, f_s, g_s = edge_rows(own_s, halo_s, one_cos(lat * rows, lat_total), True)
    w_n, f_n, g_n = edge_rows(own_n, halo_n, one_cos((lat + 1) * rows, lat_total), False)
    into_s = f_s - jnp.where(lat == 0, -g_s, g_s)
    into_n = jnp.where(lat == lax.axis_size("lat") - 1, -g_n, g_n) - f_n

    def put_rows(buf, at, value):
        for t in range(2):
            for k in range(4):
                buf[t, k, at : at + 1, :] = value[k : k + 1, t * LANES : (t + 1) * LANES]

    corners = []
    for own, halo, w, into, flux, at, beyond in (
        (own_s, halo_s, w_s, into_s, g_s - f_s, 0, -1),
        (own_n, halo_n, w_n, into_n, f_n - g_n, rows - 1, rows),
    ):
        halo_number, halo_total = halo[16:20] + into, halo[12:16] + w
        d_own = jnp.where(inside, (own[16:20] + flux) / (own[12:16] + w), 0.0)
        put_rows(new_ref, at, own[0:4] + d_own)
        put_rows(delta, PAD + at, d_own)
        put_rows(delta, PAD + beyond, jnp.where(inside, halo_number / halo_total, 0.0))
        put_rows(clatb, PAD + beyond, halo[8:12])
        corners.append((w, halo_number, halo_total, at))
    pack[pl.ds(rows, 256 - rows), :] = jnp.zeros((256 - rows, LANES), F32)
    shape = (BLOCK, LANES)
    lane = lax.broadcasted_iota(jnp.int32, shape, 1)
    tiles = [pl.ds(t * LANES, LANES) for t in range(2)]

    def gather(r, carry):
        row = pl.multiple_of(r * BLOCK, BLOCK)
        acc = [jnp.zeros(shape, F32) for _ in range(4)]
        for k in range(4):
            for i, ref in enumerate((clon_ref, clat_ref, cv_ref)):
                index = i * 4 + k
                both = merged(ref, k, row, BLOCK, lane)
                acc[k] = jnp.where(window_mask(lane, index), window_move(both, index), acc[k])
        pack[pl.ds(row, BLOCK), :] = (acc[0] + acc[1]) + (acc[2] + acc[3])
        return carry

    lax.fori_loop(0, rows // BLOCK, gather, 0)
    packed[...] = pack[...].T
    m_s = metric(face_cos(lat * rows, (4, width), 1, lat_total))
    m_n = metric(face_cos(lat * rows + 1, (4, width), 1, lat_total))

    def column(field, offset):
        return jnp.concatenate(
            [packed[pl.ds(window_row(field * 4 + k, offset), 1), :] for k in range(4)], 0
        )

    for side, (edge, inner, source) in enumerate(((2, 3, 0), (1, 0, width - 1))):
        clon, clat, below = [column(i, edge) for i in range(3)]
        ends = [jnp.zeros((4, width), F32), jnp.zeros((4, width), F32), jnp.ones((4, width), F32)]
        for *values, at in corners:
            for i, value in enumerate(values):
                ends[i] = jnp.where(wide == at, pltpu.roll(value, (at - source) % width, 1), ends[i])
        terms = (
            0.5 * m_n * (clat + pltpu.roll(clat, width - 1, 1)),
            0.5 * m_s * (clat + pltpu.roll(clat, 1, 1)),
            0.5 * (clon + column(0, inner)),
            up_level(below),
            below,
            *ends,
        )
        for i, term in enumerate(terms):
            terms_ref[pl.ds((side * EDGE_TERMS + i) * 4, 4), :] = term


def residual(lat_total, rows, cv_ref, state, res_ref, scratch):
    _, delta, w_west, w_east, clatb = state
    cosines = scratch[-1]
    cosines[...] = face_cos(lax.axis_index("lat") * rows, cosines.shape, 0, lat_total)
    lane = lax.broadcasted_iota(jnp.int32, (BLOCK, LANES), 1)
    tiles = [pl.ds(t * LANES, LANES) for t in range(2)]

    def second(r, carry):
        row = pl.multiple_of(r * BLOCK, BLOCK)
        at = pl.ds(row, BLOCK)
        m_s, m_n = metric(cosines[at, :]), metric(cosines[pl.ds(row + 1, BLOCK), :])
        for k in range(4):

            def get(buf, shift=0, level=k):
                return [buf[t, level, pl.ds(row + PAD + shift, BLOCK), :] for t in range(2)]

            d, d_s, d_n = get(delta), get(delta, -1), get(delta, 1)
            clat, clat_s, clat_n = get(clatb), get(clatb, -1), get(clatb, 1)
            d_w, d_e = roll_west(d, lane), roll_east(d, lane)
            for t in range(2):
                x_w, x_e = w_west[t, k, at, :] * d_w[t], w_east[t, k, at, :] * d_e[t]
                y = m_n * (clat[t] + clat_n[t]) * d_n[t] + m_s * (clat[t] + clat_s[t]) * d_s[t]
                out = 0.5 * ((x_w + x_e) + y)
                if k > 0:
                    out += cv_ref[k, at, tiles[t]] * get(delta, 0, k - 1)[t]
                if k < 3:
                    out += cv_ref[k + 1, at, tiles[t]] * get(delta, 0, k + 1)[t]
                res_ref[t, k, at, :] = out
        return carry

    lax.fori_loop(0, rows // BLOCK, second, 0)


def interior_call(lat_total, shape, kernel, inputs, kept, after, results):
    lev, rows, width = shape
    tiles = width // LANES
    vmem = pl.BlockSpec(memory_space=pltpu.VMEM)
    shapes = {
        "plane": (tiles, lev, rows, LANES),
        "padded": (tiles, lev, rows + 2 * PAD, LANES),
        "message": (COL_FIELDS * lev, 256),
        "terms": (2 * EDGE_TERMS * lev, 256),
    }
    operands = (*inputs, *kept, *after)
    return pl.pallas_call(
        lambda *refs: kernel(lat_total, rows, *refs),
        in_specs=[vmem] * len(operands),
        out_specs=[vmem] * len(results),
        out_shape=[jax.ShapeDtypeStruct(shapes[name], F32) for name in results],
        scratch_shapes=[
            pltpu.VMEM((256, LANES), F32),
            pltpu.VMEM((LANES, 256), F32),
            pltpu.VMEM((rows + 8, LANES), F32),
        ],
        input_output_aliases={len(inputs) + i: i for i in range(len(kept))},
        compiler_params=pltpu.CompilerParams(vmem_limit_bytes=VMEM_LIMIT),
        cost_estimate=pl.CostEstimate(flops=20_000_000, bytes_accessed=16_000_000, transcendentals=0),
        name=kernel.__name__,
    )(*operands)


def final_kernel(rows, *refs):
    new_in, res_in, terms, own_w, own_e, halo_w, halo_e = refs[:7]
    new_hbm, res_hbm, new_buf, res_buf, stack, colv, sems = refs[7:]
    width = 2 * LANES
    wide = lax.broadcasted_iota(jnp.int32, (4, width), 1)
    low, high, inside = wide == 0, wide == rows - 1, wide < rows
    own, halo = (own_w, own_e), (halo_w, halo_e)

    def ends(x):
        south, north = pltpu.roll(x, width - rows, 1), pltpu.roll(x, width - 2, 1)
        return jnp.where(low, south, jnp.where(high, north, 0.0))

    for side, (edge, inner, sign) in enumerate(((2, 3, 1.0), (1, 0, -1.0))):
        o_p, o_we, o_clon, o_total, o_number = [own[side][pl.ds(4 * i, 4), :] for i in range(5)]
        h_p, h_we, h_clon, h_total, h_number = [halo[side][pl.ds(4 * i, 4), :] for i in range(5)]
        a_n, a_s, w_in, above, below, c_w, c_number, c_total = [
            terms[pl.ds((side * EDGE_TERMS + i) * 4, 4), :] for i in range(EDGE_TERMS)
        ]
        w = 0.5 * (o_clon + h_clon)
        h = w * (o_p - h_p) - sign * (0.5 * (o_we + h_we))
        d = jnp.where(inside, (o_number - h) / (o_total + w), 0.0)
        beyond = jnp.where(inside, w * ((h_number + h) / (h_total + w)), 0.0)
        corner = c_w * ((c_number - ends(h)) / (c_total + ends(w)))
        at_edge = a_n * pltpu.roll(d, width - 1, 1) + a_s * pltpu.roll(d, 1, 1)
        at_edge += above * up_level(d) + below * down_level(d) + (beyond + corner)
        for first, x in ((edge, at_edge), (inner, w_in * d), (16 + edge, d)):
            for t in range(2):
                stack[t, pl.ds(first, 4, stride=4), :] = x[:, t * LANES : (t + 1) * LANES]
    for t in range(2):
        colv[pl.ds(t * LANES, LANES), :] = stack[t].T

    per = rows // CHUNKS
    lane = lax.broadcasted_iota(jnp.int32, (per, LANES), 1)
    edges = (lane < 2, lane >= LANES - 2)
    edge = (lane == 0, lane == LANES - 1)

    def sends(chunk):
        return [
            pltpu.make_async_copy(
                buf.at[t, :, pl.ds(chunk * per, per), :],
                out.at[:, pl.ds(chunk * per, per), pl.ds(t * LANES, LANES)],
                sems.at[chunk, i, t],
            )
            for i, (buf, out) in enumerate(((new_buf, new_hbm), (res_buf, res_hbm)))
            for t in range(2)
        ]

    for chunk in range(CHUNKS):
        at = pl.ds(chunk * per, per)
        packed = colv[at, :]
        for k in range(4):
            to_res = pltpu.roll(packed, (-4 * k - 2) % LANES, 1)
            to_new = pltpu.roll(packed, (-4 * (4 + k) - 2) % LANES, 1)
            for t in range(2):
                res_buf[t, k, at, :] = res_in[t, k, at, :] + jnp.where(edges[t], to_res, 0.0)
                new_buf[t, k, at, :] = new_in[t, k, at, :] + jnp.where(edge[t], to_new, 0.0)
        for copy in sends(chunk):
            copy.start()
    for chunk in range(CHUNKS):
        for copy in sends(chunk):
            copy.wait()


def final_call(shape, planes, messages):
    lev, rows, width = shape
    tiles = width // LANES
    hbm, vmem = pl.BlockSpec(memory_space=pl.ANY), pl.BlockSpec(memory_space=pltpu.VMEM)
    out = jax.ShapeDtypeStruct(shape, F32)
    return pl.pallas_call(
        lambda *refs: final_kernel(rows, *refs),
        in_specs=[vmem] * 7,
        out_specs=[hbm, hbm],
        out_shape=[out, out],
        scratch_shapes=[pltpu.VMEM((tiles, lev, rows, LANES), F32)] * 2
        + [
            pltpu.VMEM((2, LANES, LANES), F32),
            pltpu.VMEM((256, LANES), F32),
            pltpu.SemaphoreType.DMA((CHUNKS, 2, tiles)),
        ],
        compiler_params=pltpu.CompilerParams(vmem_limit_bytes=VMEM_LIMIT),
        name="edges_and_store",
    )(*planes, *messages)


def per_device(pressure, wind_east, wind_north, forcing, coef_lon, coef_lat, coef_vert, diag_coef):
    fields = (pressure, wind_east, wind_north, forcing, coef_lon, coef_lat, coef_vert, diag_coef)
    rows = pressure.shape[1]
    lat_total = rows * lax.axis_size("lat")
    rows_near, rows_far, eastward, westward = exchange_pairs(
        lax.axis_size("lon"), lax.axis_size("lat")
    )
    near, far = rows_call(lat_total, fields)
    far_in = lax.ppermute(far, AXES, rows_far)
    near_in = lax.ppermute(near, AXES, rows_near)
    cols, p_planes, wn_planes, clat_planes = edge_call(lat_total, fields)
    row_messages = (near, far, near_in, far_in)
    shape = pressure.shape
    planes = (p_planes, wn_planes, clat_planes)
    kinds = ("plane", "padded", "plane", "plane", "padded")
    state = interior_call(
        lat_total, shape, interior_ahead, (*fields, *planes), (), (), kinds[:-1]
    )
    west, east, sent = columns_call(lat_total, rows, cols, *row_messages, state[0])
    from_west = lax.ppermute(sent, AXES, eastward)
    *state, west, terms, residual_part = interior_call(
        lat_total,
        shape,
        interior_between,
        (*fields, *row_messages, *planes[:2]),
        (*state, clat_planes, west),
        (),
        (*kinds, "message", "terms", "plane"),
    )
    from_east = lax.ppermute(west, AXES, westward)
    new_pressure, *_, terms, residual_part = interior_call(
        lat_total,
        shape,
        interior,
        (*fields, *row_messages, *planes[:2]),
        (*state, terms, residual_part),
        (west,),
        (*kinds, "terms", "plane"),
    )
    col_messages = (west, east, from_west, from_east)
    return final_call(shape, (new_pressure, residual_part, terms), col_messages)


def solution(mesh):
    spec = P(None, "lat", "lon")
    return jax.shard_map(
        per_device, mesh=mesh, in_specs=(spec,) * 8, out_specs=(spec, spec), check_vma=False
    )
```

time: 21 us -> 19.5 us (0.929)
  the two profiles are of different devices: /device:TPU:2 before, /device:TPU:25 now
where the time goes in v4:
time: 19.5 us; the launch traced here: 19.4 us
  Pallas kernels  10.1 us (52%)
  starting transfers between devices  6.55 us (34%)
  waiting for transfers between devices  1.49 us (8%)
  between operations  0.77 us (4%)
  local copies, waits for them, and re-layouts  0.49 us (3%)
    pallas_call x3, Pallas kernels, interior_call(): pl.pallas_call(lambda *refs: kernel(lat_total, rows, *refs), in_specs=[vm...  5.14 us
    ppermute x1, starting transfers between devices, per_device(): from_east = lax.ppermute(west, AXES, westward)  3.22 us
    pallas_call x1, Pallas kernels, edge_call(): pl.pallas_call(lambda *refs: edge_kernel(lat_total, rows, *refs), in_spec...  1.83 us
    pallas_call x1, Pallas kernels, final_call(): pl.pallas_call(lambda *refs: final_kernel(rows, *refs), in_specs=[vmem] *...  1.73 us
    ppermute x1, starting transfers between devices, per_device(): from_west = lax.ppermute(sent, AXES, eastward)  1.71 us
    pallas_call x1, Pallas kernels, rows_call(): pl.pallas_call(lambda *refs: rows_kernel(lat_total, rows, *refs), grid=(1...  1.32 us
    ppermute x1, waiting for transfers between devices, per_device(): from_west = lax.ppermute(sent, AXES, eastward)  1.09 us
    ppermute x1, starting transfers between devices, per_device(): far_in = lax.ppermute(far, AXES, rows_far)  0.85 us
  transfers between devices with their start and end apart: 4, of which 2 were waited for; matrix products, arithmetic and copies ran while one was open for 0% of the time, Pallas kernels for 36%

profile of v4, /device:TPU:25, one launch (start us, length us, event | category | flops | bytes accessed | tf_op | source)
XLA Modules:
  0.0 19.4 jit_solution(6817830609190370560)
XLA Ops:
  0.6 0.0 copy-start.7
  0.6 0.0 copy-start.6
  0.7 0.0 copy-start.5
  0.7 0.0 copy-start.4
  0.7 0.0 copy-start.3
  0.7 0.0 copy-start.2
  0.7 0.0 copy-start.1
  0.7 0.0 copy-start
  0.7 1.3 %row_messages.1 = (f32[28,256]{1,0:T(8,128)S(1)}, f32[28,256]{1,0:T(8,128)S(1)}) custom-call(f32[4,240,256]{2,1,0:T(8,128)} %refs_0_.9, f32[4,240,256]{2,1,0:T(8,128)} %refs_1_.9, f32[4,240,256]{2,1,0:T(8,128)} %refs_2_.9, f32[4,240,256]{2,1,0:T(8,128)} %refs_3_.9, f32[4,240,256]{2,1,0:T(8,128)} %refs_4_.9, f32[4,240,256]{2,1,0:T(8,128)} %refs_5_.9, ...), custom_call_target="tpu_custom_call" | custom-call | tf_op jit(solution)/shard_map/row_messages/pallas_call | solution.py:105
  2.0 0.8 %collective-permute-start = (f32[28,256]{1,0:T(8,128)S(1)}, f32[28,256]{1,0:T(8,128)S(1)}, u32[]{:S(2)}, u32[]{:S(2)}) collective-permute-start(f32[28,256]{1,0:T(8,128)S(1)} %get-tuple-element.26.refs_1_.refs_8_), channel_id=1, source_target_pairs={{0,1},{1,0},{2,3},{3,2},{4,5},{5,4},{6,7},{7,6},{8,9},{9,8},{10,11... | collective-permute-start | bytes 86024 | tf_op jit(solution)/shard_map/ppermute | solution.py:656
  2.8 0.9 %collective-permute-start.1 = (f32[28,256]{1,0:T(8,128)S(1)}, f32[28,256]{1,0:T(8,128)S(1)}, u32[]{:S(2)}, u32[]{:S(2)}) collective-permute-start(f32[28,256]{1,0:T(8,128)S(1)} %get-tuple-element.27.refs_2_.refs_9_), channel_id=1, source_target_pairs={{0,128},{1,2},{2,1},{3,4},{4,3},{5,6},{6,5},{7,8},{8,7},{9,10},{10... | collective-permute-start | bytes 86024 | tf_op jit(solution)/shard_map/ppermute | solution.py:655
  3.7 0.0 copy-done.7
  3.7 0.0 copy-done.6
  3.7 0.0 copy-done.5
  3.7 0.0 copy-done.4
  3.7 0.0 copy-done.3
  3.7 0.0 copy-done.2
  3.7 0.2 copy-done.1
  3.9 0.3 %copy-done = f32[4,240,256]{2,1,0:T(8,128)S(1)} copy-done((f32[4,240,256]{2,1,0:T(8,128)S(1)}, f32[4,240,256]{2,1,0:T(8,128)}, u32[]{:S(2)}) %copy-start) | copy-done | bytes 983064
  4.2 1.8 %edge_columns.1 = (f32[40,256]{1,0:T(8,128)S(1)}, f32[2,4,256,128]{3,2,1,0:T(8,128)S(1)}, f32[2,4,256,128]{3,2,1,0:T(8,128)S(1)}, f32[2,4,256,128]{3,2,1,0:T(8,128)S(1)}) custom-call(f32[4,240,256]{2,1,0:T(8,128)S(1)} %copy-done, f32[4,240,256]{2,1,0:T(8,128)S(1)} %copy-done.1, f32[4,240,256]{2,1,0:T(8,128)S(1)} %copy-done.2, f32[4,240,256]{2,1,0:T(8,128)S(1)} %copy-done.3, ...), custom_call_target="tpu_custom_call" | custom-call | flops 10000000 | bytes 8000000 | tf_op jit(solution)/shard_map/edge_columns/pallas_call | solution.py:229
  6.0 1.8 %interior_ahead.1 = (f32[2,4,240,128]{3,2,1,0:T(8,128)S(1)}, f32[2,4,256,128]{3,2,1,0:T(8,128)S(1)}, f32[2,4,240,128]{3,2,1,0:T(8,128)S(1)}, f32[2,4,240,128]{3,2,1,0:T(8,128)S(1)}) custom-call(f32[4,240,256]{2,1,0:T(8,128)S(1)} %copy-done, f32[4,240,256]{2,1,0:T(8,128)S(1)} %copy-done.1, f32[4,240,256]{2,1,0:T(8,128)S(1)} %copy-done.2, ...), custom_call_target="tpu_custom_call" | custom-call | flops 20000000 | bytes 16000000 | tf_op jit(solution)/shard_map/interior_ahead/pallas_call | solution.py:546
  7.8 0.0 collective-permute-done.refs_3_.refs_10_
  7.8 0.4 %collective-permute-done.1.refs_4_.refs_11_ = f32[28,256]{1,0:T(8,128)S(1)} collective-permute-done((f32[28,256]{1,0:T(8,128)S(1)}, f32[28,256]{1,0:T(8,128)S(1)}, u32[]{:S(2)}, u32[]{:S(2)}) %collective-permute-start.1) | collective-permute-done | bytes 28704 | tf_op jit(solution)/shard_map/ppermute | solution.py:655
  8.3 0.1 column_messages.1
  8.4 1.7 %collective-permute-start.2 = (f32[20,256]{1,0:T(8,128)S(1)}, f32[20,256]{1,0:T(8,128)S(1)}, u32[]{:S(2)}, u32[]{:S(2)}) collective-permute-start(f32[20,256]{1,0:T(8,128)S(1)} %get-tuple-element.49), channel_id=1, source_target_pairs={{0,16},{1,17},{2,18},{3,19},{4,20},{5,21},{6,22},{7,23},{8,24},{9,... | collective-permute-start | bytes 61448 | tf_op jit(solution)/shard_map/ppermute | solution.py:666
  10.1 3.3 %interior_between.1 = (f32[2,4,240,128]{3,2,1,0:T(8,128)S(1)}, f32[2,4,256,128]{3,2,1,0:T(8,128)S(1)}, f32[2,4,240,128]{3,2,1,0:T(8,128)S(1)}, f32[2,4,240,128]{...) custom-call(f32[4,240,256]{2,1,0:T(8,128)S(1)} %copy-done, ...), custom_call_target="tpu_custom_call", output_to_operand_aliasing={{0}: (14, {}), {1}: (15, {}), {2}: (16, {}), {3}: (17, {}),... | custom-call | flops 20000000 | bytes 16000000 | tf_op jit(solution)/shard_map/interior_between/pallas_call | solution.py:546
  13.4 3.2 %collective-permute-start.3 = (f32[20,256]{1,0:T(8,128)S(1)}, f32[20,256]{1,0:T(8,128)S(1)}, u32[]{:S(2)}, u32[]{:S(2)}) collective-permute-start(f32[20,256]{1,0:T(8,128)S(1)} %get-tuple-element.44.refs_21_.refs_3_), channel_id=1, source_target_pairs={{0,240},{1,241},{2,242},{3,243},{4,244},{5,245},{6,246},{7,247},{8... | collective-permute-start | bytes 61448 | tf_op jit(solution)/shard_map/ppermute | solution.py:676
  16.6 1.1 %collective-permute-done.2.refs_5_ = f32[20,256]{1,0:T(8,128)S(1)} collective-permute-done((f32[20,256]{1,0:T(8,128)S(1)}, f32[20,256]{1,0:T(8,128)S(1)}, u32[]{:S(2)}, u32[]{:S(2)}) %collective-permute-start.2) | collective-permute-done | bytes 20512 | tf_op jit(solution)/shard_map/ppermute | solution.py:666
  17.7 0.0 collective-permute-done.3.refs_6_
  17.7 1.7 %edges_and_store.1 = (f32[4,240,256]{2,1,0:T(8,128)}, f32[4,240,256]{2,1,0:T(8,128)}) custom-call(f32[2,4,240,128]{3,2,1,0:T(8,128)S(1)} %get-tuple-element.45.refs_0_, f32[2,4,240,128]{3,2,1,0:T(8,128)S(1)} %get-tuple-element.46.refs_1_, f32[64,256]{1,0:T(8,128)S(1)} %get-tuple-element.47.refs_2_, f32[20,256]{1,0:T(8,128)S(1)} %get-tuple-element.44.refs_21_.refs_3_, ...), custom_call_target="tpu_custom_call" | custom-call | tf_op jit(solution)/shard_map/edges_and_store/pallas_call | solution.py:631
  (1 shorter events, 0.0 us)
Async XLA Ops:
  0.6 3.0 %copy-start.7 = (f32[4,240,256]{2,1,0:T(8,128)S(1)}, f32[4,240,256]{2,1,0:T(8,128)}, u32[]{:S(2)}) copy-start(f32[4,240,256]{2,1,0:T(8,128)} %refs_7_.9) | copy-start | bytes 2949124
  0.6 3.0 %copy-start.6 = (f32[4,240,256]{2,1,0:T(8,128)S(1)}, f32[4,240,256]{2,1,0:T(8,128)}, u32[]{:S(2)}) copy-start(f32[4,240,256]{2,1,0:T(8,128)} %refs_6_.9) | copy-start | bytes 2949124
  0.7 3.0 %copy-start.5 = (f32[4,240,256]{2,1,0:T(8,128)S(1)}, f32[4,240,256]{2,1,0:T(8,128)}, u32[]{:S(2)}) copy-start(f32[4,240,256]{2,1,0:T(8,128)} %refs_5_.9) | copy-start | bytes 2949124
  0.7 3.0 %copy-start.4 = (f32[4,240,256]{2,1,0:T(8,128)S(1)}, f32[4,240,256]{2,1,0:T(8,128)}, u32[]{:S(2)}) copy-start(f32[4,240,256]{2,1,0:T(8,128)} %refs_4_.9) | copy-start | bytes 2949124
  0.7 3.0 %copy-start.3 = (f32[4,240,256]{2,1,0:T(8,128)S(1)}, f32[4,240,256]{2,1,0:T(8,128)}, u32[]{:S(2)}) copy-start(f32[4,240,256]{2,1,0:T(8,128)} %refs_3_.9) | copy-start | bytes 2949124
  0.7 3.0 %copy-start.2 = (f32[4,240,256]{2,1,0:T(8,128)S(1)}, f32[4,240,256]{2,1,0:T(8,128)}, u32[]{:S(2)}) copy-start(f32[4,240,256]{2,1,0:T(8,128)} %refs_2_.9) | copy-start | bytes 2949124
  0.7 3.2 %copy-start.1 = (f32[4,240,256]{2,1,0:T(8,128)S(1)}, f32[4,240,256]{2,1,0:T(8,128)}, u32[]{:S(2)}) copy-start(f32[4,240,256]{2,1,0:T(8,128)} %refs_1_.9) | copy-start | bytes 2949124
  0.7 3.4 %copy-start = (f32[4,240,256]{2,1,0:T(8,128)S(1)}, f32[4,240,256]{2,1,0:T(8,128)}, u32[]{:S(2)}) copy-start(f32[4,240,256]{2,1,0:T(8,128)} %refs_0_.9) | copy-start | bytes 2949124
  2.0 5.8 %collective-permute-start = (f32[28,256]{1,0:T(8,128)S(1)}, f32[28,256]{1,0:T(8,128)S(1)}, u32[]{:S(2)}, u32[]{:S(2)}) collective-permute-start(f32[28,256]{1,0:T(8,128)S(1)} %get-tuple-element.26.refs_1_.refs_8_), channel_id=1, source_target_pairs={{0,1},{1,0},{2,3},{3,2},{4,5},{5,4},{6,7},{7,6},{8,9},{9,8},{10,11... | collective-permute-start | bytes 86024 | tf_op jit(solution)/shard_map/ppermute | solution.py:656
  2.8 5.4 %collective-permute-start.1 = (f32[28,256]{1,0:T(8,128)S(1)}, f32[28,256]{1,0:T(8,128)S(1)}, u32[]{:S(2)}, u32[]{:S(2)}) collective-permute-start(f32[28,256]{1,0:T(8,128)S(1)} %get-tuple-element.27.refs_2_.refs_9_), channel_id=1, source_target_pairs={{0,128},{1,2},{2,1},{3,4},{4,3},{5,6},{6,5},{7,8},{8,7},{9,10},{10... | collective-permute-start | bytes 86024 | tf_op jit(solution)/shard_map/ppermute | solution.py:655
  8.4 9.3 %collective-permute-start.2 = (f32[20,256]{1,0:T(8,128)S(1)}, f32[20,256]{1,0:T(8,128)S(1)}, u32[]{:S(2)}, u32[]{:S(2)}) collective-permute-start(f32[20,256]{1,0:T(8,128)S(1)} %get-tuple-element.49), channel_id=1, source_target_pairs={{0,16},{1,17},{2,18},{3,19},{4,20},{5,21},{6,22},{7,23},{8,24},{9,... | collective-permute-start | bytes 61448 | tf_op jit(solution)/shard_map/ppermute | solution.py:666
  13.4 4.3 %collective-permute-start.3 = (f32[20,256]{1,0:T(8,128)S(1)}, f32[20,256]{1,0:T(8,128)S(1)}, u32[]{:S(2)}, u32[]{:S(2)}) collective-permute-start(f32[20,256]{1,0:T(8,128)S(1)} %get-tuple-element.44.refs_21_.refs_3_), channel_id=1, source_target_pairs={{0,240},{1,241},{2,242},{3,243},{4,244},{5,245},{6,246},{7,247},{8... | collective-permute-start | bytes 61448 | tf_op jit(solution)/shard_map/ppermute | solution.py:676

commit v5 on v4

--- a/solution.py
+++ b/solution.py
@@ -10,7 +10,7 @@
 F32 = jnp.float32
 AXES = ("lon", "lat")
 LANES = 128
-ROW_FIELDS = 7
+ROW_FIELDS = 6
 COL_FIELDS = 5
 
 
@@ -85,7 +85,9 @@
         below = cvert * (p - down_level(p))
         total = diag + w_east + pltpu.roll(w_east, 1, 1) + w_in + cvert + w_up
         number = forcing - diag * p + h_east - pltpu.roll(h_east, 1, 1) + h_in + h_up - below
-        return jnp.concatenate((p, wn, clat, total, number, clon, we), 0)
+        ends = jnp.where(lane == 1, pltpu.roll(we, 1, 1), clon)
+        ends = jnp.where(lane == width - 2, pltpu.roll(we, width - 1, 1), ends)
+        return jnp.concatenate((p, wn, clat, total, number, ends), 0)
 
     start = lat * rows
     south = message(low, 0, 1, start + 1, 1.0)
@@ -101,7 +103,7 @@
     high = pl.BlockSpec((lev, 8, width), lambda i: (0, rows // 8 - 1, 0))
     shape = jax.ShapeDtypeStruct((ROW_FIELDS * lev, width), F32)
     pinned = [pltpu.with_memory_space_constraint(f, pltpu.HBM) for f in fields]
-    out = pl.BlockSpec((ROW_FIELDS * lev, width), lambda i: (0, 0))
+    out = pl.BlockSpec(memory_space=pltpu.VMEM)
     return pl.pallas_call(
         lambda *refs: rows_kernel(lat_total, rows, *refs),
         grid=(1,),
@@ -113,7 +115,7 @@
     )(*pinned, *pinned)
 
 
-CHUNKS = 5
+CHUNKS = 3
 PAD = 8
 BLOCK = 48
 VMEM_LIMIT = 24 * 2**20
@@ -255,7 +257,7 @@
     return jnp.where(even, far, near), jnp.where(even, near, far)
 
 
-def columns_kernel(lat_total, rows, cols, near, far, near_in, far_in, _, west_ref, east_ref, sent_ref):
+def columns_kernel(lat_total, rows, cols, far, near, far_in, near_in, _, west_ref, east_ref, sent_ref):
     lat = lax.axis_index("lat")
     even = lat % 2 == 0
     own_s, own_n = pick(even, near[...], far[...])
@@ -267,11 +269,11 @@
     lane = lax.broadcasted_iota(jnp.int32, (4, width), 1)
 
     def side(at):
-        source = 0 if at == 0 else width - 1
+        source, inner = (0, 1) if at == 0 else (width - 1, width - 2)
         base = at * COL_FIELDS * 4
         p, we, clon, total, number = [cols[pl.ds(base + i * 4, 4), :] for i in range(COL_FIELDS)]
 
-        def put(x, value, target):
+        def put(x, value, target, source=source):
             return jnp.where(lane == target, pltpu.roll(value, (target - source) % width, 1), x)
 
         no = jnp.zeros_like(p)
@@ -279,7 +281,7 @@
         number = number + put(put(no, -h_s, 0), h_n, rows - 1)
         p = put(put(p, halo_s[0:4], rows), halo_n[0:4], rows + 1)
         clon = put(put(clon, halo_s[20:24], rows), halo_n[20:24], rows + 1)
-        we = put(put(we, halo_s[24:28], rows), halo_n[24:28], rows + 1)
+        we = put(put(we, halo_s[20:24], rows, inner), halo_n[20:24], rows + 1, inner)
         return jnp.concatenate((p, we, clon, total, number), 0)
 
     west_ref[...] = side(0)
@@ -288,7 +290,7 @@
     sent_ref[...] = east
 
 
-def columns_call(lat_total, rows, cols, near, far, near_in, far_in, after):
+def columns_call(lat_total, rows, cols, far, near, far_in, near_in, after):
     shape = jax.ShapeDtypeStruct((cols.shape[0] // 2, cols.shape[1]), F32)
     vmem = pl.BlockSpec(memory_space=pltpu.VMEM)
     return pl.pallas_call(
@@ -298,7 +300,7 @@
         out_shape=[shape] * 3,
         compiler_params=pltpu.CompilerParams(vmem_limit_bytes=SMALL_VMEM),
         name="column_messages",
-    )(cols, near, far, near_in, far_in, after)
+    )(cols, far, near, far_in, near_in, after)
 
 
 def roll_west(tiles, lane):
@@ -313,46 +315,71 @@
 
 EDGE_TERMS = 8
 STATE = 5
-AHEAD = 3
-BETWEEN = 3
+FIRST_AHEAD = 3
+OTHERS_AHEAD = 2
+BETWEEN = (5, 3, 3, 1)
 
 
 def place():
     return lax.rem(lax.axis_index("lon"), lax.axis_size("lon") // 2)
 
 
+def shares(blocks):
+    here, lat, last = place(), lax.axis_index("lat"), lax.axis_size("lat") - 1
+    slow = (lat == 0) | (lat == last) | (lat == last // 2)
+    ahead = jnp.where(slow, OTHERS_AHEAD, 0)
+    ahead = jnp.where((here == 0) & (lat != 1), FIRST_AHEAD, jnp.where(here == 0, OTHERS_AHEAD, ahead))
+    between = ahead
+    for at, count in enumerate(BETWEEN):
+        between = jnp.where(here == at, jnp.maximum(count, ahead), between)
+    between = jnp.where(here == 1, ahead + BETWEEN[1], between)
+    return jnp.minimum(ahead, blocks), jnp.minimum(between, blocks)
+
+
+def late_residual():
+    return (place() > 0) | (lax.axis_index("lat") == 1)
+
+
 def interior_ahead(lat_total, rows, *refs):
-    @pl.when(place() == 0)
+    ahead, _ = shares(rows // BLOCK)
+
+    @pl.when(ahead > 0)
     def _():
-        correction(lat_total, rows, refs[:8], refs[8:11], refs[11:15], refs[15:], 0, AHEAD)
+        correction(lat_total, rows, refs[:8], refs[8:11], refs[11:15], refs[15:], 0, ahead)
 
 
 def interior_between(lat_total, rows, *refs):
     fields, messages, planes, refs = refs[:8], refs[8:12], refs[12:14], refs[14 + STATE + 1 :]
     state, (_, terms_ref, res_ref), scratch = refs[:STATE], refs[STATE : STATE + 3], refs[STATE + 3 :]
-    first = place() == 0
-
-    @pl.when(place() < 2)
+    ahead, between = shares(rows // BLOCK)
+
+    @pl.when(between > ahead)
     def _():
-        begin, end = jnp.where(first, AHEAD, 0), jnp.where(first, rows // BLOCK, BETWEEN)
-        planes_here = (*planes, state[4])
-        correction(lat_total, rows, fields, planes_here, state[:4], scratch, begin, end)
-
-    @pl.when(first)
+        here = (*planes, state[4])
+        correction(lat_total, rows, fields, here, state[:4], scratch, ahead, between)
+
+    @pl.when(place() == 0)
     def _():
         edges(lat_total, rows, fields[4:7], messages, state, terms_ref, scratch)
+
+    @pl.when(jnp.logical_not(late_residual()))
+    def _():
         residual(lat_total, rows, fields[6], state, res_ref, scratch)
 
 
 def interior(lat_total, rows, *refs):
     fields, messages, planes, refs = refs[:8], refs[8:12], refs[12:14], refs[14 + STATE + 2 + 1 :]
     state, terms_ref, res_ref, scratch = refs[:STATE], refs[STATE], refs[STATE + 1], refs[STATE + 2 :]
+    _, between = shares(rows // BLOCK)
 
     @pl.when(place() > 0)
     def _():
-        begin, planes_here = jnp.where(place() == 1, BETWEEN, 0), (*planes, state[4])
-        correction(lat_total, rows, fields, planes_here, state[:4], scratch, begin, rows // BLOCK)
+        here = (*planes, state[4])
+        correction(lat_total, rows, fields, here, state[:4], scratch, between, rows // BLOCK)
         edges(lat_total, rows, fields[4:7], messages, state, terms_ref, scratch)
+
+    @pl.when(late_residual())
+    def _():
         residual(lat_total, rows, fields[6], state, res_ref, scratch)
 
 
@@ -423,7 +450,7 @@
 
 def edges(lat_total, rows, coefs, messages, state, terms_ref, scratch):
     clon_ref, clat_ref, cv_ref = coefs
-    near, far, near_in, far_in = [m[...] for m in messages]
+    far, near, far_in, near_in = [m[...] for m in messages]
     new_ref, delta, _, _, clatb = state
     pack, packed, _ = scratch
     lat = lax.axis_index("lat")
@@ -599,12 +626,11 @@
     def sends(chunk):
         return [
             pltpu.make_async_copy(
-                buf.at[t, :, pl.ds(chunk * per, per), :],
-                out.at[:, pl.ds(chunk * per, per), pl.ds(t * LANES, LANES)],
-                sems.at[chunk, i, t],
+                buf.at[:, pl.ds(chunk * per, per), :],
+                out.at[:, pl.ds(chunk * per, per), :],
+                sems.at[chunk, i],
             )
             for i, (buf, out) in enumerate(((new_buf, new_hbm), (res_buf, res_hbm)))
-            for t in range(2)
         ]
 
     for chunk in range(CHUNKS):
@@ -614,8 +640,9 @@
             to_res = pltpu.roll(packed, (-4 * k - 2) % LANES, 1)
             to_new = pltpu.roll(packed, (-4 * (4 + k) - 2) % LANES, 1)
             for t in range(2):
-                res_buf[t, k, at, :] = res_in[t, k, at, :] + jnp.where(edges[t], to_res, 0.0)
-                new_buf[t, k, at, :] = new_in[t, k, at, :] + jnp.where(edge[t], to_new, 0.0)
+                tile = pl.ds(t * LANES, LANES)
+                res_buf[k, at, tile] = res_in[t, k, at, :] + jnp.where(edges[t], to_res, 0.0)
+                new_buf[k, at, tile] = new_in[t, k, at, :] + jnp.where(edge[t], to_new, 0.0)
         for copy in sends(chunk):
             copy.start()
     for chunk in range(CHUNKS):
@@ -625,7 +652,6 @@
 
 def final_call(shape, planes, messages):
     lev, rows, width = shape
-    tiles = width // LANES
     hbm, vmem = pl.BlockSpec(memory_space=pl.ANY), pl.BlockSpec(memory_space=pltpu.VMEM)
     out = jax.ShapeDtypeStruct(shape, F32)
     return pl.pallas_call(
@@ -633,11 +659,11 @@
         in_specs=[vmem] * 7,
         out_specs=[hbm, hbm],
         out_shape=[out, out],
-        scratch_shapes=[pltpu.VMEM((tiles, lev, rows, LANES), F32)] * 2
+        scratch_shapes=[pltpu.VMEM(shape, F32)] * 2
         + [
             pltpu.VMEM((2, LANES, LANES), F32),
             pltpu.VMEM((256, LANES), F32),
-            pltpu.SemaphoreType.DMA((CHUNKS, 2, tiles)),
+            pltpu.SemaphoreType.DMA((CHUNKS, 2)),
         ],
         compiler_params=pltpu.CompilerParams(vmem_limit_bytes=VMEM_LIMIT),
         name="edges_and_store",
@@ -655,7 +681,7 @@
     far_in = lax.ppermute(far, AXES, rows_far)
     near_in = lax.ppermute(near, AXES, rows_near)
     cols, p_planes, wn_planes, clat_planes = edge_call(lat_total, fields)
-    row_messages = (near, far, near_in, far_in)
+    row_messages = (far, near, far_in, near_in)
     shape = pressure.shape
     planes = (p_planes, wn_planes, clat_planes)
     kinds = ("plane", "padded", "plane", "plane", "padded")

time: 19.5 us -> 18.7 us (0.959)
  the two profiles are of different devices: /device:TPU:25 before, /device:TPU:2 now
where the time goes in v5:
time: 18.7 us; the launch traced here: 18.6 us
  Pallas kernels  10.1 us (54%)
  starting transfers between devices  5.95 us (32%)
  waiting for transfers between devices  1.67 us (9%)
  between operations  0.8 us (4%)
    pallas_call x3, Pallas kernels, interior_call(): pl.pallas_call(lambda *refs: kernel(lat_total, rows, *refs), in_specs=[vm...  5.18 us
    ppermute x1, starting transfers between devices, per_device(): far_in = lax.ppermute(far, AXES, rows_far)  2.51 us
    ppermute x1, starting transfers between devices, per_device(): from_east = lax.ppermute(west, AXES, westward)  2.29 us
    pallas_call x1, Pallas kernels, edge_call(): pl.pallas_call(lambda *refs: edge_kernel(lat_total, rows, *refs), in_spec...  1.84 us
    ppermute x1, waiting for transfers between devices, per_device(): from_west = lax.ppermute(sent, AXES, eastward)  1.66 us
    pallas_call x1, Pallas kernels, final_call(): pl.pallas_call(lambda *refs: final_kernel(rows, *refs), in_specs=[vmem] *...  1.66 us
    pallas_call x1, Pallas kernels, rows_call(): pl.pallas_call(lambda *refs: rows_kernel(lat_total, rows, *refs), grid=(1...  1.32 us
    ppermute x1, starting transfers between devices, per_device(): from_west = lax.ppermute(sent, AXES, eastward)  1.14 us
  transfers between devices with their start and end apart: 4, of which 1 were waited for; matrix products, arithmetic and copies ran while one was open for 0% of the time, Pallas kernels for 38%

profile of v5, /device:TPU:2, one launch (start us, length us, event | category | flops | bytes accessed | tf_op | source)
XLA Modules:
  0.0 18.6 jit_solution(9506406508914716741)
XLA Ops:
  0.6 0.0 copy-start.7
  0.6 0.0 copy-start.6
  0.7 0.0 copy-start.5
  0.7 0.0 copy-start.4
  0.7 0.0 copy-start.3
  0.7 0.0 copy-start.2
  0.7 0.0 copy-start.1
  0.7 0.0 copy-start
  0.7 1.3 %row_messages.1 = (f32[24,256]{1,0:T(8,128)S(1)}, f32[24,256]{1,0:T(8,128)S(1)}) custom-call(f32[4,240,256]{2,1,0:T(8,128)} %refs_0_.9, f32[4,240,256]{2,1,0:T(8,128)} %refs_1_.9, f32[4,240,256]{2,1,0:T(8,128)} %refs_2_.9, f32[4,240,256]{2,1,0:T(8,128)} %refs_3_.9, f32[4,240,256]{2,1,0:T(8,128)} %refs_4_.9, f32[4,240,256]{2,1,0:T(8,128)} %refs_5_.9, ...), custom_call_target="tpu_custom_call" | custom-call | tf_op jit(solution)/shard_map/row_messages/pallas_call | solution.py:107
  2.0 2.5 %collective-permute-start = (f32[24,256]{1,0:T(8,128)S(1)}, f32[24,256]{1,0:T(8,128)S(1)}, u32[]{:S(2)}, u32[]{:S(2)}) collective-permute-start(f32[24,256]{1,0:T(8,128)S(1)} %get-tuple-element.26.refs_1_.refs_8_), channel_id=1, source_target_pairs={{0,128},{1,2},{2,1},{3,4},{4,3},{5,6},{6,5},{7,8},{8,7},{9,10},{10... | collective-permute-start | bytes 73736 | tf_op jit(solution)/shard_map/ppermute | solution.py:681
  4.6 0.0 collective-permute-start.1
  4.6 0.0 copy-done.7
  4.6 0.0 copy-done.6
  4.6 0.0 copy-done.5
  4.6 0.0 copy-done.4
  4.6 0.0 copy-done.3
  4.6 0.0 copy-done.2
  4.6 0.0 copy-done.1
  4.6 0.0 copy-done
  4.6 1.8 %edge_columns.1 = (f32[40,256]{1,0:T(8,128)S(1)}, f32[2,4,256,128]{3,2,1,0:T(8,128)S(1)}, f32[2,4,256,128]{3,2,1,0:T(8,128)S(1)}, f32[2,4,256,128]{3,2,1,0:T(8,128)S(1)}) custom-call(f32[4,240,256]{2,1,0:T(8,128)S(1)} %copy-done, f32[4,240,256]{2,1,0:T(8,128)S(1)} %copy-done.1, f32[4,240,256]{2,1,0:T(8,128)S(1)} %copy-done.2, f32[4,240,256]{2,1,0:T(8,128)S(1)} %copy-done.3, ...), custom_call_target="tpu_custom_call" | custom-call | flops 10000000 | bytes 8000000 | tf_op jit(solution)/shard_map/edge_columns/pallas_call | solution.py:231
  6.5 1.8 %interior_ahead.1 = (f32[2,4,240,128]{3,2,1,0:T(8,128)S(1)}, f32[2,4,256,128]{3,2,1,0:T(8,128)S(1)}, f32[2,4,240,128]{3,2,1,0:T(8,128)S(1)}, f32[2,4,240,128]{3,2,1,0:T(8,128)S(1)}) custom-call(f32[4,240,256]{2,1,0:T(8,128)S(1)} %copy-done, f32[4,240,256]{2,1,0:T(8,128)S(1)} %copy-done.1, f32[4,240,256]{2,1,0:T(8,128)S(1)} %copy-done.2, ...), custom_call_target="tpu_custom_call" | custom-call | flops 20000000 | bytes 16000000 | tf_op jit(solution)/shard_map/interior_ahead/pallas_call | solution.py:573
  8.3 0.0 collective-permute-done.refs_3_.refs_10_
  8.3 0.0 collective-permute-done.1.refs_4_.refs_11_
  8.3 0.1 column_messages.1
  8.5 1.1 %collective-permute-start.2 = (f32[20,256]{1,0:T(8,128)S(1)}, f32[20,256]{1,0:T(8,128)S(1)}, u32[]{:S(2)}, u32[]{:S(2)}) collective-permute-start(f32[20,256]{1,0:T(8,128)S(1)} %get-tuple-element.49), channel_id=1, source_target_pairs={{0,16},{1,17},{2,18},{3,19},{4,20},{5,21},{6,22},{7,23},{8,24},{9,... | collective-permute-start | bytes 61448 | tf_op jit(solution)/shard_map/ppermute | solution.py:692
  9.6 3.3 %interior_between.1 = (f32[2,4,240,128]{3,2,1,0:T(8,128)S(1)}, f32[2,4,256,128]{3,2,1,0:T(8,128)S(1)}, f32[2,4,240,128]{3,2,1,0:T(8,128)S(1)}, f32[2,4,240,128]{...) custom-call(f32[4,240,256]{2,1,0:T(8,128)S(1)} %copy-done, ...), custom_call_target="tpu_custom_call", output_to_operand_aliasing={{0}: (14, {}), {1}: (15, {}), {2}: (16, {}), {3}: (17, {}),... | custom-call | flops 20000000 | bytes 16000000 | tf_op jit(solution)/shard_map/interior_between/pallas_call | solution.py:573
  13.0 2.3 %collective-permute-start.3 = (f32[20,256]{1,0:T(8,128)S(1)}, f32[20,256]{1,0:T(8,128)S(1)}, u32[]{:S(2)}, u32[]{:S(2)}) collective-permute-start(f32[20,256]{1,0:T(8,128)S(1)} %get-tuple-element.44.refs_21_.refs_3_), channel_id=1, source_target_pairs={{0,240},{1,241},{2,242},{3,243},{4,244},{5,245},{6,246},{7,247},{8... | collective-permute-start | bytes 61448 | tf_op jit(solution)/shard_map/ppermute | solution.py:702
  15.3 1.7 %collective-permute-done.2.refs_5_ = f32[20,256]{1,0:T(8,128)S(1)} collective-permute-done((f32[20,256]{1,0:T(8,128)S(1)}, f32[20,256]{1,0:T(8,128)S(1)}, u32[]{:S(2)}, u32[]{:S(2)}) %collective-permute-start.2) | collective-permute-done | bytes 20512 | tf_op jit(solution)/shard_map/ppermute | solution.py:692
  16.9 0.0 collective-permute-done.3.refs_6_
  16.9 1.7 %edges_and_store.1 = (f32[4,240,256]{2,1,0:T(8,128)}, f32[4,240,256]{2,1,0:T(8,128)}) custom-call(f32[2,4,240,128]{3,2,1,0:T(8,128)S(1)} %get-tuple-element.45.refs_0_, f32[2,4,240,128]{3,2,1,0:T(8,128)S(1)} %get-tuple-element.46.refs_1_, f32[64,256]{1,0:T(8,128)S(1)} %get-tuple-element.47.refs_2_, f32[20,256]{1,0:T(8,128)S(1)} %get-tuple-element.44.refs_21_.refs_3_, ...), custom_call_target="tpu_custom_call" | custom-call | tf_op jit(solution)/shard_map/edges_and_store/pallas_call | solution.py:657
  (1 shorter events, 0.0 us)
Async XLA Ops:
  0.6 3.9 %copy-start.7 = (f32[4,240,256]{2,1,0:T(8,128)S(1)}, f32[4,240,256]{2,1,0:T(8,128)}, u32[]{:S(2)}) copy-start(f32[4,240,256]{2,1,0:T(8,128)} %refs_7_.9) | copy-start | bytes 2949124
  0.6 3.9 %copy-start.6 = (f32[4,240,256]{2,1,0:T(8,128)S(1)}, f32[4,240,256]{2,1,0:T(8,128)}, u32[]{:S(2)}) copy-start(f32[4,240,256]{2,1,0:T(8,128)} %refs_6_.9) | copy-start | bytes 2949124
  0.7 3.9 %copy-start.5 = (f32[4,240,256]{2,1,0:T(8,128)S(1)}, f32[4,240,256]{2,1,0:T(8,128)}, u32[]{:S(2)}) copy-start(f32[4,240,256]{2,1,0:T(8,128)} %refs_5_.9) | copy-start | bytes 2949124
  0.7 3.9 %copy-start.4 = (f32[4,240,256]{2,1,0:T(8,128)S(1)}, f32[4,240,256]{2,1,0:T(8,128)}, u32[]{:S(2)}) copy-start(f32[4,240,256]{2,1,0:T(8,128)} %refs_4_.9) | copy-start | bytes 2949124
  0.7 3.9 %copy-start.3 = (f32[4,240,256]{2,1,0:T(8,128)S(1)}, f32[4,240,256]{2,1,0:T(8,128)}, u32[]{:S(2)}) copy-start(f32[4,240,256]{2,1,0:T(8,128)} %refs_3_.9) | copy-start | bytes 2949124
  0.7 3.9 %copy-start.2 = (f32[4,240,256]{2,1,0:T(8,128)S(1)}, f32[4,240,256]{2,1,0:T(8,128)}, u32[]{:S(2)}) copy-start(f32[4,240,256]{2,1,0:T(8,128)} %refs_2_.9) | copy-start | bytes 2949124
  0.7 3.9 %copy-start.1 = (f32[4,240,256]{2,1,0:T(8,128)S(1)}, f32[4,240,256]{2,1,0:T(8,128)}, u32[]{:S(2)}) copy-start(f32[4,240,256]{2,1,0:T(8,128)} %refs_1_.9) | copy-start | bytes 2949124
  0.7 3.9 %copy-start = (f32[4,240,256]{2,1,0:T(8,128)S(1)}, f32[4,240,256]{2,1,0:T(8,128)}, u32[]{:S(2)}) copy-start(f32[4,240,256]{2,1,0:T(8,128)} %refs_0_.9) | copy-start | bytes 2949124
  2.0 6.3 %collective-permute-start = (f32[24,256]{1,0:T(8,128)S(1)}, f32[24,256]{1,0:T(8,128)S(1)}, u32[]{:S(2)}, u32[]{:S(2)}) collective-permute-start(f32[24,256]{1,0:T(8,128)S(1)} %get-tuple-element.26.refs_1_.refs_8_), channel_id=1, source_target_pairs={{0,128},{1,2},{2,1},{3,4},{4,3},{5,6},{6,5},{7,8},{8,7},{9,10},{10... | collective-permute-start | bytes 73736 | tf_op jit(solution)/shard_map/ppermute | solution.py:681
  4.6 3.8 %collective-permute-start.1 = (f32[24,256]{1,0:T(8,128)S(1)}, f32[24,256]{1,0:T(8,128)S(1)}, u32[]{:S(2)}, u32[]{:S(2)}) collective-permute-start(f32[24,256]{1,0:T(8,128)S(1)} %get-tuple-element.27.refs_2_.refs_9_), channel_id=1, source_target_pairs={{0,1},{1,0},{2,3},{3,2},{4,5},{5,4},{6,7},{7,6},{8,9},{9,8},{10,11... | collective-permute-start | bytes 73736 | tf_op jit(solution)/shard_map/ppermute | solution.py:682
  8.5 8.4 %collective-permute-start.2 = (f32[20,256]{1,0:T(8,128)S(1)}, f32[20,256]{1,0:T(8,128)S(1)}, u32[]{:S(2)}, u32[]{:S(2)}) collective-permute-start(f32[20,256]{1,0:T(8,128)S(1)} %get-tuple-element.49), channel_id=1, source_target_pairs={{0,16},{1,17},{2,18},{3,19},{4,20},{5,21},{6,22},{7,23},{8,24},{9,... | collective-permute-start | bytes 61448 | tf_op jit(solution)/shard_map/ppermute | solution.py:692
  13.0 4.0 %collective-permute-start.3 = (f32[20,256]{1,0:T(8,128)S(1)}, f32[20,256]{1,0:T(8,128)S(1)}, u32[]{:S(2)}, u32[]{:S(2)}) collective-permute-start(f32[20,256]{1,0:T(8,128)S(1)} %get-tuple-element.44.refs_21_.refs_3_), channel_id=1, source_target_pairs={{0,240},{1,241},{2,242},{3,243},{4,244},{5,245},{6,246},{7,247},{8... | collective-permute-start | bytes 61448 | tf_op jit(solution)/shard_map/ppermute | solution.py:702

commit v6 on v5

--- a/solution.py
+++ b/solution.py
@@ -83,8 +83,12 @@
         w_up = up_level(cvert)
         h_up = w_up * (up_level(p) - p)
         below = cvert * (p - down_level(p))
-        total = diag + w_east + pltpu.roll(w_east, 1, 1) + w_in + cvert + w_up
-        number = forcing - diag * p + h_east - pltpu.roll(h_east, 1, 1) + h_in + h_up - below
+        west = lane > 0
+        clon_w, p_w, we_w = [pltpu.roll(x, 1, 1) for x in (clon, p, we)]
+        w_west = jnp.where(west, 0.5 * (clon + clon_w), 0.0)
+        h_west = jnp.where(west, w_west * (p - p_w) - 0.5 * (we_w + we), 0.0)
+        total = diag + w_east + w_west + w_in + cvert + w_up
+        number = forcing - diag * p + h_east - h_west + h_in + h_up - below
         ends = jnp.where(lane == 1, pltpu.roll(we, 1, 1), clon)
         ends = jnp.where(lane == width - 2, pltpu.roll(we, width - 1, 1), ends)
         return jnp.concatenate((p, wn, clat, total, number, ends), 0)
@@ -317,7 +321,7 @@
 STATE = 5
 FIRST_AHEAD = 3
 OTHERS_AHEAD = 2
-BETWEEN = (5, 3, 3, 1)
+BETWEEN = (5, 3, 3, 1, 2, 1)
 
 
 def place():

time: 18.7 us -> 18.6 us (level)
  no operation moved by 1% of the time
where the time goes in v6:
time: 18.6 us; the launch traced here: 18.5 us
  Pallas kernels  10.1 us (54%)
  starting transfers between devices  5.95 us (32%)
  waiting for transfers between devices  1.67 us (9%)
  between operations  0.8 us (4%)
    pallas_call x3, Pallas kernels, interior_call(): pl.pallas_call(lambda *refs: kernel(lat_total, rows, *refs), in_specs=[vm...  5.18 us
    ppermute x1, starting transfers between devices, per_device(): far_in = lax.ppermute(far, AXES, rows_far)  2.51 us
    ppermute x1, starting transfers between devices, per_device(): from_east = lax.ppermute(west, AXES, westward)  2.29 us
    pallas_call x1, Pallas kernels, edge_call(): pl.pallas_call(lambda *refs: edge_kernel(lat_total, rows, *refs), in_spec...  1.84 us
    pallas_call x1, Pallas kernels, final_call(): pl.pallas_call(lambda *refs: final_kernel(rows, *refs), in_specs=[vmem] *...  1.66 us
    ppermute x1, waiting for transfers between devices, per_device(): from_west = lax.ppermute(sent, AXES, eastward)  1.66 us
    pallas_call x1, Pallas kernels, rows_call(): pl.pallas_call(lambda *refs: rows_kernel(lat_total, rows, *refs), grid=(1...  1.27 us
    ppermute x1, starting transfers between devices, per_device(): from_west = lax.ppermute(sent, AXES, eastward)  1.14 us
  transfers between devices with their start and end apart: 4, of which 1 were waited for; matrix products, arithmetic and copies ran while one was open for 0% of the time, Pallas kernels for 38%

profile of v6, /device:TPU:2, one launch (start us, length us, event | category | flops | bytes accessed | tf_op | source)
XLA Modules:
  0.0 18.5 jit_solution(5043057267736582742)
XLA Ops:
  0.6 0.0 copy-start.7
  0.6 0.0 copy-start.6
  0.7 0.0 copy-start.5
  0.7 0.0 copy-start.4
  0.7 0.0 copy-start.3
  0.7 0.0 copy-start.2
  0.7 0.0 copy-start.1
  0.7 0.0 copy-start
  0.7 1.3 %row_messages.1 = (f32[24,256]{1,0:T(8,128)S(1)}, f32[24,256]{1,0:T(8,128)S(1)}) custom-call(f32[4,240,256]{2,1,0:T(8,128)} %refs_0_.9, f32[4,240,256]{2,1,0:T(8,128)} %refs_1_.9, f32[4,240,256]{2,1,0:T(8,128)} %refs_2_.9, f32[4,240,256]{2,1,0:T(8,128)} %refs_3_.9, f32[4,240,256]{2,1,0:T(8,128)} %refs_4_.9, f32[4,240,256]{2,1,0:T(8,128)} %refs_5_.9, ...), custom_call_target="tpu_custom_call" | custom-call | tf_op jit(solution)/shard_map/row_messages/pallas_call | solution.py:111
  2.0 2.5 %collective-permute-start = (f32[24,256]{1,0:T(8,128)S(1)}, f32[24,256]{1,0:T(8,128)S(1)}, u32[]{:S(2)}, u32[]{:S(2)}) collective-permute-start(f32[24,256]{1,0:T(8,128)S(1)} %get-tuple-element.26.refs_1_.refs_8_), channel_id=1, source_target_pairs={{0,128},{1,2},{2,1},{3,4},{4,3},{5,6},{6,5},{7,8},{8,7},{9,10},{10... | collective-permute-start | bytes 73736 | tf_op jit(solution)/shard_map/ppermute | solution.py:685
  4.5 0.0 collective-permute-start.1
  4.5 0.0 copy-done.7
  4.5 0.0 copy-done.6
  4.5 0.0 copy-done.5
  4.5 0.0 copy-done.4
  4.5 0.0 copy-done.3
  4.5 0.0 copy-done.2
  4.5 0.0 copy-done.1
  4.6 0.0 copy-done
  4.6 1.8 %edge_columns.1 = (f32[40,256]{1,0:T(8,128)S(1)}, f32[2,4,256,128]{3,2,1,0:T(8,128)S(1)}, f32[2,4,256,128]{3,2,1,0:T(8,128)S(1)}, f32[2,4,256,128]{3,2,1,0:T(8,128)S(1)}) custom-call(f32[4,240,256]{2,1,0:T(8,128)S(1)} %copy-done, f32[4,240,256]{2,1,0:T(8,128)S(1)} %copy-done.1, f32[4,240,256]{2,1,0:T(8,128)S(1)} %copy-done.2, f32[4,240,256]{2,1,0:T(8,128)S(1)} %copy-done.3, ...), custom_call_target="tpu_custom_call" | custom-call | flops 10000000 | bytes 8000000 | tf_op jit(solution)/shard_map/edge_columns/pallas_call | solution.py:235
  6.4 1.8 %interior_ahead.1 = (f32[2,4,240,128]{3,2,1,0:T(8,128)S(1)}, f32[2,4,256,128]{3,2,1,0:T(8,128)S(1)}, f32[2,4,240,128]{3,2,1,0:T(8,128)S(1)}, f32[2,4,240,128]{3,2,1,0:T(8,128)S(1)}) custom-call(f32[4,240,256]{2,1,0:T(8,128)S(1)} %copy-done, f32[4,240,256]{2,1,0:T(8,128)S(1)} %copy-done.1, f32[4,240,256]{2,1,0:T(8,128)S(1)} %copy-done.2, ...), custom_call_target="tpu_custom_call" | custom-call | flops 20000000 | bytes 16000000 | tf_op jit(solution)/shard_map/interior_ahead/pallas_call | solution.py:577
  8.3 0.0 collective-permute-done.refs_3_.refs_10_
  8.3 0.0 collective-permute-done.1.refs_4_.refs_11_
  8.3 0.1 column_messages.1
  8.4 1.1 %collective-permute-start.2 = (f32[20,256]{1,0:T(8,128)S(1)}, f32[20,256]{1,0:T(8,128)S(1)}, u32[]{:S(2)}, u32[]{:S(2)}) collective-permute-start(f32[20,256]{1,0:T(8,128)S(1)} %get-tuple-element.49), channel_id=1, source_target_pairs={{0,16},{1,17},{2,18},{3,19},{4,20},{5,21},{6,22},{7,23},{8,24},{9,... | collective-permute-start | bytes 61448 | tf_op jit(solution)/shard_map/ppermute | solution.py:696
  9.6 3.3 %interior_between.1 = (f32[2,4,240,128]{3,2,1,0:T(8,128)S(1)}, f32[2,4,256,128]{3,2,1,0:T(8,128)S(1)}, f32[2,4,240,128]{3,2,1,0:T(8,128)S(1)}, f32[2,4,240,128]{...) custom-call(f32[4,240,256]{2,1,0:T(8,128)S(1)} %copy-done, ...), custom_call_target="tpu_custom_call", output_to_operand_aliasing={{0}: (14, {}), {1}: (15, {}), {2}: (16, {}), {3}: (17, {}),... | custom-call | flops 20000000 | bytes 16000000 | tf_op jit(solution)/shard_map/interior_between/pallas_call | solution.py:577
  12.9 2.3 %collective-permute-start.3 = (f32[20,256]{1,0:T(8,128)S(1)}, f32[20,256]{1,0:T(8,128)S(1)}, u32[]{:S(2)}, u32[]{:S(2)}) collective-permute-start(f32[20,256]{1,0:T(8,128)S(1)} %get-tuple-element.44.refs_21_.refs_3_), channel_id=1, source_target_pairs={{0,240},{1,241},{2,242},{3,243},{4,244},{5,245},{6,246},{7,247},{8... | collective-permute-start | bytes 61448 | tf_op jit(solution)/shard_map/ppermute | solution.py:706
  15.2 1.7 %collective-permute-done.2.refs_5_ = f32[20,256]{1,0:T(8,128)S(1)} collective-permute-done((f32[20,256]{1,0:T(8,128)S(1)}, f32[20,256]{1,0:T(8,128)S(1)}, u32[]{:S(2)}, u32[]{:S(2)}) %collective-permute-start.2) | collective-permute-done | bytes 20512 | tf_op jit(solution)/shard_map/ppermute | solution.py:696
  16.9 0.0 collective-permute-done.3.refs_6_
  16.9 1.7 %edges_and_store.1 = (f32[4,240,256]{2,1,0:T(8,128)}, f32[4,240,256]{2,1,0:T(8,128)}) custom-call(f32[2,4,240,128]{3,2,1,0:T(8,128)S(1)} %get-tuple-element.45.refs_0_, f32[2,4,240,128]{3,2,1,0:T(8,128)S(1)} %get-tuple-element.46.refs_1_, f32[64,256]{1,0:T(8,128)S(1)} %get-tuple-element.47.refs_2_, f32[20,256]{1,0:T(8,128)S(1)} %get-tuple-element.44.refs_21_.refs_3_, ...), custom_call_target="tpu_custom_call" | custom-call | tf_op jit(solution)/shard_map/edges_and_store/pallas_call | solution.py:661
  (1 shorter events, 0.0 us)
Async XLA Ops:
  0.6 3.9 %copy-start.7 = (f32[4,240,256]{2,1,0:T(8,128)S(1)}, f32[4,240,256]{2,1,0:T(8,128)}, u32[]{:S(2)}) copy-start(f32[4,240,256]{2,1,0:T(8,128)} %refs_7_.9) | copy-start | bytes 2949124
  0.6 3.9 %copy-start.6 = (f32[4,240,256]{2,1,0:T(8,128)S(1)}, f32[4,240,256]{2,1,0:T(8,128)}, u32[]{:S(2)}) copy-start(f32[4,240,256]{2,1,0:T(8,128)} %refs_6_.9) | copy-start | bytes 2949124
  0.7 3.9 %copy-start.5 = (f32[4,240,256]{2,1,0:T(8,128)S(1)}, f32[4,240,256]{2,1,0:T(8,128)}, u32[]{:S(2)}) copy-start(f32[4,240,256]{2,1,0:T(8,128)} %refs_5_.9) | copy-start | bytes 2949124
  0.7 3.9 %copy-start.4 = (f32[4,240,256]{2,1,0:T(8,128)S(1)}, f32[4,240,256]{2,1,0:T(8,128)}, u32[]{:S(2)}) copy-start(f32[4,240,256]{2,1,0:T(8,128)} %refs_4_.9) | copy-start | bytes 2949124
  0.7 3.9 %copy-start.3 = (f32[4,240,256]{2,1,0:T(8,128)S(1)}, f32[4,240,256]{2,1,0:T(8,128)}, u32[]{:S(2)}) copy-start(f32[4,240,256]{2,1,0:T(8,128)} %refs_3_.9) | copy-start | bytes 2949124
  0.7 3.9 %copy-start.2 = (f32[4,240,256]{2,1,0:T(8,128)S(1)}, f32[4,240,256]{2,1,0:T(8,128)}, u32[]{:S(2)}) copy-start(f32[4,240,256]{2,1,0:T(8,128)} %refs_2_.9) | copy-start | bytes 2949124
  0.7 3.9 %copy-start.1 = (f32[4,240,256]{2,1,0:T(8,128)S(1)}, f32[4,240,256]{2,1,0:T(8,128)}, u32[]{:S(2)}) copy-start(f32[4,240,256]{2,1,0:T(8,128)} %refs_1_.9) | copy-start | bytes 2949124
  0.7 3.9 %copy-start = (f32[4,240,256]{2,1,0:T(8,128)S(1)}, f32[4,240,256]{2,1,0:T(8,128)}, u32[]{:S(2)}) copy-start(f32[4,240,256]{2,1,0:T(8,128)} %refs_0_.9) | copy-start | bytes 2949124
  2.0 6.3 %collective-permute-start = (f32[24,256]{1,0:T(8,128)S(1)}, f32[24,256]{1,0:T(8,128)S(1)}, u32[]{:S(2)}, u32[]{:S(2)}) collective-permute-start(f32[24,256]{1,0:T(8,128)S(1)} %get-tuple-element.26.refs_1_.refs_8_), channel_id=1, source_target_pairs={{0,128},{1,2},{2,1},{3,4},{4,3},{5,6},{6,5},{7,8},{8,7},{9,10},{10... | collective-permute-start | bytes 73736 | tf_op jit(solution)/shard_map/ppermute | solution.py:685
  4.5 3.8 %collective-permute-start.1 = (f32[24,256]{1,0:T(8,128)S(1)}, f32[24,256]{1,0:T(8,128)S(1)}, u32[]{:S(2)}, u32[]{:S(2)}) collective-permute-start(f32[24,256]{1,0:T(8,128)S(1)} %get-tuple-element.27.refs_2_.refs_9_), channel_id=1, source_target_pairs={{0,1},{1,0},{2,3},{3,2},{4,5},{5,4},{6,7},{7,6},{8,9},{9,8},{10,11... | collective-permute-start | bytes 73736 | tf_op jit(solution)/shard_map/ppermute | solution.py:686
  8.4 8.4 %collective-permute-start.2 = (f32[20,256]{1,0:T(8,128)S(1)}, f32[20,256]{1,0:T(8,128)S(1)}, u32[]{:S(2)}, u32[]{:S(2)}) collective-permute-start(f32[20,256]{1,0:T(8,128)S(1)} %get-tuple-element.49), channel_id=1, source_target_pairs={{0,16},{1,17},{2,18},{3,19},{4,20},{5,21},{6,22},{7,23},{8,24},{9,... | collective-permute-start | bytes 61448 | tf_op jit(solution)/shard_map/ppermute | solution.py:696
  12.9 4.0 %collective-permute-start.3 = (f32[20,256]{1,0:T(8,128)S(1)}, f32[20,256]{1,0:T(8,128)S(1)}, u32[]{:S(2)}, u32[]{:S(2)}) collective-permute-start(f32[20,256]{1,0:T(8,128)S(1)} %get-tuple-element.44.refs_21_.refs_3_), channel_id=1, source_target_pairs={{0,240},{1,241},{2,242},{3,243},{4,244},{5,245},{6,246},{7,247},{8... | collective-permute-start | bytes 61448 | tf_op jit(solution)/shard_map/ppermute | solution.py:706

commit v7 on v6

--- a/solution.py
+++ b/solution.py
@@ -97,8 +97,16 @@
     south = message(low, 0, 1, start + 1, 1.0)
     north = message(high, 7, 6, start + rows - 1, -1.0)
     even = lat % 2 == 0
-    near_ref[...] = jnp.where(even, north, south)
-    far_ref[...] = jnp.where(even, south, north)
+
+    @pl.when(even)
+    def _():
+        near_ref[...] = north
+        far_ref[...] = south
+
+    @pl.when(jnp.logical_not(even))
+    def _():
+        near_ref[...] = south
+        far_ref[...] = north
 
 
 def rows_call(lat_total, fields):
@@ -119,7 +127,7 @@
     )(*pinned, *pinned)
 
 
-CHUNKS = 3
+CUTS = (0, 24, 96, 240)
 PAD = 8
 BLOCK = 48
 VMEM_LIMIT = 24 * 2**20
@@ -291,17 +299,21 @@
     west_ref[...] = side(0)
     east = side(1)
     east_ref[...] = east
-    sent_ref[...] = east
+    for i in range(COL_FIELDS):
+        for t in range(2):
+            half = east[4 * i : 4 * i + 4, t * LANES : (t + 1) * LANES]
+            sent_ref[pl.ds(8 * i + 4 * t, 4), :] = half
 
 
 def columns_call(lat_total, rows, cols, far, near, far_in, near_in, after):
     shape = jax.ShapeDtypeStruct((cols.shape[0] // 2, cols.shape[1]), F32)
+    packed = jax.ShapeDtypeStruct((cols.shape[0], LANES), F32)
     vmem = pl.BlockSpec(memory_space=pltpu.VMEM)
     return pl.pallas_call(
         lambda *refs: columns_kernel(lat_total, rows, *refs),
         in_specs=[vmem] * 6,
         out_specs=[vmem] * 3,
-        out_shape=[shape] * 3,
+        out_shape=[shape, shape, packed],
         compiler_params=pltpu.CompilerParams(vmem_limit_bytes=SMALL_VMEM),
         name="column_messages",
     )(cols, far, near, far_in, near_in, after)
@@ -597,7 +609,7 @@
     width = 2 * LANES
     wide = lax.broadcasted_iota(jnp.int32, (4, width), 1)
     low, high, inside = wide == 0, wide == rows - 1, wide < rows
-    own, halo = (own_w, own_e), (halo_w, halo_e)
+    own = (own_w, own_e)
 
     def ends(x):
         south, north = pltpu.roll(x, width - rows, 1), pltpu.roll(x, width - 2, 1)
@@ -605,7 +617,11 @@
 
     for side, (edge, inner, sign) in enumerate(((2, 3, 1.0), (1, 0, -1.0))):
         o_p, o_we, o_clon, o_total, o_number = [own[side][pl.ds(4 * i, 4), :] for i in range(5)]
-        h_p, h_we, h_clon, h_total, h_number = [halo[side][pl.ds(4 * i, 4), :] for i in range(5)]
+        if side == 0:
+            h = [[halo_w[pl.ds(8 * i + 4 * t, 4), :] for t in range(2)] for i in range(5)]
+            h_p, h_we, h_clon, h_total, h_number = [jnp.concatenate(pair, 1) for pair in h]
+        else:
+            h_p, h_we, h_clon, h_total, h_number = [halo_e[pl.ds(4 * i, 4), :] for i in range(5)]
         a_n, a_s, w_in, above, below, c_w, c_number, c_total = [
             terms[pl.ds((side * EDGE_TERMS + i) * 4, 4), :] for i in range(EDGE_TERMS)
         ]
@@ -622,23 +638,22 @@
     for t in range(2):
         colv[pl.ds(t * LANES, LANES), :] = stack[t].T
 
-    per = rows // CHUNKS
-    lane = lax.broadcasted_iota(jnp.int32, (per, LANES), 1)
-    edges = (lane < 2, lane >= LANES - 2)
-    edge = (lane == 0, lane == LANES - 1)
+    cuts = [rows * cut // CUTS[-1] for cut in CUTS]
+    chunks = [(begin, end - begin) for begin, end in zip(cuts, cuts[1:])]
 
     def sends(chunk):
         return [
             pltpu.make_async_copy(
-                buf.at[:, pl.ds(chunk * per, per), :],
-                out.at[:, pl.ds(chunk * per, per), :],
-                sems.at[chunk, i],
+                buf.at[:, pl.ds(*chunks[chunk]), :], out.at[:, pl.ds(*chunks[chunk]), :], sems.at[chunk, i]
             )
             for i, (buf, out) in enumerate(((new_buf, new_hbm), (res_buf, res_hbm)))
         ]
 
-    for chunk in range(CHUNKS):
-        at = pl.ds(chunk * per, per)
+    for chunk, (begin, count) in enumerate(chunks):
+        at = pl.ds(begin, count)
+        lane = lax.broadcasted_iota(jnp.int32, (count, LANES), 1)
+        edges = (lane < 2, lane >= LANES - 2)
+        edge = (lane == 0, lane == LANES - 1)
         packed = colv[at, :]
         for k in range(4):
             to_res = pltpu.roll(packed, (-4 * k - 2) % LANES, 1)
@@ -649,7 +664,7 @@
                 new_buf[k, at, tile] = new_in[t, k, at, :] + jnp.where(edge[t], to_new, 0.0)
         for copy in sends(chunk):
             copy.start()
-    for chunk in range(CHUNKS):
+    for chunk in range(len(chunks)):
         for copy in sends(chunk):
             copy.wait()
 
@@ -667,7 +682,7 @@
         + [
             pltpu.VMEM((2, LANES, LANES), F32),
             pltpu.VMEM((256, LANES), F32),
-            pltpu.SemaphoreType.DMA((CHUNKS, 2)),
+            pltpu.SemaphoreType.DMA((len(CUTS) - 1, 2)),
         ],
         compiler_params=pltpu.CompilerParams(vmem_limit_bytes=VMEM_LIMIT),
         name="edges_and_store",

time: 18.6 us -> 18.6 us (level)
  no operation moved by 1% of the time
where the time goes in v7:
time: 18.6 us; the launch traced here: 18.5 us
  Pallas kernels  10 us (54%)
  starting transfers between devices  5.95 us (32%)
  waiting for transfers between devices  1.62 us (9%)
  between operations  0.81 us (4%)
    pallas_call x3, Pallas kernels, interior_call(): pl.pallas_call(lambda *refs: kernel(lat_total, rows, *refs), in_specs=[vm...  5.18 us
    ppermute x1, starting transfers between devices, per_device(): far_in = lax.ppermute(far, AXES, rows_far)  2.51 us
    ppermute x1, starting transfers between devices, per_device(): from_east = lax.ppermute(west, AXES, westward)  2.29 us
    pallas_call x1, Pallas kernels, edge_call(): pl.pallas_call(lambda *refs: edge_kernel(lat_total, rows, *refs), in_spec...  1.84 us
    pallas_call x1, Pallas kernels, final_call(): pl.pallas_call(lambda *refs: final_kernel(rows, *refs), in_specs=[vmem] *...  1.63 us
    ppermute x1, waiting for transfers between devices, per_device(): from_west = lax.ppermute(sent, AXES, eastward)  1.62 us
    pallas_call x1, Pallas kernels, rows_call(): pl.pallas_call(lambda *refs: rows_kernel(lat_total, rows, *refs), grid=(1...  1.27 us
    ppermute x1, starting transfers between devices, per_device(): from_west = lax.ppermute(sent, AXES, eastward)  1.14 us
  transfers between devices with their start and end apart: 4, of which 1 were waited for; matrix products, arithmetic and copies ran while one was open for 0% of the time, Pallas kernels for 38%

profile of v7, /device:TPU:2, one launch (start us, length us, event | category | flops | bytes accessed | tf_op | source)
XLA Modules:
  0.0 18.5 jit_solution(17179901091992344566)
XLA Ops:
  0.6 0.0 copy-start.7
  0.6 0.0 copy-start.6
  0.7 0.0 copy-start.5
  0.7 0.0 copy-start.4
  0.7 0.0 copy-start.3
  0.7 0.0 copy-start.2
  0.7 0.0 copy-start.1
  0.7 0.0 copy-start
  0.7 1.3 %row_messages.1 = (f32[24,256]{1,0:T(8,128)S(1)}, f32[24,256]{1,0:T(8,128)S(1)}) custom-call(f32[4,240,256]{2,1,0:T(8,128)} %refs_0_.9, f32[4,240,256]{2,1,0:T(8,128)} %refs_1_.9, f32[4,240,256]{2,1,0:T(8,128)} %refs_2_.9, f32[4,240,256]{2,1,0:T(8,128)} %refs_3_.9, f32[4,240,256]{2,1,0:T(8,128)} %refs_4_.9, f32[4,240,256]{2,1,0:T(8,128)} %refs_5_.9, ...), custom_call_target="tpu_custom_call" | custom-call | tf_op jit(solution)/shard_map/row_messages/pallas_call | solution.py:119
  2.0 2.5 %collective-permute-start = (f32[24,256]{1,0:T(8,128)S(1)}, f32[24,256]{1,0:T(8,128)S(1)}, u32[]{:S(2)}, u32[]{:S(2)}) collective-permute-start(f32[24,256]{1,0:T(8,128)S(1)} %get-tuple-element.26.refs_1_.refs_8_), channel_id=1, source_target_pairs={{0,128},{1,2},{2,1},{3,4},{4,3},{5,6},{6,5},{7,8},{8,7},{9,10},{10... | collective-permute-start | bytes 73736 | tf_op jit(solution)/shard_map/ppermute | solution.py:700
  4.5 0.0 collective-permute-start.1
  4.5 0.0 copy-done.7
  4.5 0.0 copy-done.6
  4.5 0.0 copy-done.5
  4.5 0.0 copy-done.4
  4.5 0.0 copy-done.3
  4.5 0.0 copy-done.2
  4.6 0.0 copy-done.1
  4.6 0.0 copy-done
  4.6 1.8 %edge_columns.1 = (f32[40,256]{1,0:T(8,128)S(1)}, f32[2,4,256,128]{3,2,1,0:T(8,128)S(1)}, f32[2,4,256,128]{3,2,1,0:T(8,128)S(1)}, f32[2,4,256,128]{3,2,1,0:T(8,128)S(1)}) custom-call(f32[4,240,256]{2,1,0:T(8,128)S(1)} %copy-done, f32[4,240,256]{2,1,0:T(8,128)S(1)} %copy-done.1, f32[4,240,256]{2,1,0:T(8,128)S(1)} %copy-done.2, f32[4,240,256]{2,1,0:T(8,128)S(1)} %copy-done.3, ...), custom_call_target="tpu_custom_call" | custom-call | flops 10000000 | bytes 8000000 | tf_op jit(solution)/shard_map/edge_columns/pallas_call | solution.py:243
  6.4 1.8 %interior_ahead.1 = (f32[2,4,240,128]{3,2,1,0:T(8,128)S(1)}, f32[2,4,256,128]{3,2,1,0:T(8,128)S(1)}, f32[2,4,240,128]{3,2,1,0:T(8,128)S(1)}, f32[2,4,240,128]{3,2,1,0:T(8,128)S(1)}) custom-call(f32[4,240,256]{2,1,0:T(8,128)S(1)} %copy-done, f32[4,240,256]{2,1,0:T(8,128)S(1)} %copy-done.1, f32[4,240,256]{2,1,0:T(8,128)S(1)} %copy-done.2, ...), custom_call_target="tpu_custom_call" | custom-call | flops 20000000 | bytes 16000000 | tf_op jit(solution)/shard_map/interior_ahead/pallas_call | solution.py:589
  8.3 0.0 collective-permute-done.refs_3_.refs_10_
  8.3 0.0 collective-permute-done.1.refs_4_.refs_11_
  8.3 0.1 column_messages.1
  8.4 1.1 %collective-permute-start.2 = (f32[40,128]{1,0:T(8,128)S(1)}, f32[40,128]{1,0:T(8,128)S(1)}, u32[]{:S(2)}, u32[]{:S(2)}) collective-permute-start(f32[40,128]{1,0:T(8,128)S(1)} %get-tuple-element.49), channel_id=1, source_target_pairs={{0,16},{1,17},{2,18},{3,19},{4,20},{5,21},{6,22},{7,23},{8,24},{9,... | collective-permute-start | bytes 61448 | tf_op jit(solution)/shard_map/ppermute | solution.py:711
  9.6 3.3 %interior_between.1 = (f32[2,4,240,128]{3,2,1,0:T(8,128)S(1)}, f32[2,4,256,128]{3,2,1,0:T(8,128)S(1)}, f32[2,4,240,128]{3,2,1,0:T(8,128)S(1)}, f32[2,4,240,128]{...) custom-call(f32[4,240,256]{2,1,0:T(8,128)S(1)} %copy-done, ...), custom_call_target="tpu_custom_call", output_to_operand_aliasing={{0}: (14, {}), {1}: (15, {}), {2}: (16, {}), {3}: (17, {}),... | custom-call | flops 20000000 | bytes 16000000 | tf_op jit(solution)/shard_map/interior_between/pallas_call | solution.py:589
  12.9 2.3 %collective-permute-start.3 = (f32[20,256]{1,0:T(8,128)S(1)}, f32[20,256]{1,0:T(8,128)S(1)}, u32[]{:S(2)}, u32[]{:S(2)}) collective-permute-start(f32[20,256]{1,0:T(8,128)S(1)} %get-tuple-element.44.refs_21_.refs_3_), channel_id=1, source_target_pairs={{0,240},{1,241},{2,242},{3,243},{4,244},{5,245},{6,246},{7,247},{8... | collective-permute-start | bytes 61448 | tf_op jit(solution)/shard_map/ppermute | solution.py:721
  15.2 1.6 %collective-permute-done.2.refs_5_ = f32[40,128]{1,0:T(8,128)S(1)} collective-permute-done((f32[40,128]{1,0:T(8,128)S(1)}, f32[40,128]{1,0:T(8,128)S(1)}, u32[]{:S(2)}, u32[]{:S(2)}) %collective-permute-start.2) | collective-permute-done | bytes 20512 | tf_op jit(solution)/shard_map/ppermute | solution.py:711
  16.8 0.0 collective-permute-done.3.refs_6_
  16.8 1.6 %edges_and_store.1 = (f32[4,240,256]{2,1,0:T(8,128)}, f32[4,240,256]{2,1,0:T(8,128)}) custom-call(f32[2,4,240,128]{3,2,1,0:T(8,128)S(1)} %get-tuple-element.45.refs_0_, f32[2,4,240,128]{3,2,1,0:T(8,128)S(1)} %get-tuple-element.46.refs_1_, f32[64,256]{1,0:T(8,128)S(1)} %get-tuple-element.47.refs_2_, f32[20,256]{1,0:T(8,128)S(1)} %get-tuple-element.44.refs_21_.refs_3_, ...), custom_call_target="tpu_custom_call" | custom-call | tf_op jit(solution)/shard_map/edges_and_store/pallas_call | solution.py:676
  (1 shorter events, 0.0 us)
Async XLA Ops:
  0.6 3.9 %copy-start.7 = (f32[4,240,256]{2,1,0:T(8,128)S(1)}, f32[4,240,256]{2,1,0:T(8,128)}, u32[]{:S(2)}) copy-start(f32[4,240,256]{2,1,0:T(8,128)} %refs_7_.9) | copy-start | bytes 2949124
  0.6 3.9 %copy-start.6 = (f32[4,240,256]{2,1,0:T(8,128)S(1)}, f32[4,240,256]{2,1,0:T(8,128)}, u32[]{:S(2)}) copy-start(f32[4,240,256]{2,1,0:T(8,128)} %refs_6_.9) | copy-start | bytes 2949124
  0.7 3.9 %copy-start.5 = (f32[4,240,256]{2,1,0:T(8,128)S(1)}, f32[4,240,256]{2,1,0:T(8,128)}, u32[]{:S(2)}) copy-start(f32[4,240,256]{2,1,0:T(8,128)} %refs_5_.9) | copy-start | bytes 2949124
  0.7 3.9 %copy-start.4 = (f32[4,240,256]{2,1,0:T(8,128)S(1)}, f32[4,240,256]{2,1,0:T(8,128)}, u32[]{:S(2)}) copy-start(f32[4,240,256]{2,1,0:T(8,128)} %refs_4_.9) | copy-start | bytes 2949124
  0.7 3.9 %copy-start.3 = (f32[4,240,256]{2,1,0:T(8,128)S(1)}, f32[4,240,256]{2,1,0:T(8,128)}, u32[]{:S(2)}) copy-start(f32[4,240,256]{2,1,0:T(8,128)} %refs_3_.9) | copy-start | bytes 2949124
  0.7 3.9 %copy-start.2 = (f32[4,240,256]{2,1,0:T(8,128)S(1)}, f32[4,240,256]{2,1,0:T(8,128)}, u32[]{:S(2)}) copy-start(f32[4,240,256]{2,1,0:T(8,128)} %refs_2_.9) | copy-start | bytes 2949124
  0.7 3.9 %copy-start.1 = (f32[4,240,256]{2,1,0:T(8,128)S(1)}, f32[4,240,256]{2,1,0:T(8,128)}, u32[]{:S(2)}) copy-start(f32[4,240,256]{2,1,0:T(8,128)} %refs_1_.9) | copy-start | bytes 2949124
  0.7 3.9 %copy-start = (f32[4,240,256]{2,1,0:T(8,128)S(1)}, f32[4,240,256]{2,1,0:T(8,128)}, u32[]{:S(2)}) copy-start(f32[4,240,256]{2,1,0:T(8,128)} %refs_0_.9) | copy-start | bytes 2949124
  2.0 6.3 %collective-permute-start = (f32[24,256]{1,0:T(8,128)S(1)}, f32[24,256]{1,0:T(8,128)S(1)}, u32[]{:S(2)}, u32[]{:S(2)}) collective-permute-start(f32[24,256]{1,0:T(8,128)S(1)} %get-tuple-element.26.refs_1_.refs_8_), channel_id=1, source_target_pairs={{0,128},{1,2},{2,1},{3,4},{4,3},{5,6},{6,5},{7,8},{8,7},{9,10},{10... | collective-permute-start | bytes 73736 | tf_op jit(solution)/shard_map/ppermute | solution.py:700
  4.5 3.8 %collective-permute-start.1 = (f32[24,256]{1,0:T(8,128)S(1)}, f32[24,256]{1,0:T(8,128)S(1)}, u32[]{:S(2)}, u32[]{:S(2)}) collective-permute-start(f32[24,256]{1,0:T(8,128)S(1)} %get-tuple-element.27.refs_2_.refs_9_), channel_id=1, source_target_pairs={{0,1},{1,0},{2,3},{3,2},{4,5},{5,4},{6,7},{7,6},{8,9},{9,8},{10,11... | collective-permute-start | bytes 73736 | tf_op jit(solution)/shard_map/ppermute | solution.py:701
  8.4 8.4 %collective-permute-start.2 = (f32[40,128]{1,0:T(8,128)S(1)}, f32[40,128]{1,0:T(8,128)S(1)}, u32[]{:S(2)}, u32[]{:S(2)}) collective-permute-start(f32[40,128]{1,0:T(8,128)S(1)} %get-tuple-element.49), channel_id=1, source_target_pairs={{0,16},{1,17},{2,18},{3,19},{4,20},{5,21},{6,22},{7,23},{8,24},{9,... | collective-permute-start | bytes 61448 | tf_op jit(solution)/shard_map/ppermute | solution.py:711
  12.9 3.9 %collective-permute-start.3 = (f32[20,256]{1,0:T(8,128)S(1)}, f32[20,256]{1,0:T(8,128)S(1)}, u32[]{:S(2)}, u32[]{:S(2)}) collective-permute-start(f32[20,256]{1,0:T(8,128)S(1)} %get-tuple-element.44.refs_21_.refs_3_), channel_id=1, source_target_pairs={{0,240},{1,241},{2,242},{3,243},{4,244},{5,245},{6,246},{7,247},{8... | collective-permute-start | bytes 61448 | tf_op jit(solution)/shard_map/ppermute | solution.py:721

commit v8 on v7

--- a/solution.py
+++ b/solution.py
@@ -333,7 +333,7 @@
 STATE = 5
 FIRST_AHEAD = 3
 OTHERS_AHEAD = 2
-BETWEEN = (5, 3, 3, 1, 2, 1)
+BETWEEN = (5, 4, 3, 1, 2, 1)
 
 
 def place():

time: 18.6 us -> 18.6 us (level)
  no operation moved by 1% of the time
where the time goes in v8:
time: 18.6 us; the launch traced here: 18.5 us
  Pallas kernels  10 us (54%)
  starting transfers between devices  5.95 us (32%)
  waiting for transfers between devices  1.62 us (9%)
  between operations  0.81 us (4%)
    pallas_call x3, Pallas kernels, interior_call(): pl.pallas_call(lambda *refs: kernel(lat_total, rows, *refs), in_specs=[vm...  5.18 us
    ppermute x1, starting transfers between devices, per_device(): far_in = lax.ppermute(far, AXES, rows_far)  2.51 us
    ppermute x1, starting transfers between devices, per_device(): from_east = lax.ppermute(west, AXES, westward)  2.29 us
    pallas_call x1, Pallas kernels, edge_call(): pl.pallas_call(lambda *refs: edge_kernel(lat_total, rows, *refs), in_spec...  1.84 us
    pallas_call x1, Pallas kernels, final_call(): pl.pallas_call(lambda *refs: final_kernel(rows, *refs), in_specs=[vmem] *...  1.63 us
    ppermute x1, waiting for transfers between devices, per_device(): from_west = lax.ppermute(sent, AXES, eastward)  1.62 us
    pallas_call x1, Pallas kernels, rows_call(): pl.pallas_call(lambda *refs: rows_kernel(lat_total, rows, *refs), grid=(1...  1.27 us
    ppermute x1, starting transfers between devices, per_device(): from_west = lax.ppermute(sent, AXES, eastward)  1.14 us
  transfers between devices with their start and end apart: 4, of which 1 were waited for; matrix products, arithmetic and copies ran while one was open for 0% of the time, Pallas kernels for 38%

profile of v8, /device:TPU:2, one launch (start us, length us, event | category | flops | bytes accessed | tf_op | source)
XLA Modules:
  0.0 18.5 jit_solution(5543540379401480234)
XLA Ops:
  0.6 0.0 copy-start.7
  0.6 0.0 copy-start.6
  0.7 0.0 copy-start.5
  0.7 0.0 copy-start.4
  0.7 0.0 copy-start.3
  0.7 0.0 copy-start.2
  0.7 0.0 copy-start.1
  0.7 0.0 copy-start
  0.7 1.3 %row_messages.1 = (f32[24,256]{1,0:T(8,128)S(1)}, f32[24,256]{1,0:T(8,128)S(1)}) custom-call(f32[4,240,256]{2,1,0:T(8,128)} %refs_0_.9, f32[4,240,256]{2,1,0:T(8,128)} %refs_1_.9, f32[4,240,256]{2,1,0:T(8,128)} %refs_2_.9, f32[4,240,256]{2,1,0:T(8,128)} %refs_3_.9, f32[4,240,256]{2,1,0:T(8,128)} %refs_4_.9, f32[4,240,256]{2,1,0:T(8,128)} %refs_5_.9, ...), custom_call_target="tpu_custom_call" | custom-call | tf_op jit(solution)/shard_map/row_messages/pallas_call | solution.py:119
  2.0 2.5 %collective-permute-start = (f32[24,256]{1,0:T(8,128)S(1)}, f32[24,256]{1,0:T(8,128)S(1)}, u32[]{:S(2)}, u32[]{:S(2)}) collective-permute-start(f32[24,256]{1,0:T(8,128)S(1)} %get-tuple-element.26.refs_1_.refs_8_), channel_id=1, source_target_pairs={{0,128},{1,2},{2,1},{3,4},{4,3},{5,6},{6,5},{7,8},{8,7},{9,10},{10... | collective-permute-start | bytes 73736 | tf_op jit(solution)/shard_map/ppermute | solution.py:700
  4.5 0.0 collective-permute-start.1
  4.5 0.0 copy-done.7
  4.5 0.0 copy-done.6
  4.5 0.0 copy-done.5
  4.5 0.0 copy-done.4
  4.5 0.0 copy-done.3
  4.5 0.0 copy-done.2
  4.6 0.0 copy-done.1
  4.6 0.0 copy-done
  4.6 1.8 %edge_columns.1 = (f32[40,256]{1,0:T(8,128)S(1)}, f32[2,4,256,128]{3,2,1,0:T(8,128)S(1)}, f32[2,4,256,128]{3,2,1,0:T(8,128)S(1)}, f32[2,4,256,128]{3,2,1,0:T(8,128)S(1)}) custom-call(f32[4,240,256]{2,1,0:T(8,128)S(1)} %copy-done, f32[4,240,256]{2,1,0:T(8,128)S(1)} %copy-done.1, f32[4,240,256]{2,1,0:T(8,128)S(1)} %copy-done.2, f32[4,240,256]{2,1,0:T(8,128)S(1)} %copy-done.3, ...), custom_call_target="tpu_custom_call" | custom-call | flops 10000000 | bytes 8000000 | tf_op jit(solution)/shard_map/edge_columns/pallas_call | solution.py:243
  6.4 1.8 %interior_ahead.1 = (f32[2,4,240,128]{3,2,1,0:T(8,128)S(1)}, f32[2,4,256,128]{3,2,1,0:T(8,128)S(1)}, f32[2,4,240,128]{3,2,1,0:T(8,128)S(1)}, f32[2,4,240,128]{3,2,1,0:T(8,128)S(1)}) custom-call(f32[4,240,256]{2,1,0:T(8,128)S(1)} %copy-done, f32[4,240,256]{2,1,0:T(8,128)S(1)} %copy-done.1, f32[4,240,256]{2,1,0:T(8,128)S(1)} %copy-done.2, ...), custom_call_target="tpu_custom_call" | custom-call | flops 20000000 | bytes 16000000 | tf_op jit(solution)/shard_map/interior_ahead/pallas_call | solution.py:589
  8.3 0.0 collective-permute-done.refs_3_.refs_10_
  8.3 0.0 collective-permute-done.1.refs_4_.refs_11_
  8.3 0.1 column_messages.1
  8.4 1.1 %collective-permute-start.2 = (f32[40,128]{1,0:T(8,128)S(1)}, f32[40,128]{1,0:T(8,128)S(1)}, u32[]{:S(2)}, u32[]{:S(2)}) collective-permute-start(f32[40,128]{1,0:T(8,128)S(1)} %get-tuple-element.49), channel_id=1, source_target_pairs={{0,16},{1,17},{2,18},{3,19},{4,20},{5,21},{6,22},{7,23},{8,24},{9,... | collective-permute-start | bytes 61448 | tf_op jit(solution)/shard_map/ppermute | solution.py:711
  9.6 3.3 %interior_between.1 = (f32[2,4,240,128]{3,2,1,0:T(8,128)S(1)}, f32[2,4,256,128]{3,2,1,0:T(8,128)S(1)}, f32[2,4,240,128]{3,2,1,0:T(8,128)S(1)}, f32[2,4,240,128]{...) custom-call(f32[4,240,256]{2,1,0:T(8,128)S(1)} %copy-done, ...), custom_call_target="tpu_custom_call", output_to_operand_aliasing={{0}: (14, {}), {1}: (15, {}), {2}: (16, {}), {3}: (17, {}),... | custom-call | flops 20000000 | bytes 16000000 | tf_op jit(solution)/shard_map/interior_between/pallas_call | solution.py:589
  12.9 2.3 %collective-permute-start.3 = (f32[20,256]{1,0:T(8,128)S(1)}, f32[20,256]{1,0:T(8,128)S(1)}, u32[]{:S(2)}, u32[]{:S(2)}) collective-permute-start(f32[20,256]{1,0:T(8,128)S(1)} %get-tuple-element.44.refs_21_.refs_3_), channel_id=1, source_target_pairs={{0,240},{1,241},{2,242},{3,243},{4,244},{5,245},{6,246},{7,247},{8... | collective-permute-start | bytes 61448 | tf_op jit(solution)/shard_map/ppermute | solution.py:721
  15.2 1.6 %collective-permute-done.2.refs_5_ = f32[40,128]{1,0:T(8,128)S(1)} collective-permute-done((f32[40,128]{1,0:T(8,128)S(1)}, f32[40,128]{1,0:T(8,128)S(1)}, u32[]{:S(2)}, u32[]{:S(2)}) %collective-permute-start.2) | collective-permute-done | bytes 20512 | tf_op jit(solution)/shard_map/ppermute | solution.py:711
  16.8 0.0 collective-permute-done.3.refs_6_
  16.8 1.6 %edges_and_store.1 = (f32[4,240,256]{2,1,0:T(8,128)}, f32[4,240,256]{2,1,0:T(8,128)}) custom-call(f32[2,4,240,128]{3,2,1,0:T(8,128)S(1)} %get-tuple-element.45.refs_0_, f32[2,4,240,128]{3,2,1,0:T(8,128)S(1)} %get-tuple-element.46.refs_1_, f32[64,256]{1,0:T(8,128)S(1)} %get-tuple-element.47.refs_2_, f32[20,256]{1,0:T(8,128)S(1)} %get-tuple-element.44.refs_21_.refs_3_, ...), custom_call_target="tpu_custom_call" | custom-call | tf_op jit(solution)/shard_map/edges_and_store/pallas_call | solution.py:676
  (1 shorter events, 0.0 us)
Async XLA Ops:
  0.6 3.9 %copy-start.7 = (f32[4,240,256]{2,1,0:T(8,128)S(1)}, f32[4,240,256]{2,1,0:T(8,128)}, u32[]{:S(2)}) copy-start(f32[4,240,256]{2,1,0:T(8,128)} %refs_7_.9) | copy-start | bytes 2949124
  0.6 3.9 %copy-start.6 = (f32[4,240,256]{2,1,0:T(8,128)S(1)}, f32[4,240,256]{2,1,0:T(8,128)}, u32[]{:S(2)}) copy-start(f32[4,240,256]{2,1,0:T(8,128)} %refs_6_.9) | copy-start | bytes 2949124
  0.7 3.9 %copy-start.5 = (f32[4,240,256]{2,1,0:T(8,128)S(1)}, f32[4,240,256]{2,1,0:T(8,128)}, u32[]{:S(2)}) copy-start(f32[4,240,256]{2,1,0:T(8,128)} %refs_5_.9) | copy-start | bytes 2949124
  0.7 3.9 %copy-start.4 = (f32[4,240,256]{2,1,0:T(8,128)S(1)}, f32[4,240,256]{2,1,0:T(8,128)}, u32[]{:S(2)}) copy-start(f32[4,240,256]{2,1,0:T(8,128)} %refs_4_.9) | copy-start | bytes 2949124
  0.7 3.9 %copy-start.3 = (f32[4,240,256]{2,1,0:T(8,128)S(1)}, f32[4,240,256]{2,1,0:T(8,128)}, u32[]{:S(2)}) copy-start(f32[4,240,256]{2,1,0:T(8,128)} %refs_3_.9) | copy-start | bytes 2949124
  0.7 3.9 %copy-start.2 = (f32[4,240,256]{2,1,0:T(8,128)S(1)}, f32[4,240,256]{2,1,0:T(8,128)}, u32[]{:S(2)}) copy-start(f32[4,240,256]{2,1,0:T(8,128)} %refs_2_.9) | copy-start | bytes 2949124
  0.7 3.9 %copy-start.1 = (f32[4,240,256]{2,1,0:T(8,128)S(1)}, f32[4,240,256]{2,1,0:T(8,128)}, u32[]{:S(2)}) copy-start(f32[4,240,256]{2,1,0:T(8,128)} %refs_1_.9) | copy-start | bytes 2949124
  0.7 3.9 %copy-start = (f32[4,240,256]{2,1,0:T(8,128)S(1)}, f32[4,240,256]{2,1,0:T(8,128)}, u32[]{:S(2)}) copy-start(f32[4,240,256]{2,1,0:T(8,128)} %refs_0_.9) | copy-start | bytes 2949124
  2.0 6.3 %collective-permute-start = (f32[24,256]{1,0:T(8,128)S(1)}, f32[24,256]{1,0:T(8,128)S(1)}, u32[]{:S(2)}, u32[]{:S(2)}) collective-permute-start(f32[24,256]{1,0:T(8,128)S(1)} %get-tuple-element.26.refs_1_.refs_8_), channel_id=1, source_target_pairs={{0,128},{1,2},{2,1},{3,4},{4,3},{5,6},{6,5},{7,8},{8,7},{9,10},{10... | collective-permute-start | bytes 73736 | tf_op jit(solution)/shard_map/ppermute | solution.py:700
  4.5 3.8 %collective-permute-start.1 = (f32[24,256]{1,0:T(8,128)S(1)}, f32[24,256]{1,0:T(8,128)S(1)}, u32[]{:S(2)}, u32[]{:S(2)}) collective-permute-start(f32[24,256]{1,0:T(8,128)S(1)} %get-tuple-element.27.refs_2_.refs_9_), channel_id=1, source_target_pairs={{0,1},{1,0},{2,3},{3,2},{4,5},{5,4},{6,7},{7,6},{8,9},{9,8},{10,11... | collective-permute-start | bytes 73736 | tf_op jit(solution)/shard_map/ppermute | solution.py:701
  8.4 8.4 %collective-permute-start.2 = (f32[40,128]{1,0:T(8,128)S(1)}, f32[40,128]{1,0:T(8,128)S(1)}, u32[]{:S(2)}, u32[]{:S(2)}) collective-permute-start(f32[40,128]{1,0:T(8,128)S(1)} %get-tuple-element.49), channel_id=1, source_target_pairs={{0,16},{1,17},{2,18},{3,19},{4,20},{5,21},{6,22},{7,23},{8,24},{9,... | collective-permute-start | bytes 61448 | tf_op jit(solution)/shard_map/ppermute | solution.py:711
  12.9 3.9 %collective-permute-start.3 = (f32[20,256]{1,0:T(8,128)S(1)}, f32[20,256]{1,0:T(8,128)S(1)}, u32[]{:S(2)}, u32[]{:S(2)}) collective-permute-start(f32[20,256]{1,0:T(8,128)S(1)} %get-tuple-element.44.refs_21_.refs_3_), channel_id=1, source_target_pairs={{0,240},{1,241},{2,242},{3,243},{4,244},{5,245},{6,246},{7,247},{8... | collective-permute-start | bytes 61448 | tf_op jit(solution)/shard_map/ppermute | solution.py:721
